TPU v7x, 512 devices: a whole 4x4x16 slice. The times are simulated.
512 devices in a mesh: seq: 128 (over z, x_lo, y), head: 4 (over x_hi, core).
Axes of the slice: x: 4 (x_hi: 2, x_lo: 2; x = x_hi * 2 + x_lo), y: 4, z: 16, core: 2. Of those that a mesh axis runs over, the one named last changes fastest.
Arguments:
- frames_in: bfloat16 [32768, 1024], P(('seq', 'head')), may hold values from -12 to 12
- query_weight: bfloat16 [1024, 1024], P(None, 'head'), may hold values from -0.1875 to 0.1875
- key_weight: bfloat16 [1024, 1024], P(None, 'head'), may hold values from -0.1875 to 0.1875
- value_weight: bfloat16 [1024, 1024], P(None, 'head'), may hold values from -0.1875 to 0.1875
- out_weight: bfloat16 [1024, 1024], P('head'), may hold values from -0.1875 to 0.1875
- read_mask: int32 [128, 3], replicated, may hold values from 0 to 1, as said below
- out_grad: bfloat16 [32768, 1024], P(('seq', 'head')), may hold values from -24 to 24
Outputs:
- mixed: bfloat16 [32768, 1024], P(('seq', 'head'))
- frames_grad: bfloat16 [32768, 1024], P(('seq', 'head'))
- grad_value_weight: float32 [1024, 1024], P('seq', 'head')
- grad_out_weight: float32 [1024, 1024], P('head', 'seq')
Inputs may be any that keep to these rules, and one draw needn't show every extreme that they name: read_mask[i, k - 1] is 1 only where stretch i - k exists and lies in the same dialogue as stretch i.
All inputs are finite; a program needn't handle non-finite values.
Results may differ from a plain program's by a relative error of at most 0.023.
The roundings to bfloat16 on the way count: a program that leaves them out, or rounds other values in their place, can miss the bound.
Values may be sent and summed in bfloat16 or wider, within the bound.
No kernel may reach another device: no remote copies, remote signals or barrier semaphores. Data moves between devices by JAX's collectives and lax.ppermute only.
A program may use at most 64 MiB of HBM per device.

v0:
```python
import jax
import jax.numpy as jnp
from jax import lax
from jax.sharding import PartitionSpec as P

HEAD_DIM = 64
WINDOW = 4


def passed_along(value, axis, steps):
    count = lax.axis_size(axis)
    first, last = (max(0, -steps), min(count, count - steps))
    return lax.ppermute(value, axis, [(source, source + steps) for source in range(first, last)])


def block_scores(left, parts, listed, factor, filler):
    pieces = []
    for number in range(len(parts)):
        part = parts[number]
        piece = jnp.where(
            listed[number],
            jnp.dot(left, part.T, preferred_element_type=jnp.float32) * factor,
            filler,
        )
        pieces.append(piece)
    return jnp.concatenate(pieces, axis=1)


def block_product(weights, parts):
    return jnp.dot(weights, jnp.concatenate(parts, axis=0), preferred_element_type=jnp.float32)


def block_transposed(weights, right, count):
    span = weights.shape[1] // count
    results = []
    for number in range(count):
        tile = weights[:, number * span : (number + 1) * span]
        results.append(jnp.einsum("qk,qe->ke", tile, right, preferred_element_type=jnp.float32))
    return results


def columns(array, head):
    return array[:, head * HEAD_DIM : (head + 1) * HEAD_DIM]


def per_device(frames_in, query_weight, key_weight, value_weight, out_weight, read_mask, out_grad):
    factor = HEAD_DIM ** (-0.5)
    feature_count = query_weight.shape[1]
    head_count = feature_count // HEAD_DIM
    stretch_id = lax.axis_index("seq")
    frames_all = lax.all_gather(frames_in, "head", axis=0, tiled=True)
    queries = jnp.dot(frames_all, query_weight, preferred_element_type=jnp.float32).astype(
        jnp.bfloat16
    )
    keys = jnp.dot(frames_all, key_weight, preferred_element_type=jnp.float32).astype(jnp.bfloat16)
    values = jnp.dot(frames_all, value_weight, preferred_element_type=jnp.float32).astype(
        jnp.bfloat16
    )
    mask_row = lax.dynamic_slice_in_dim(read_mask, stretch_id, 1, 0)[0] > 0
    listed = jnp.concatenate([jnp.ones((1,), jnp.bool_), mask_row])
    key_blocks = [keys]
    value_blocks = [values]
    for distance in range(1, WINDOW):
        far_keys, far_values = passed_along((keys, values), "seq", distance)
        key_blocks.append(far_keys)
        value_blocks.append(far_values)
    attended_heads = []
    total_heads = []
    for head in range(head_count):
        query_head = columns(queries, head)
        key_parts = [columns(block, head) for block in key_blocks]
        value_parts = [columns(block, head) for block in value_blocks]
        scores = block_scores(query_head, key_parts, listed, factor, -1e30)
        top = jnp.max(scores, axis=1)
        log_total = top + jnp.log(jnp.sum(jnp.exp(scores - top[:, None]), axis=1))
        weights_soft = jnp.exp(scores - log_total[:, None]).astype(jnp.bfloat16)
        attended_heads.append(block_product(weights_soft, value_parts).astype(jnp.bfloat16))
        total_heads.append(log_total)
    attended = jnp.concatenate(attended_heads, axis=1)
    total_all = jnp.stack(total_heads)
    part = jnp.dot(attended, out_weight, preferred_element_type=jnp.float32).astype(jnp.bfloat16)
    mixed = lax.psum_scatter(
        lax.optimization_barrier(part).astype(jnp.float32).astype(jnp.bfloat16),
        "head",
        scatter_dimension=0,
        tiled=True,
    )
    grads_all = lax.all_gather(out_grad, "head", axis=0, tiled=True)
    out_back = jnp.einsum(
        "fd,gd->fg", grads_all, out_weight, preferred_element_type=jnp.float32
    ).astype(jnp.bfloat16)
    out_weight_term = jnp.einsum(
        "fg,fd->gd", attended, grads_all, preferred_element_type=jnp.float32
    )
    query_heads = []
    own_key_heads = []
    own_value_heads = []
    far_key_heads = []
    far_value_heads = []
    dot_heads = []
    for head in range(head_count):
        query_head = columns(queries, head)
        back_head = columns(out_back, head)
        key_parts = [columns(block, head) for block in key_blocks]
        value_parts = [columns(block, head) for block in value_blocks]
        back_dot = jnp.sum(
            back_head.astype(jnp.float32) * columns(attended, head).astype(jnp.float32), axis=1
        )
        scores = block_scores(query_head, key_parts, listed, factor, -1e30)
        weights_full = jnp.exp(scores - total_all[head][:, None])
        weights_soft = weights_full.astype(jnp.bfloat16)
        back_scores = block_scores(back_head, value_parts, listed, 1.0, 0.0)
        score_grad = (weights_full * (back_scores - back_dot[:, None]) * factor).astype(
            jnp.bfloat16
        )
        query_heads.append(block_product(score_grad, key_parts).astype(jnp.bfloat16))
        dot_heads.append(back_dot)
        key_terms = block_transposed(score_grad, query_head, WINDOW)
        value_terms = block_transposed(weights_soft, back_head, WINDOW)
        own_key_heads.append(key_terms[0])
        own_value_heads.append(value_terms[0])
        far_key_heads.append(key_terms[1:])
        far_value_heads.append(value_terms[1:])
    query_grad = jnp.concatenate(query_heads, axis=1)
    key_total = jnp.concatenate(own_key_heads, axis=1)
    value_total = jnp.concatenate(own_value_heads, axis=1)
    for distance in range(1, WINDOW):
        key_part = jnp.concatenate(
            [far_key_heads[head][distance - 1] for head in range(head_count)], axis=1
        )
        value_part = jnp.concatenate(
            [far_value_heads[head][distance - 1] for head in range(head_count)], axis=1
        )
        back_key, back_value = (
            passed_along(key_part.astype(jnp.bfloat16), "seq", -distance).astype(key_part.dtype),
            passed_along(value_part.astype(jnp.bfloat16), "seq", -distance).astype(
                value_part.dtype
            ),
        )
        key_total = key_total + back_key
        value_total = value_total + back_value
    key_grad = key_total.astype(jnp.bfloat16)
    value_grad = value_total.astype(jnp.bfloat16)
    term = jnp.einsum("fg,dg->fd", query_grad, query_weight, preferred_element_type=jnp.float32)
    term = term + jnp.einsum("fg,dg->fd", key_grad, key_weight, preferred_element_type=jnp.float32)
    term = term + jnp.einsum(
        "fg,dg->fd", value_grad, value_weight, preferred_element_type=jnp.float32
    )
    rounded = lax.optimization_barrier(term.astype(jnp.bfloat16))
    frames_grad = lax.psum_scatter(
        rounded.astype(jnp.float32).astype(jnp.bfloat16), "head", scatter_dimension=0, tiled=True
    )
    value_weight_term = jnp.einsum(
        "fd,fg->dg", frames_all, value_grad, preferred_element_type=jnp.float32
    )
    grad_value_weight, grad_out_weight = (
        lax.psum_scatter(value_weight_term, "seq", scatter_dimension=0, tiled=True),
        lax.psum_scatter(out_weight_term, "seq", scatter_dimension=1, tiled=True),
    )
    return (mixed, frames_grad, grad_value_weight, grad_out_weight)


def solution(mesh):
    in_specs = (
        P(("seq", "head"), None),
        P(None, "head"),
        P(None, "head"),
        P(None, "head"),
        P("head", None),
        P(),
        P(("seq", "head"), None),
    )
    out_specs = (
        P(("seq", "head"), None),
        P(("seq", "head"), None),
        P("seq", "head"),
        P("head", "seq"),
    )
    return jax.shard_map(
        per_device, mesh=mesh, in_specs=in_specs, out_specs=out_specs, check_vma=False
    )
```

profile of v0, /device:TPU:4, one launch (start us, length us, event | category | flops | bytes accessed | tf_op | source)
XLA Modules:
  0.0 1495.6 jit_solution(3764759582307194358)
XLA Ops:
  7.2 11.9 all_gather.6
  20.2 2.4 collective-permute-start.2
  22.6 3.8 collective-permute-start.1
  26.4 2.9 collective-permute-start
  29.6 3.2 collective-permute-start.3
  32.8 5.4 collective-permute-start.4
  43.3 8.0 all_gather.7
  58.2 2.3 collective-permute-start.5
  60.6 1.7 fusion.274
  62.3 1.7 fusion.275
  64.0 1.7 fusion.277
  66.4 1.7 fusion.270
  68.1 1.7 fusion.271
  69.8 1.7 fusion.273
  72.2 1.7 fusion.266
  73.9 1.7 fusion.267
  75.6 1.7 fusion.269
  78.0 1.7 fusion.265
  79.7 1.7 fusion.263
  81.4 1.7 fusion.262
  92.8 1.7 convolution_select_fusion.10
  94.4 1.7 convolution_select_fusion.11
  98.5 1.7 convolution_select_fusion.7
  103.4 1.7 convolution_select_fusion.4
  105.1 1.6 convolution_select_fusion.5
  108.2 1.7 convolution_select_fusion.1
  109.9 1.6 convolution_select_fusion.2
  137.6 10.4 collective-permute-done.8
  154.4 31.4 %reduce-scatter.7.cloned.1.call-done = bf16[64,1024]{1,0:T(8,128)(2,1)} async-done(((bf16[256,1024]{1,0:T(8,128)(2,1)}), bf16[64,1024]{1,0:T(8,128)(2,1)}) %reduce-scatter.7.cloned.1.call-update) | async-done | bytes 131088 | tf_op jit(solution)/shard_map/reduce_scatter | solution.py:82
  185.9 47.4 %reduce-scatter.9.cloned.1.call-done = bf16[64,1024]{1,0:T(8,128)(2,1)} async-done(((bf16[256,1024]{1,0:T(8,128)(2,1)}), bf16[64,1024]{1,0:T(8,128)(2,1)}) %reduce-scatter.9.cloned.1.call-update) | async-done | bytes 131088 | tf_op jit(solution)/shard_map/reduce_scatter | solution.py:150
  233.3 631.2 %reduce-scatter.11.cloned.1.call-done = f32[256,8]{0,1:T(8,128)} async-done(((f32[256,1024]{0,1:T(8,128)}), f32[256,8]{0,1:T(8,128)}) %reduce-scatter.11.cloned.1.call-update) | async-done | bytes 8208 | tf_op jit(solution)/shard_map/reduce_scatter | solution.py:158
  864.4 624.6 %reduce-scatter.13.cloned.1.call-done = f32[8,256]{1,0:T(8,128)} async-done(((f32[1024,256]{1,0:T(8,128)}), f32[8,256]{1,0:T(8,128)}) %reduce-scatter.13.cloned.1.call-update) | async-done | bytes 8208
  (214 shorter events, 64.0 us)
Async XLA Ops:
  7.2 44.2 %copy-start = (bf16[256,1024]{1,0:T(8,128)(2,1)S(1)}, bf16[256,1024]{1,0:T(8,128)(2,1)}, u32[]{:S(2)}) copy-start(bf16[256,1024]{1,0:T(8,128)(2,1)} %param.11) | copy-start | bytes 1572868
  7.2 12.0 copy-start.2
  7.2 178.7 %reduce-scatter.7.cloned.1.call-start = ((), (), s32[]{:S(2)}) async-start(), calls=%async_computation.4 | async-start | bytes 655360 | tf_op jit(solution)/shard_map/reduce_scatter | solution.py:82
  19.1 10.1 copy-start.4
  20.1 18.1 %copy-start.1 = (bf16[1024,256]{1,0:T(8,128)(2,1)S(1)}, bf16[1024,256]{1,0:T(8,128)(2,1)}, u32[]{:S(2)}) copy-start(bf16[1024,256]{1,0:T(8,128)(2,1)} %param.8) | copy-start | bytes 1572868
  20.2 38.1 %collective-permute-start.2 = (bf16[256,256]{0,1:T(8,128)(2,1)}, bf16[256,256]{0,1:T(8,128)(2,1)}, u32[]{:S(2)}, u32[]{:S(2)}) collective-permute-start(bf16[256,256]{0,1:T(8,128)(2,1)} %convolution_convert_fusion.3), channel_id=1, source_target_pairs={{0,12},{4,16},{8,20},{12,24},{16,28},{20,32},{24,36},{28,40},{32,4... | collective-permute-start | bytes 393224 | tf_op jit(solution)/shard_map/ppermute | solution.py:13
  22.6 39.7 %collective-permute-start.1 = (bf16[256,256]{0,1:T(8,128)(2,1)}, bf16[256,256]{0,1:T(8,128)(2,1)}, u32[]{:S(2)}, u32[]{:S(2)}) collective-permute-start(bf16[256,256]{0,1:T(8,128)(2,1)} %convolution_convert_fusion.3), channel_id=1, source_target_pairs={{0,8},{4,12},{8,16},{12,20},{16,24},{20,28},{24,32},{28,36},{32,40... | collective-permute-start | bytes 393224 | tf_op jit(solution)/shard_map/ppermute | solution.py:13
  26.4 37.6 %collective-permute-start = (bf16[256,256]{0,1:T(8,128)(2,1)}, bf16[256,256]{0,1:T(8,128)(2,1)}, u32[]{:S(2)}, u32[]{:S(2)}) collective-permute-start(bf16[256,256]{0,1:T(8,128)(2,1)} %convolution_convert_fusion.3), channel_id=1, source_target_pairs={{0,4},{4,8},{8,12},{12,16},{16,20},{20,24},{24,28},{28,32},{32,36}... | collective-permute-start | bytes 393224 | tf_op jit(solution)/shard_map/ppermute | solution.py:13
  29.6 58.2 %collective-permute-start.3 = (bf16[256,256]{0,1:T(8,128)(2,1)S(1)}, bf16[256,256]{0,1:T(8,128)(2,1)}, u32[]{:S(2)}, u32[]{:S(2)}) collective-permute-start(bf16[256,256]{0,1:T(8,128)(2,1)S(1)} %convolution_convert_fusion.2), channel_id=1, source_target_pairs={{0,4},{4,8},{8,12},{12,16},{16,20},{20,24},{24,28},{28,32},{32,36}... | collective-permute-start | bytes 393224 | tf_op jit(solution)/shard_map/ppermute | solution.py:13
  32.8 55.9 %collective-permute-start.4 = (bf16[256,256]{0,1:T(8,128)(2,1)S(1)}, bf16[256,256]{0,1:T(8,128)(2,1)}, u32[]{:S(2)}, u32[]{:S(2)}) collective-permute-start(bf16[256,256]{0,1:T(8,128)(2,1)S(1)} %convolution_convert_fusion.2), channel_id=1, source_target_pairs={{0,8},{4,12},{8,16},{12,20},{16,24},{20,28},{24,32},{28,36},{32,40... | collective-permute-start | bytes 393224 | tf_op jit(solution)/shard_map/ppermute | solution.py:13
  58.2 31.3 %collective-permute-start.5 = (bf16[256,256]{0,1:T(8,128)(2,1)S(1)}, bf16[256,256]{0,1:T(8,128)(2,1)S(1)}, u32[]{:S(2)}, u32[]{:S(2)}) collective-permute-start(bf16[256,256]{0,1:T(8,128)(2,1)S(1)} %convolution_convert_fusion.2), channel_id=1, source_target_pairs={{0,12},{4,16},{8,20},{12,24},{16,28},{20,32},{24,36},{28,40},{32,4... | collective-permute-start | bytes 393224 | tf_op jit(solution)/shard_map/ppermute | solution.py:13
  90.5 36.1 %copy-start.25 = (bf16[256,64]{0,1:T(8,128)(2,1)}, bf16[256,64]{0,1:T(8,128)(2,1)S(1)}, u32[]{:S(2)}) copy-start(bf16[256,64]{0,1:T(8,128)(2,1)S(1)} %convolution_convert_fusion.23) | copy-start | bytes 98308
  91.2 35.4 %copy-start.27 = (bf16[256,64]{0,1:T(8,128)(2,1)}, bf16[256,64]{0,1:T(8,128)(2,1)S(1)}, u32[]{:S(2)}) copy-start(bf16[256,64]{0,1:T(8,128)(2,1)S(1)} %convolution_convert_fusion.22) | copy-start | bytes 98308
  92.0 34.6 %copy-start.29 = (bf16[256,64]{0,1:T(8,128)(2,1)}, bf16[256,64]{0,1:T(8,128)(2,1)S(1)}, u32[]{:S(2)}) copy-start(bf16[256,64]{0,1:T(8,128)(2,1)S(1)} %convolution_convert_fusion.21) | copy-start | bytes 98308
  92.8 33.9 %copy-start.31 = (bf16[256,64]{0,1:T(8,128)(2,1)}, bf16[256,64]{0,1:T(8,128)(2,1)S(1)}, u32[]{:S(2)}) copy-start(bf16[256,64]{0,1:T(8,128)(2,1)S(1)} %get-tuple-element.83) | copy-start | bytes 98308
  97.3 17.3 %copy-start.10 = (bf16[256,1024]{0,1:T(8,128)(2,1)}, bf16[256,1024]{0,1:T(8,128)(2,1)S(1)}, u32[]{:S(2)}) copy-start(bf16[256,1024]{0,1:T(8,128)(2,1)S(1)} %fusion.15) | copy-start | bytes 1572868
  102.1 12.6 copy-start.12
  107.0 8.0 copy-start.14
  111.8 3.9 copy-start.16
  117.3 17.7 %collective-permute-start.9 = (bf16[256,256]{0,1:T(8,128)(2,1)}, bf16[256,256]{0,1:T(8,128)(2,1)}, u32[]{:S(2)}, u32[]{:S(2)}) collective-permute-start(bf16[256,256]{0,1:T(8,128)(2,1)} %pad_maximum_fusion.8), channel_id=1, source_target_pairs={{4,0},{8,4},{12,8},{16,12},{20,16},{24,20},{28,24},{32,28},{36,32}... | collective-permute-start | bytes 393224 | tf_op jit(solution)/shard_map/ppermute | solution.py:13
  119.2 17.2 %collective-permute-start.10 = (bf16[256,256]{0,1:T(8,128)(2,1)}, bf16[256,256]{0,1:T(8,128)(2,1)}, u32[]{:S(2)}, u32[]{:S(2)}) collective-permute-start(bf16[256,256]{0,1:T(8,128)(2,1)} %pad_maximum_fusion.9), channel_id=1, source_target_pairs={{8,0},{12,4},{16,8},{20,12},{24,16},{28,20},{32,24},{36,28},{40,32... | collective-permute-start | bytes 393224 | tf_op jit(solution)/shard_map/ppermute | solution.py:13
  121.2 15.2 %collective-permute-start.11 = (bf16[256,256]{0,1:T(8,128)(2,1)}, bf16[256,256]{0,1:T(8,128)(2,1)}, u32[]{:S(2)}, u32[]{:S(2)}) collective-permute-start(bf16[256,256]{0,1:T(8,128)(2,1)} %pad_maximum_fusion.10), channel_id=1, source_target_pairs={{12,0},{16,4},{20,8},{24,12},{28,16},{32,20},{36,24},{40,28},{44,3... | collective-permute-start | bytes 393224 | tf_op jit(solution)/shard_map/ppermute | solution.py:13
  123.2 14.3 collective-permute-start.6
  125.3 12.3 collective-permute-start.7
  127.8 105.5 %reduce-scatter.9.cloned.1.call-start = ((), (), s32[]{:S(2)}) async-start(), calls=%async_computation.5 | async-start | bytes 655360 | tf_op jit(solution)/shard_map/reduce_scatter | solution.py:150
  134.8 13.2 copy-start.3
  134.9 13.1 copy-start.18
  134.9 13.1 copy-start.19
  135.0 13.0 collective-permute-start.8
  137.6 11.8 copy-start.5
  150.6 713.9 %reduce-scatter.11.cloned.1.call-start = ((), (), s32[]{:S(2)}) async-start(), calls=%async_computation.6 | async-start | bytes 1056768 | tf_op jit(solution)/shard_map/reduce_scatter | solution.py:158
  152.7 1336.3 %reduce-scatter.13.cloned.1.call-start = ((), (), s32[]{:S(2)}) async-start(), calls=%async_computation.7 | async-start | bytes 1056768
  (28 other events, 43.5 us)
Sparse Core Ops, SparseCore 0:
  127.9 57.9 reduce-scatter.6
  189.8 43.4 reduce-scatter.8
  236.6 627.7 reduce-scatter.10
  867.9 621.0 reduce-scatter.12
where the time goes:
time: 1500 us
  waiting for transfers between devices  1350 us (90%)
  matrix products  65.8 us (4%)
  starting transfers between devices  28.2 us (2%)
  blocking collectives  19.9 us (1%)
    reduce_scatter x1, waiting for transfers between devices, per_device(): lax.psum_scatter(out_weight_term, 'seq', scatter_dimension=1, tiled=True)  631 us
    unnamed x5, waiting for transfers between devices  625 us
    reduce_scatter x1, waiting for transfers between devices, per_device(): lax.psum_scatter(rounded.astype(jnp.float32).astype(jnp.bfloat16), 'head'...  47.4 us
    dot_general x32, matrix products, block_scores(): jnp.dot(left, part.T, preferred_element_type=jnp.float32) * factor  44.7 us
    reduce_scatter x1, waiting for transfers between devices, per_device(): lax.psum_scatter(lax.optimization_barrier(part).astype(jnp.float32).astyp...  31.4 us
  transfers between devices with their start and end apart: 16, of which 5 were waited for; matrix products, arithmetic and copies ran while one was open for 4% of the time, Pallas kernels for 0%

commit v1 on v0

v1 whole, which is shorter than its diff:
```python
import functools

import jax
import jax.numpy as jnp
from jax import lax
from jax.experimental import pallas as pl
from jax.experimental.pallas import tpu as pltpu
from jax.sharding import PartitionSpec as P

HEAD_DIM = 64
WINDOW = 4
FAR = 1e30
VMEM_LIMIT = 48 * 1024 * 1024

F32 = jnp.float32
BF16 = jnp.bfloat16


def dot_nn(left, right):
    return jnp.dot(left, right, preferred_element_type=F32)


def dot_nt(left, right):
    return lax.dot_general(left, right, (((1,), (1,)), ((), ())), preferred_element_type=F32)


def dot_tn(left, right):
    return lax.dot_general(left, right, (((0,), (0,)), ((), ())), preferred_element_type=F32)


def turned(array):
    return jnp.transpose(array.astype(F32)).astype(BF16)


def call(kernel, outs, operands, scratch=(), smem=0, flops=0, transcendentals=0):
    specs = [pl.BlockSpec(memory_space=pltpu.SMEM)] * smem
    specs += [pl.BlockSpec(memory_space=pltpu.VMEM)] * (len(operands) - smem)
    touched = sum(o.size * o.dtype.itemsize for o in (*operands, *outs))
    return pl.pallas_call(
        kernel,
        out_shape=outs,
        in_specs=specs,
        out_specs=[pl.BlockSpec(memory_space=pltpu.VMEM)] * len(outs),
        scratch_shapes=list(scratch),
        compiler_params=pltpu.CompilerParams(vmem_limit_bytes=VMEM_LIMIT),
        cost_estimate=pl.CostEstimate(
            flops=flops, bytes_accessed=touched, transcendentals=transcendentals
        ),
    )(*operands)


def shape_of(shape, dtype):
    return jax.ShapeDtypeStruct(shape, dtype)


def head_rows(array, head):
    rows = lax.broadcasted_iota(jnp.int32, array.shape, 0)
    inside = (rows >= head * HEAD_DIM) & (rows < (head + 1) * HEAD_DIM)
    return jnp.where(inside, array, jnp.zeros_like(array))


def kv_kernel(frames_ref, key_weight_ref, value_weight_ref, kv_ref):
    span = key_weight_ref.shape[1]
    kv_ref[:, :span] = dot_nn(frames_ref[...], key_weight_ref[...]).astype(BF16)
    kv_ref[:, span:] = dot_nn(frames_ref[...], value_weight_ref[...]).astype(BF16)


def query_kernel(frames_ref, grads_ref, query_weight_ref, out_weight_ref, qt_ref, back_ref):
    queries = dot_nn(frames_ref[...], query_weight_ref[...]).astype(BF16).astype(F32)
    qt_ref[...] = (jnp.transpose(queries) * (HEAD_DIM**-0.5)).astype(BF16)
    back_ref[...] = dot_nt(out_weight_ref[...], grads_ref[...]).astype(BF16)


def relay_kernel(head_ref, before_ref, after_ref, relay_ref):
    odd = lax.rem(head_ref[0], 2) == 1

    @pl.when(odd)
    def _():
        relay_ref[...] = after_ref[...]

    @pl.when(jnp.logical_not(odd))
    def _():
        relay_ref[...] = before_ref[...]


def attention_kernel(
    mask_ref, qt_ref, bt_ref, kv0, kv1, kv2, kv3, att_ref, dq_ref, own_ref, far1, far2, far3,
    soft, grad, back_stack, query_stack, att_t, dq_t,
):
    kvs = (kv0, kv1, kv2, kv3)
    span, count = qt_ref.shape
    heads = span // HEAD_DIM
    keep = [None] + [mask_ref[0, k] > 0 for k in range(WINDOW - 1)]
    keys_t = [turned(kv[:, :span]) for kv in kvs]
    values_t = [turned(kv[:, span:]) for kv in kvs]
    for head in range(heads):
        mine = slice(head * HEAD_DIM, (head + 1) * HEAD_DIM)
        lanes = slice(head * count, (head + 1) * count)
        query = head_rows(qt_ref[...], head)
        back = head_rows(bt_ref[...], head)
        query_stack[:, lanes] = query
        back_stack[:, lanes] = back
        scores = [dot_nn(kv[:, :span], query) for kv in kvs]
        top = jnp.max(scores[0], axis=0, keepdims=True)
        for k in range(1, WINDOW):
            block_top = jnp.max(scores[k], axis=0, keepdims=True)
            top = jnp.maximum(top, jnp.where(keep[k], block_top, -FAR))
        raised = [jnp.exp(scores[0] - top)]
        for k in range(1, WINDOW):
            raised.append(jnp.exp(scores[k] - jnp.where(keep[k], top, FAR)))
        total = sum(jnp.sum(part, axis=0, keepdims=True) for part in raised)
        inverse = 1.0 / total
        weights = [part * inverse for part in raised]
        out = jnp.zeros((HEAD_DIM, count), F32)
        for k in range(WINDOW):
            rounded = weights[k].astype(BF16)
            soft[k, :, lanes] = rounded
            out = out + dot_nn(values_t[k][mine, :], rounded)
        out = out.astype(BF16).astype(F32)
        att_t[mine, :] = out
        back_dot = jnp.sum(out * bt_ref[mine, :].astype(F32), axis=0, keepdims=True)
        out = jnp.zeros((HEAD_DIM, count), F32)
        for k in range(WINDOW):
            back_scores = dot_nn(kvs[k][:, span:], back)
            score_grad = (weights[k] * (back_scores - back_dot)).astype(BF16)
            grad[k, :, lanes] = score_grad
            out = out + dot_nn(keys_t[k][mine, :], score_grad)
        dq_t[mine, :] = out * (HEAD_DIM**-0.5)
    for k, far in ((1, far1), (2, far2), (3, far3)):
        far[:, :span] = dot_nt(grad[k], query_stack[...]).astype(BF16)
        far[:, span:] = dot_nt(soft[k], back_stack[...]).astype(BF16)
    own_ref[:, :span] = dot_nt(grad[0], query_stack[...])
    own_ref[:, span:] = dot_nt(soft[0], back_stack[...])
    att_ref[...] = jnp.transpose(att_t[...]).astype(BF16)
    dq_ref[...] = jnp.transpose(dq_t[...]).astype(BF16)


def shares(head_ref, term, outs):
    half = outs[0].shape[0]
    for other, out in enumerate(outs):
        start = pl.multiple_of(jnp.bitwise_xor(head_ref[0], other) * half, half)
        out[...] = term[pl.ds(start, half), :].astype(BF16)


def added(parts):
    total = parts[0][...].astype(F32)
    for part in parts[1:]:
        total = total + part[...].astype(F32)
    return total


def mix_kernel(head_ref, att_ref, out_weight_ref, grads_ref, own_ref, send1, send2, send3, term_ref, held):
    held[...] = dot_nn(att_ref[...], out_weight_ref[...])
    shares(head_ref, held, (own_ref, send1, send2, send3))
    term_ref[...] = dot_tn(grads_ref[...], att_ref[...])


def weights_kernel(
    cuts, frames_ref, own_ref, far1, far2, far3, out_term_ref, part0, part1, part2, part3,
    kv_grad_ref, terms_ref, mixed_ref,
):
    outer, inner, tail = cuts
    rounded = added((own_ref, far1, far2, far3)).astype(BF16)
    kv_grad_ref[...] = rounded
    span = rounded.shape[1] // 2
    value_term = dot_tn(frames_ref[...], rounded[:, span:]).reshape(outer, inner, tail, span)
    out_term = out_term_ref[...].reshape(outer, inner, tail, span)
    for i in range(inner):
        piece = jnp.stack([value_term[:, i], out_term[:, i]], axis=1)
        terms_ref[i] = piece.reshape(2 * outer * tail, span).astype(BF16)
    mixed_ref[...] = added((part0, part1, part2, part3)).astype(BF16)


def input_kernel(
    head_ref, dq_ref, kv_grad_ref, query_weight_ref, key_weight_ref, value_weight_ref,
    own_ref, send1, send2, send3, held,
):
    span = dq_ref.shape[1]
    term = dot_nt(dq_ref[...], query_weight_ref[...])
    term = term + dot_nt(kv_grad_ref[:, :span], key_weight_ref[...])
    held[...] = term + dot_nt(kv_grad_ref[:, span:], value_weight_ref[...])
    shares(head_ref, held, (own_ref, send1, send2, send3))


def near_kernel(pieces_ref, part0, part1, part2, part3, terms_ref, frames_grad_ref):
    terms_ref[...] = added([pieces_ref.at[i] for i in range(pieces_ref.shape[0])]).astype(BF16)
    frames_grad_ref[...] = added((part0, part1, part2, part3)).astype(BF16)


def far_kernel(pieces_ref, value_ref, out_ref):
    total = added([pieces_ref.at[i] for i in range(pieces_ref.shape[0])])
    rows = value_ref.shape[0]
    value_ref[...] = total[:rows]
    out_ref[...] = total[rows:]


def passed_along(value, steps):
    count = lax.axis_size("seq")
    return lax.ppermute(value, "seq", [(i, (i + steps) % count) for i in range(count)])


def relayed(value):
    count, groups = lax.axis_size("seq"), lax.axis_size("head")
    pairs = []
    for i in range(count):
        for group in range(groups):
            to = (i + (1 if group % 2 == 0 else -1)) % count
            pairs.append((i * groups + group, to * groups + group))
    return lax.ppermute(value, ("seq", "head"), pairs)


def exchanged(sends):
    count = lax.axis_size("head")
    received = {}
    for other in range(count - 1, 0, -1):
        pairs = [(i, i ^ other) for i in range(count)]
        received[other] = lax.ppermute(sends[other - 1], "head", pairs)
    return [received[other] for other in range(1, count)]


def per_device(inner, frames_in, query_weight, key_weight, value_weight, out_weight, read_mask, out_grad):
    seq = lax.axis_size("seq")
    groups = lax.axis_size("head")
    outer = seq // inner
    width, span = query_weight.shape
    tail = width // seq
    near = [[o * inner + i for i in range(inner)] for o in range(outer)]
    across = [[o * inner + i for o in range(outer)] for i in range(inner)]
    mask = lax.dynamic_slice_in_dim(read_mask, lax.axis_index("seq"), 1, 0)
    group = jnp.full((1,), lax.axis_index("head"), jnp.int32)

    share = frames_in.shape[0]
    count = groups * share
    square = 2 * count * span
    heads = span // HEAD_DIM
    pairs = heads * WINDOW * count * count
    side = shape_of((span, count), BF16)
    shared = [shape_of((share, width), BF16)] * groups
    held = pltpu.VMEM((count, width), F32)

    frames = lax.all_gather(frames_in, "head", axis=0, tiled=True)
    kv_shape = shape_of((count, 2 * span), BF16)
    [kv] = call(kv_kernel, [kv_shape], [frames, key_weight, value_weight], flops=2 * square * width)
    kv3 = passed_along(kv, 3)
    kv1 = passed_along(kv, 1)
    grads = lax.all_gather(out_grad, "head", axis=0, tiled=True)
    [relay] = call(relay_kernel, [kv_shape], [group, kv1, kv3], smem=1)
    kv2 = relayed(relay)
    qt, bt = call(
        query_kernel,
        [side, side],
        [frames, grads, query_weight, out_weight],
        flops=2 * square * width,
    )
    attended, dq, own, *fars = call(
        attention_kernel,
        [shape_of((count, span), BF16)] * 2
        + [shape_of((count, 2 * span), F32)]
        + [kv_shape] * (WINDOW - 1),
        [mask, qt, bt, kv, kv1, kv2, kv3],
        [pltpu.VMEM((WINDOW, count, heads * count), BF16)] * 2
        + [pltpu.VMEM((span, heads * count), BF16)] * 2
        + [pltpu.VMEM((span, count), F32)] * 2,
        smem=1,
        flops=12 * pairs * span,
        transcendentals=pairs,
    )
    fars = [passed_along(fars[k - 1], -k) for k in range(1, WINDOW)]
    kept, *sends, out_term = call(
        mix_kernel,
        [*shared, shape_of((width, span), F32)],
        [group, attended, out_weight, grads],
        [held],
        smem=1,
        flops=2 * square * width,
    )
    kv_grad, terms, mixed = call(
        functools.partial(weights_kernel, (outer, inner, tail)),
        [kv_shape, shape_of((inner, 2 * outer * tail, span), BF16), shared[0]],
        [frames, own, *fars, out_term, kept, *exchanged(sends)],
        flops=square * width,
    )
    terms = lax.all_to_all(terms, "seq", 0, 0, axis_index_groups=near, tiled=True)
    kept, *sends = call(
        input_kernel,
        shared,
        [group, dq, kv_grad, query_weight, key_weight, value_weight],
        [held],
        smem=1,
        flops=3 * square * width,
    )
    terms, frames_grad = call(
        near_kernel,
        [shape_of((2 * outer * tail, span), BF16), shared[0]],
        [terms, kept, *exchanged(sends)],
    )
    terms = terms.reshape(outer, 2 * tail, span)
    terms = lax.all_to_all(terms, "seq", 0, 0, axis_index_groups=across, tiled=True)
    value_sum, out_sum = call(far_kernel, [shape_of((tail, span), F32)] * 2, [terms])
    return mixed, frames_grad, value_sum, out_sum.T


def solution(mesh):
    in_specs = (
        P(("seq", "head"), None),
        P(None, "head"),
        P(None, "head"),
        P(None, "head"),
        P("head", None),
        P(),
        P(("seq", "head"), None),
    )
    out_specs = (
        P(("seq", "head"), None),
        P(("seq", "head"), None),
        P("seq", "head"),
        P("head", "seq"),
    )
    return jax.shard_map(
        functools.partial(per_device, min(8, mesh.shape["seq"])),
        mesh=mesh,
        in_specs=in_specs,
        out_specs=out_specs,
        check_vma=False,
    )
```

time: 1500 us -> 144 us (0.10)
  the two profiles are of different devices: /device:TPU:4 before, /device:TPU:1 now
where the time goes in v1:
time: 144 us; the launch traced here: 142 us
  blocking collectives  49.9 us (35%)
  starting transfers between devices  43 us (30%)
  waiting for transfers between devices  35 us (24%)
  Pallas kernels  10.7 us (7%)
  local copies, waits for them, and re-layouts  2.26 us (2%)
    all_to_all x1, blocking collectives, per_device(): lax.all_to_all(terms, 'seq', 0, 0, axis_index_groups=across, tiled=True)  25.9 us
    ppermute x6, starting transfers between devices, exchanged(): received[other] = lax.ppermute(sends[other - 1], 'head', pairs)  21.3 us
    ppermute x5, waiting for transfers between devices, passed_along(): lax.ppermute(value, 'seq', [(i, (i + steps) % count) for i in range(count)])  17.7 us
    ppermute x6, waiting for transfers between devices, exchanged(): received[other] = lax.ppermute(sends[other - 1], 'head', pairs)  17.3 us
    ppermute x5, starting transfers between devices, passed_along(): lax.ppermute(value, 'seq', [(i, (i + steps) % count) for i in range(count)])  16 us
    all_gather x1, blocking collectives, per_device(): frames = lax.all_gather(frames_in, 'head', axis=0, tiled=True)  15.1 us
    pallas_call x9, Pallas kernels, call(): pl.pallas_call(kernel, out_shape=outs, in_specs=specs, out_specs=[pl.Bloc...  10.7 us
    all_gather x1, blocking collectives, per_device(): grads = lax.all_gather(out_grad, 'head', axis=0, tiled=True)  8.97 us
  transfers between devices with their start and end apart: 13, of which 6 were waited for; matrix products, arithmetic and copies ran while one was open for 0% of the time, Pallas kernels for 1%

profile of v1, /device:TPU:1, one launch (start us, length us, event | category | flops | bytes accessed | tf_op | source)
XLA Modules:
  0.0 141.8 jit_solution(17743518228461718188)
XLA Ops:
  0.7 15.1 %all_gather.6.frames_ref = bf16[256,1024]{1,0:T(8,128)(2,1)S(1)} all-gather(bf16[64,1024]{1,0:T(8,128)(2,1)} %param.7), channel_id=1, replica_groups=mesh['seq'=128,'head'=4] {'head'}, dimensions={0}, use_global_device_ids=true | all-gather | bytes 655360 | tf_op jit(solution)/shard_map/all_gather | solution.py:241
  15.7 1.0 copy-done.2
  16.8 0.4 shard_map.103.kv0
  17.2 1.9 %collective-permute-start.1 = (bf16[256,512]{1,0:T(8,128)(2,1)S(1)}, bf16[256,512]{1,0:T(8,128)(2,1)S(1)}, u32[]{:S(2)}, u32[]{:S(2)}) collective-permute-start(bf16[256,512]{1,0:T(8,128)(2,1)S(1)} %shard_map.103.kv0), channel_id=1, source_target_pairs={{0,12},{4,16},{8,20},{12,24},{16,28},{20,32},{24,36},{28,40},{32,4... | collective-permute-start | bytes 786440 | tf_op jit(solution)/shard_map/ppermute | solution.py:199
  19.1 1.9 %collective-permute-start = (bf16[256,512]{1,0:T(8,128)(2,1)S(1)}, bf16[256,512]{1,0:T(8,128)(2,1)S(1)}, u32[]{:S(2)}, u32[]{:S(2)}) collective-permute-start(bf16[256,512]{1,0:T(8,128)(2,1)S(1)} %shard_map.103.kv0), channel_id=1, source_target_pairs={{0,4},{4,8},{8,12},{12,16},{16,20},{20,24},{24,28},{28,32},{32,36}... | collective-permute-start | bytes 786440 | tf_op jit(solution)/shard_map/ppermute | solution.py:199
  21.1 10.6 %collective-permute-done.1.after_ref.kv3 = bf16[256,512]{1,0:T(8,128)(2,1)S(1)} collective-permute-done((bf16[256,512]{1,0:T(8,128)(2,1)S(1)}, bf16[256,512]{1,0:T(8,128)(2,1)S(1)}, u32[]{:S(2)}, u32[]{:S(2)}) %collective-permute-start.1) | collective-permute-done | bytes 262176 | tf_op jit(solution)/shard_map/ppermute | solution.py:199
  31.7 7.1 %collective-permute-done.before_ref.kv1 = bf16[256,512]{1,0:T(8,128)(2,1)S(1)} collective-permute-done((bf16[256,512]{1,0:T(8,128)(2,1)S(1)}, bf16[256,512]{1,0:T(8,128)(2,1)S(1)}, u32[]{:S(2)}, u32[]{:S(2)}) %collective-permute-start) | collective-permute-done | bytes 262176 | tf_op jit(solution)/shard_map/ppermute | solution.py:199
  38.8 2.1 %collective-permute-start.2 = (bf16[256,512]{1,0:T(8,128)(2,1)S(1)}, bf16[256,512]{1,0:T(8,128)(2,1)S(1)}, u32[]{:S(2)}, u32[]{:S(2)}) collective-permute-start(bf16[256,512]{1,0:T(8,128)(2,1)S(1)} %shard_map.104), channel_id=1, source_target_pairs={{0,4},{1,509},{2,6},{3,511},{4,8},{5,1},{6,10},{7,3},{8,12},{9,5},... | collective-permute-start | bytes 786440 | tf_op jit(solution)/shard_map/ppermute | solution.py:209
  41.0 9.0 %all_gather.7.grads_ref = bf16[256,1024]{1,0:T(8,128)(2,1)S(1)} all-gather(bf16[64,1024]{1,0:T(8,128)(2,1)S(1)} %copy-done.7), channel_id=1, replica_groups=mesh['seq'=128,'head'=4] {'head'}, dimensions={0}, use_global_device_ids=true | all-gather | bytes 655360 | tf_op jit(solution)/shard_map/all_gather | solution.py:246
  50.0 0.5 shard_map.102
  50.5 6.1 %shard_map.105 = (bf16[256,256]{1,0:T(8,128)(2,1)S(1)}, bf16[256,256]{1,0:T(8,128)(2,1)S(1)}, f32[256,512]{1,0:T(8,128)S(1)}, bf16[256,512]{1,0:T(8,128)(2,1)S(1...) custom-call(s32[1,3]{1,0:T(1,128)S(1)} %copy.12.mask_ref, bf16[256,256]{1,0:T(8,128)(2,1)S(1)} %get-tuple-element.28.qt_ref, ...), custom_call_target="tpu_custom_call" | custom-call | flops 3221225472 | bytes 2883596 | tf_op jit(solution)/shard_map/pallas_call | solution.py:39
  56.6 0.5 shard_map.106
  57.1 3.5 %collective-permute-start.6 = (bf16[64,1024]{1,0:T(8,128)(2,1)S(1)}, bf16[64,1024]{1,0:T(8,128)(2,1)S(1)}, u32[]{:S(2)}, u32[]{:S(2)}) collective-permute-start(bf16[64,1024]{1,0:T(8,128)(2,1)S(1)} %get-tuple-element.37), channel_id=1, source_target_pairs={{0,1},{1,0},{2,3},{3,2},{4,5},{5,4},{6,7},{7,6},{8,9},{9,8},{10,11... | collective-permute-start | bytes 393224 | tf_op jit(solution)/shard_map/ppermute | solution.py:217
  60.6 8.4 %collective-permute-start.3 = (bf16[256,512]{1,0:T(8,128)(2,1)S(1)}, bf16[256,512]{1,0:T(8,128)(2,1)S(1)}, u32[]{:S(2)}, u32[]{:S(2)}) collective-permute-start(bf16[256,512]{1,0:T(8,128)(2,1)S(1)} %get-tuple-element.31), channel_id=1, source_target_pairs={{0,508},{4,0},{8,4},{12,8},{16,12},{20,16},{24,20},{28,24},{32,28}... | collective-permute-start | bytes 786440 | tf_op jit(solution)/shard_map/ppermute | solution.py:199
  69.0 1.9 %collective-permute-start.4 = (bf16[256,512]{1,0:T(8,128)(2,1)S(1)}, bf16[256,512]{1,0:T(8,128)(2,1)S(1)}, u32[]{:S(2)}, u32[]{:S(2)}) collective-permute-start(bf16[256,512]{1,0:T(8,128)(2,1)S(1)} %get-tuple-element.32), channel_id=1, source_target_pairs={{0,504},{4,508},{8,0},{12,4},{16,8},{20,12},{24,16},{28,20},{32,24... | collective-permute-start | bytes 786440 | tf_op jit(solution)/shard_map/ppermute | solution.py:199
  70.9 1.9 %collective-permute-start.5 = (bf16[256,512]{1,0:T(8,128)(2,1)S(1)}, bf16[256,512]{1,0:T(8,128)(2,1)S(1)}, u32[]{:S(2)}, u32[]{:S(2)}) collective-permute-start(bf16[256,512]{1,0:T(8,128)(2,1)S(1)} %get-tuple-element.33), channel_id=1, source_target_pairs={{0,500},{4,504},{8,508},{12,0},{16,4},{20,8},{24,12},{28,16},{32,2... | collective-permute-start | bytes 786440 | tf_op jit(solution)/shard_map/ppermute | solution.py:199
  72.8 3.8 %collective-permute-start.7 = (bf16[64,1024]{1,0:T(8,128)(2,1)S(1)}, bf16[64,1024]{1,0:T(8,128)(2,1)S(1)}, u32[]{:S(2)}, u32[]{:S(2)}) collective-permute-start(bf16[64,1024]{1,0:T(8,128)(2,1)S(1)} %get-tuple-element.38), channel_id=1, source_target_pairs={{0,2},{1,3},{2,0},{3,1},{4,6},{5,7},{6,4},{7,5},{8,10},{9,11},{10,... | collective-permute-start | bytes 393224 | tf_op jit(solution)/shard_map/ppermute | solution.py:217
  76.6 4.1 %collective-permute-start.8 = (bf16[64,1024]{1,0:T(8,128)(2,1)S(1)}, bf16[64,1024]{1,0:T(8,128)(2,1)S(1)}, u32[]{:S(2)}, u32[]{:S(2)}) collective-permute-start(bf16[64,1024]{1,0:T(8,128)(2,1)S(1)} %get-tuple-element.39), channel_id=1, source_target_pairs={{0,3},{1,2},{2,1},{3,0},{4,7},{5,6},{6,5},{7,4},{8,11},{9,10},{10,... | collective-permute-start | bytes 393224 | tf_op jit(solution)/shard_map/ppermute | solution.py:217
  80.7 5.5 %collective-permute-done.7.part2 = bf16[64,1024]{1,0:T(8,128)(2,1)S(1)} collective-permute-done((bf16[64,1024]{1,0:T(8,128)(2,1)S(1)}, bf16[64,1024]{1,0:T(8,128)(2,1)S(1)}, u32[]{:S(2)}, u32[]{:S(2)}) %collective-permute-start.7) | collective-permute-done | bytes 131104 | tf_op jit(solution)/shard_map/ppermute | solution.py:217
  86.2 2.8 %collective-permute-done.8.part3 = bf16[64,1024]{1,0:T(8,128)(2,1)S(1)} collective-permute-done((bf16[64,1024]{1,0:T(8,128)(2,1)S(1)}, bf16[64,1024]{1,0:T(8,128)(2,1)S(1)}, u32[]{:S(2)}, u32[]{:S(2)}) %collective-permute-start.8) | collective-permute-done | bytes 131104 | tf_op jit(solution)/shard_map/ppermute | solution.py:217
  89.0 1.2 shard_map.107
  90.2 1.0 copy-done.6
  91.2 3.7 %all-to-all-start = ((bf16[8,256,256]{2,1,0:T(8,128)(2,1)}), bf16[8,256,256]{2,1,0:T(8,128)(2,1)S(1)}, u32[]{:S(2)}, u32[]{:S(2)}) async-start(bf16[8,256,256]{2,1,0:T(8,128)(2,1)} %copy-done.6), calls=%async_computation | async-start | bytes 2097152 | tf_op jit(solution)/shard_map/all_to_all | solution.py:283
  94.9 0.7 shard_map.108
  95.6 2.9 %collective-permute-start.9 = (bf16[64,1024]{1,0:T(8,128)(2,1)S(1)}, bf16[64,1024]{1,0:T(8,128)(2,1)S(1)}, u32[]{:S(2)}, u32[]{:S(2)}) collective-permute-start(bf16[64,1024]{1,0:T(8,128)(2,1)S(1)} %get-tuple-element.45), channel_id=1, source_target_pairs={{0,1},{1,0},{2,3},{3,2},{4,5},{5,4},{6,7},{7,6},{8,9},{9,8},{10,11... | collective-permute-start | bytes 393224 | tf_op jit(solution)/shard_map/ppermute | solution.py:217
  98.5 3.8 %collective-permute-start.10 = (bf16[64,1024]{1,0:T(8,128)(2,1)S(1)}, bf16[64,1024]{1,0:T(8,128)(2,1)S(1)}, u32[]{:S(2)}, u32[]{:S(2)}) collective-permute-start(bf16[64,1024]{1,0:T(8,128)(2,1)S(1)} %get-tuple-element.46), channel_id=1, source_target_pairs={{0,2},{1,3},{2,0},{3,1},{4,6},{5,7},{6,4},{7,5},{8,10},{9,11},{10,... | collective-permute-start | bytes 393224 | tf_op jit(solution)/shard_map/ppermute | solution.py:217
  102.3 3.2 %collective-permute-start.11 = (bf16[64,1024]{1,0:T(8,128)(2,1)S(1)}, bf16[64,1024]{1,0:T(8,128)(2,1)S(1)}, u32[]{:S(2)}, u32[]{:S(2)}) collective-permute-start(bf16[64,1024]{1,0:T(8,128)(2,1)S(1)} %get-tuple-element.47), channel_id=1, source_target_pairs={{0,3},{1,2},{2,1},{3,0},{4,7},{5,6},{6,5},{7,4},{8,11},{9,10},{10,... | collective-permute-start | bytes 393224 | tf_op jit(solution)/shard_map/ppermute | solution.py:217
  105.5 4.8 %collective-permute-done.10.part2 = bf16[64,1024]{1,0:T(8,128)(2,1)S(1)} collective-permute-done((bf16[64,1024]{1,0:T(8,128)(2,1)S(1)}, bf16[64,1024]{1,0:T(8,128)(2,1)S(1)}, u32[]{:S(2)}, u32[]{:S(2)}) %collective-permute-start.10) | collective-permute-done | bytes 131104 | tf_op jit(solution)/shard_map/ppermute | solution.py:217
  110.3 4.2 %collective-permute-done.11.part3 = bf16[64,1024]{1,0:T(8,128)(2,1)S(1)} collective-permute-done((bf16[64,1024]{1,0:T(8,128)(2,1)S(1)}, bf16[64,1024]{1,0:T(8,128)(2,1)S(1)}, u32[]{:S(2)}, u32[]{:S(2)}) %collective-permute-start.11) | collective-permute-done | bytes 131104 | tf_op jit(solution)/shard_map/ppermute | solution.py:217
  114.6 0.7 shard_map.109
  115.3 25.9 %all_to_all.10.pieces_ref = bf16[16,16,256]{2,1,0:T(8,128)(2,1)S(1)} all-to-all(bf16[16,16,256]{2,1,0:T(8,128)(2,1)S(1)} %bitcast.3), channel_id=1, replica_groups={{0,32,64,96,128,160,192,224,256,288,320,352,384,416,448,480},{4,36,68,1..., dimensions={0} | all-to-all | bytes 262144 | tf_op jit(solution)/shard_map/all_to_all | solution.py:298
  141.2 0.6 shard_map.110
  (24 shorter events, 0.2 us)
Async XLA Ops:
  0.6 40.2 %copy-start = (s32[128,3]{0,1:T(4,128)S(1)}, s32[128,3]{0,1:T(4,128)}, u32[]{:S(2)}) copy-start(s32[128,3]{0,1:T(4,128)} %param.12) | copy-start | bytes 4612
  0.6 15.1 %copy-start.1 = (bf16[1024,256]{1,0:T(8,128)(2,1)S(1)}, bf16[1024,256]{1,0:T(8,128)(2,1)}, u32[]{:S(2)}) copy-start(bf16[1024,256]{1,0:T(8,128)(2,1)} %key_weight_ref.3) | copy-start | bytes 1572868
  15.7 1.0 copy-start.2
  17.2 14.5 %collective-permute-start.1 = (bf16[256,512]{1,0:T(8,128)(2,1)S(1)}, bf16[256,512]{1,0:T(8,128)(2,1)S(1)}, u32[]{:S(2)}, u32[]{:S(2)}) collective-permute-start(bf16[256,512]{1,0:T(8,128)(2,1)S(1)} %shard_map.103.kv0), channel_id=1, source_target_pairs={{0,12},{4,16},{8,20},{12,24},{16,28},{20,32},{24,36},{28,40},{32,4... | collective-permute-start | bytes 786440 | tf_op jit(solution)/shard_map/ppermute | solution.py:199
  19.1 19.6 %collective-permute-start = (bf16[256,512]{1,0:T(8,128)(2,1)S(1)}, bf16[256,512]{1,0:T(8,128)(2,1)S(1)}, u32[]{:S(2)}, u32[]{:S(2)}) collective-permute-start(bf16[256,512]{1,0:T(8,128)(2,1)S(1)} %shard_map.103.kv0), channel_id=1, source_target_pairs={{0,4},{4,8},{8,12},{12,16},{16,20},{20,24},{24,28},{28,32},{32,36}... | collective-permute-start | bytes 786440 | tf_op jit(solution)/shard_map/ppermute | solution.py:199
  38.7 2.3 %copy-start.7 = (bf16[64,1024]{1,0:T(8,128)(2,1)S(1)}, bf16[64,1024]{1,0:T(8,128)(2,1)}, u32[]{:S(2)}) copy-start(bf16[64,1024]{1,0:T(8,128)(2,1)} %param.13) | copy-start | bytes 393220
  38.7 11.3 %copy-start.5 = (bf16[256,1024]{1,0:T(8,128)(2,1)S(1)}, bf16[256,1024]{1,0:T(8,128)(2,1)}, u32[]{:S(2)}) copy-start(bf16[256,1024]{1,0:T(8,128)(2,1)} %out_weight_ref.3) | copy-start | bytes 1572868
  38.8 11.2 %copy-start.4 = (bf16[1024,256]{1,0:T(8,128)(2,1)S(1)}, bf16[1024,256]{1,0:T(8,128)(2,1)}, u32[]{:S(2)}) copy-start(bf16[1024,256]{1,0:T(8,128)(2,1)} %query_weight_ref.3) | copy-start | bytes 1572868
  38.8 11.7 %collective-permute-start.2 = (bf16[256,512]{1,0:T(8,128)(2,1)S(1)}, bf16[256,512]{1,0:T(8,128)(2,1)S(1)}, u32[]{:S(2)}, u32[]{:S(2)}) collective-permute-start(bf16[256,512]{1,0:T(8,128)(2,1)S(1)} %shard_map.104), channel_id=1, source_target_pairs={{0,4},{1,509},{2,6},{3,511},{4,8},{5,1},{6,10},{7,3},{8,12},{9,5},... | collective-permute-start | bytes 786440 | tf_op jit(solution)/shard_map/ppermute | solution.py:209
  57.1 19.5 %collective-permute-start.6 = (bf16[64,1024]{1,0:T(8,128)(2,1)S(1)}, bf16[64,1024]{1,0:T(8,128)(2,1)S(1)}, u32[]{:S(2)}, u32[]{:S(2)}) collective-permute-start(bf16[64,1024]{1,0:T(8,128)(2,1)S(1)} %get-tuple-element.37), channel_id=1, source_target_pairs={{0,1},{1,0},{2,3},{3,2},{4,5},{5,4},{6,7},{7,6},{8,9},{9,8},{10,11... | collective-permute-start | bytes 393224 | tf_op jit(solution)/shard_map/ppermute | solution.py:217
  60.6 28.4 %collective-permute-start.3 = (bf16[256,512]{1,0:T(8,128)(2,1)S(1)}, bf16[256,512]{1,0:T(8,128)(2,1)S(1)}, u32[]{:S(2)}, u32[]{:S(2)}) collective-permute-start(bf16[256,512]{1,0:T(8,128)(2,1)S(1)} %get-tuple-element.31), channel_id=1, source_target_pairs={{0,508},{4,0},{8,4},{12,8},{16,12},{20,16},{24,20},{28,24},{32,28}... | collective-permute-start | bytes 786440 | tf_op jit(solution)/shard_map/ppermute | solution.py:199
  69.0 20.0 %collective-permute-start.4 = (bf16[256,512]{1,0:T(8,128)(2,1)S(1)}, bf16[256,512]{1,0:T(8,128)(2,1)S(1)}, u32[]{:S(2)}, u32[]{:S(2)}) collective-permute-start(bf16[256,512]{1,0:T(8,128)(2,1)S(1)} %get-tuple-element.32), channel_id=1, source_target_pairs={{0,504},{4,508},{8,0},{12,4},{16,8},{20,12},{24,16},{28,20},{32,24... | collective-permute-start | bytes 786440 | tf_op jit(solution)/shard_map/ppermute | solution.py:199
  70.9 18.1 %collective-permute-start.5 = (bf16[256,512]{1,0:T(8,128)(2,1)S(1)}, bf16[256,512]{1,0:T(8,128)(2,1)S(1)}, u32[]{:S(2)}, u32[]{:S(2)}) collective-permute-start(bf16[256,512]{1,0:T(8,128)(2,1)S(1)} %get-tuple-element.33), channel_id=1, source_target_pairs={{0,500},{4,504},{8,508},{12,0},{16,4},{20,8},{24,12},{28,16},{32,2... | collective-permute-start | bytes 786440 | tf_op jit(solution)/shard_map/ppermute | solution.py:199
  72.8 13.4 %collective-permute-start.7 = (bf16[64,1024]{1,0:T(8,128)(2,1)S(1)}, bf16[64,1024]{1,0:T(8,128)(2,1)S(1)}, u32[]{:S(2)}, u32[]{:S(2)}) collective-permute-start(bf16[64,1024]{1,0:T(8,128)(2,1)S(1)} %get-tuple-element.38), channel_id=1, source_target_pairs={{0,2},{1,3},{2,0},{3,1},{4,6},{5,7},{6,4},{7,5},{8,10},{9,11},{10,... | collective-permute-start | bytes 393224 | tf_op jit(solution)/shard_map/ppermute | solution.py:217
  76.6 12.4 %collective-permute-start.8 = (bf16[64,1024]{1,0:T(8,128)(2,1)S(1)}, bf16[64,1024]{1,0:T(8,128)(2,1)S(1)}, u32[]{:S(2)}, u32[]{:S(2)}) collective-permute-start(bf16[64,1024]{1,0:T(8,128)(2,1)S(1)} %get-tuple-element.39), channel_id=1, source_target_pairs={{0,3},{1,2},{2,1},{3,0},{4,7},{5,6},{6,5},{7,4},{8,11},{9,10},{10,... | collective-permute-start | bytes 393224 | tf_op jit(solution)/shard_map/ppermute | solution.py:217
  90.2 1.0 copy-start.6
  91.2 3.7 %copy-start.3 = (bf16[1024,256]{1,0:T(8,128)(2,1)S(1)}, bf16[1024,256]{1,0:T(8,128)(2,1)}, u32[]{:S(2)}) copy-start(bf16[1024,256]{1,0:T(8,128)(2,1)} %value_weight_ref.3) | copy-start | bytes 1572868
  91.2 23.3 %all-to-all-start = ((bf16[8,256,256]{2,1,0:T(8,128)(2,1)}), bf16[8,256,256]{2,1,0:T(8,128)(2,1)S(1)}, u32[]{:S(2)}, u32[]{:S(2)}) async-start(bf16[8,256,256]{2,1,0:T(8,128)(2,1)} %copy-done.6), calls=%async_computation | async-start | bytes 2097152 | tf_op jit(solution)/shard_map/all_to_all | solution.py:283
  95.6 9.9 %collective-permute-start.9 = (bf16[64,1024]{1,0:T(8,128)(2,1)S(1)}, bf16[64,1024]{1,0:T(8,128)(2,1)S(1)}, u32[]{:S(2)}, u32[]{:S(2)}) collective-permute-start(bf16[64,1024]{1,0:T(8,128)(2,1)S(1)} %get-tuple-element.45), channel_id=1, source_target_pairs={{0,1},{1,0},{2,3},{3,2},{4,5},{5,4},{6,7},{7,6},{8,9},{9,8},{10,11... | collective-permute-start | bytes 393224 | tf_op jit(solution)/shard_map/ppermute | solution.py:217
  98.5 11.8 %collective-permute-start.10 = (bf16[64,1024]{1,0:T(8,128)(2,1)S(1)}, bf16[64,1024]{1,0:T(8,128)(2,1)S(1)}, u32[]{:S(2)}, u32[]{:S(2)}) collective-permute-start(bf16[64,1024]{1,0:T(8,128)(2,1)S(1)} %get-tuple-element.46), channel_id=1, source_target_pairs={{0,2},{1,3},{2,0},{3,1},{4,6},{5,7},{6,4},{7,5},{8,10},{9,11},{10,... | collective-permute-start | bytes 393224 | tf_op jit(solution)/shard_map/ppermute | solution.py:217
  102.3 12.3 %collective-permute-start.11 = (bf16[64,1024]{1,0:T(8,128)(2,1)S(1)}, bf16[64,1024]{1,0:T(8,128)(2,1)S(1)}, u32[]{:S(2)}, u32[]{:S(2)}) collective-permute-start(bf16[64,1024]{1,0:T(8,128)(2,1)S(1)} %get-tuple-element.47), channel_id=1, source_target_pairs={{0,3},{1,2},{2,1},{3,0},{4,7},{5,6},{6,5},{7,4},{8,11},{9,10},{10,... | collective-permute-start | bytes 393224 | tf_op jit(solution)/shard_map/ppermute | solution.py:217

commit v2 on v1

--- a/solution.py
+++ b/solution.py
@@ -10,7 +10,7 @@
 HEAD_DIM = 64
 WINDOW = 4
 FAR = 1e30
-VMEM_LIMIT = 48 * 1024 * 1024
+VMEM_LIMIT = 24 * 1024 * 1024
 
 F32 = jnp.float32
 BF16 = jnp.bfloat16
@@ -69,18 +69,6 @@
     queries = dot_nn(frames_ref[...], query_weight_ref[...]).astype(BF16).astype(F32)
     qt_ref[...] = (jnp.transpose(queries) * (HEAD_DIM**-0.5)).astype(BF16)
     back_ref[...] = dot_nt(out_weight_ref[...], grads_ref[...]).astype(BF16)
-
-
-def relay_kernel(head_ref, before_ref, after_ref, relay_ref):
-    odd = lax.rem(head_ref[0], 2) == 1
-
-    @pl.when(odd)
-    def _():
-        relay_ref[...] = after_ref[...]
-
-    @pl.when(jnp.logical_not(odd))
-    def _():
-        relay_ref[...] = before_ref[...]
 
 
 def attention_kernel(
@@ -135,6 +123,25 @@
     dq_ref[...] = jnp.transpose(dq_t[...]).astype(BF16)
 
 
+def added(parts):
+    total = parts[0][...].astype(F32)
+    for part in parts[1:]:
+        total = total + part[...].astype(F32)
+    return total
+
+
+def weights_kernel(cuts, frames_ref, grads_ref, att_ref, own_ref, far1, far2, far3, kv_grad_ref, terms_ref):
+    outer, inner, tail = cuts
+    rounded = added((own_ref, far1, far2, far3)).astype(BF16)
+    kv_grad_ref[...] = rounded
+    span = rounded.shape[1] // 2
+    value_term = dot_tn(frames_ref[...], rounded[:, span:]).reshape(outer, inner, tail, span)
+    out_term = dot_tn(grads_ref[...], att_ref[...]).reshape(outer, inner, tail, span)
+    for i in range(inner):
+        piece = jnp.stack([value_term[:, i], out_term[:, i]], axis=1)
+        terms_ref[i] = piece.reshape(2 * outer * tail, span).astype(BF16)
+
+
 def shares(head_ref, term, outs):
     half = outs[0].shape[0]
     for other, out in enumerate(outs):
@@ -142,44 +149,17 @@
         out[...] = term[pl.ds(start, half), :].astype(BF16)
 
 
-def added(parts):
-    total = parts[0][...].astype(F32)
-    for part in parts[1:]:
-        total = total + part[...].astype(F32)
-    return total
-
-
-def mix_kernel(head_ref, att_ref, out_weight_ref, grads_ref, own_ref, send1, send2, send3, term_ref, held):
-    held[...] = dot_nn(att_ref[...], out_weight_ref[...])
-    shares(head_ref, held, (own_ref, send1, send2, send3))
-    term_ref[...] = dot_tn(grads_ref[...], att_ref[...])
-
-
-def weights_kernel(
-    cuts, frames_ref, own_ref, far1, far2, far3, out_term_ref, part0, part1, part2, part3,
-    kv_grad_ref, terms_ref, mixed_ref,
-):
-    outer, inner, tail = cuts
-    rounded = added((own_ref, far1, far2, far3)).astype(BF16)
-    kv_grad_ref[...] = rounded
-    span = rounded.shape[1] // 2
-    value_term = dot_tn(frames_ref[...], rounded[:, span:]).reshape(outer, inner, tail, span)
-    out_term = out_term_ref[...].reshape(outer, inner, tail, span)
-    for i in range(inner):
-        piece = jnp.stack([value_term[:, i], out_term[:, i]], axis=1)
-        terms_ref[i] = piece.reshape(2 * outer * tail, span).astype(BF16)
-    mixed_ref[...] = added((part0, part1, part2, part3)).astype(BF16)
-
-
 def input_kernel(
-    head_ref, dq_ref, kv_grad_ref, query_weight_ref, key_weight_ref, value_weight_ref,
-    own_ref, send1, send2, send3, held,
+    head_ref, dq_ref, kv_grad_ref, query_weight_ref, key_weight_ref, value_weight_ref, att_ref, out_weight_ref,
+    own_ref, send1, send2, send3, mixed_own_ref, mixed_send1, mixed_send2, mixed_send3, held_mixed, held,
 ):
     span = dq_ref.shape[1]
+    held_mixed[...] = dot_nn(att_ref[...], out_weight_ref[...])
     term = dot_nt(dq_ref[...], query_weight_ref[...])
     term = term + dot_nt(kv_grad_ref[:, :span], key_weight_ref[...])
     held[...] = term + dot_nt(kv_grad_ref[:, span:], value_weight_ref[...])
     shares(head_ref, held, (own_ref, send1, send2, send3))
+    shares(head_ref, held_mixed, (mixed_own_ref, mixed_send1, mixed_send2, mixed_send3))
 
 
 def near_kernel(pieces_ref, part0, part1, part2, part3, terms_ref, frames_grad_ref):
@@ -194,19 +174,14 @@
     out_ref[...] = total[rows:]
 
 
+def mixed_kernel(part0, part1, part2, part3, mixed_ref):
+    mixed_ref[...] = added((part0, part1, part2, part3)).astype(BF16)
+
+
 def passed_along(value, steps):
     count = lax.axis_size("seq")
-    return lax.ppermute(value, "seq", [(i, (i + steps) % count) for i in range(count)])
-
-
-def relayed(value):
-    count, groups = lax.axis_size("seq"), lax.axis_size("head")
-    pairs = []
-    for i in range(count):
-        for group in range(groups):
-            to = (i + (1 if group % 2 == 0 else -1)) % count
-            pairs.append((i * groups + group, to * groups + group))
-    return lax.ppermute(value, ("seq", "head"), pairs)
+    first, last = max(0, -steps), min(count, count - steps)
+    return lax.ppermute(value, "seq", [(i, i + steps) for i in range(first, last)])
 
 
 def exchanged(sends):
@@ -235,17 +210,13 @@
     heads = span // HEAD_DIM
     pairs = heads * WINDOW * count * count
     side = shape_of((span, count), BF16)
-    shared = [shape_of((share, width), BF16)] * groups
+    kv_shape = shape_of((count, 2 * span), BF16)
     held = pltpu.VMEM((count, width), F32)
 
     frames = lax.all_gather(frames_in, "head", axis=0, tiled=True)
-    kv_shape = shape_of((count, 2 * span), BF16)
     [kv] = call(kv_kernel, [kv_shape], [frames, key_weight, value_weight], flops=2 * square * width)
-    kv3 = passed_along(kv, 3)
-    kv1 = passed_along(kv, 1)
+    kvs = [kv] + [passed_along(kv, steps) for steps in range(1, WINDOW)]
     grads = lax.all_gather(out_grad, "head", axis=0, tiled=True)
-    [relay] = call(relay_kernel, [kv_shape], [group, kv1, kv3], smem=1)
-    kv2 = relayed(relay)
     qt, bt = call(
         query_kernel,
         [side, side],
@@ -257,7 +228,7 @@
         [shape_of((count, span), BF16)] * 2
         + [shape_of((count, 2 * span), F32)]
         + [kv_shape] * (WINDOW - 1),
-        [mask, qt, bt, kv, kv1, kv2, kv3],
+        [mask, qt, bt, *kvs],
         [pltpu.VMEM((WINDOW, count, heads * count), BF16)] * 2
         + [pltpu.VMEM((span, heads * count), BF16)] * 2
         + [pltpu.VMEM((span, count), F32)] * 2,
@@ -266,36 +237,32 @@
         transcendentals=pairs,
     )
     fars = [passed_along(fars[k - 1], -k) for k in range(1, WINDOW)]
-    kept, *sends, out_term = call(
-        mix_kernel,
-        [*shared, shape_of((width, span), F32)],
-        [group, attended, out_weight, grads],
-        [held],
+    kv_grad, terms = call(
+        functools.partial(weights_kernel, (outer, inner, tail)),
+        [kv_shape, shape_of((inner, 2 * outer * tail, span), BF16)],
+        [frames, grads, attended, own, *fars],
+        flops=2 * square * width,
+    )
+    terms = lax.all_to_all(terms, "seq", 0, 0, axis_index_groups=near, tiled=True)
+    shared = shape_of((share, width), BF16)
+    sends = call(
+        input_kernel,
+        [shared] * (2 * groups),
+        [group, dq, kv_grad, query_weight, key_weight, value_weight, attended, out_weight],
+        [held, held],
         smem=1,
-        flops=2 * square * width,
-    )
-    kv_grad, terms, mixed = call(
-        functools.partial(weights_kernel, (outer, inner, tail)),
-        [kv_shape, shape_of((inner, 2 * outer * tail, span), BF16), shared[0]],
-        [frames, own, *fars, out_term, kept, *exchanged(sends)],
-        flops=square * width,
-    )
-    terms = lax.all_to_all(terms, "seq", 0, 0, axis_index_groups=near, tiled=True)
-    kept, *sends = call(
-        input_kernel,
-        shared,
-        [group, dq, kv_grad, query_weight, key_weight, value_weight],
-        [held],
-        smem=1,
-        flops=3 * square * width,
-    )
+        flops=4 * square * width,
+    )
+    frames_parts = [sends[0], *exchanged(sends[1:groups])]
+    mixed_parts = [sends[groups], *exchanged(sends[groups + 1 :])]
     terms, frames_grad = call(
         near_kernel,
-        [shape_of((2 * outer * tail, span), BF16), shared[0]],
-        [terms, kept, *exchanged(sends)],
+        [shape_of((2 * outer * tail, span), BF16), shared],
+        [terms, *frames_parts],
     )
     terms = terms.reshape(outer, 2 * tail, span)
     terms = lax.all_to_all(terms, "seq", 0, 0, axis_index_groups=across, tiled=True)
+    [mixed] = call(mixed_kernel, [shared], mixed_parts)
     value_sum, out_sum = call(far_kernel, [shape_of((tail, span), F32)] * 2, [terms])
     return mixed, frames_grad, value_sum, out_sum.T
 

time: 144 us -> 136 us (0.944)
  blocking collectives: 49.9 us -> 24.3 us
  starting transfers between devices: 43 us -> 62.6 us
  waiting for transfers between devices: 35 us -> 28.6 us
  local copies, waits for them, and re-layouts: 2.26 us -> 7.94 us
    all_to_all x1 -> x0, blocking collectives: 25.9 us -> none  [per_device(): lax.all_to_all(terms, 'seq', 0, 0, axis_index_groups=across, tiled=True)]
    all_to_all x0 -> x1, starting transfers between devices: none -> 18.4 us  [per_device(): lax.all_to_all(terms, 'seq', 0, 0, axis_index_groups=across, tiled=True)]
    all_to_all x1, starting transfers between devices: 3.69 us -> 15.2 us  [per_device(): lax.all_to_all(terms, 'seq', 0, 0, axis_index_groups=near, tiled=True)]
    ppermute x6, starting transfers between devices: 18.1 us -> 9.34 us  [passed_along(): lax.ppermute(value, 'seq', [(i, i + steps) for i in range(first, last)])]
    ppermute x6, waiting for transfers between devices: 17.3 us -> 9.68 us  [exchanged(): received[other] = lax.ppermute(sends[other - 1], 'head', pairs)]
    unnamed x17 -> x41, local copies, waits for them, and re-layouts: 2.18 us -> 7.86 us
    ppermute x6, starting transfers between devices: 21.3 us -> 19.7 us  [exchanged(): received[other] = lax.ppermute(sends[other - 1], 'head', pairs)]
    pallas_call x9 -> x8, Pallas kernels: 10.7 us -> 10.6 us  [call(): pl.pallas_call(kernel, out_shape=outs, in_specs=specs, out_specs=[pl.Bloc...]
  transfers between devices with their start and end apart: 13 -> 14, of which waited for: 6 -> 7; matrix products, arithmetic and copies ran while one was open for 0% -> 0% of each run, Pallas kernels for 1% -> 1%
where the time goes in v2:
time: 136 us; the launch traced here: 135 us
  starting transfers between devices  62.6 us (46%)
  waiting for transfers between devices  28.6 us (21%)
  blocking collectives  24.3 us (18%)
  Pallas kernels  10.6 us (8%)
  local copies, waits for them, and re-layouts  7.94 us (6%)
    ppermute x6, starting transfers between devices, exchanged(): received[other] = lax.ppermute(sends[other - 1], 'head', pairs)  19.7 us
    ppermute x6, waiting for transfers between devices, passed_along(): lax.ppermute(value, 'seq', [(i, i + steps) for i in range(first, last)])  19 us
    all_to_all x1, starting transfers between devices, per_device(): lax.all_to_all(terms, 'seq', 0, 0, axis_index_groups=across, tiled=True)  18.4 us
    all_to_all x1, starting transfers between devices, per_device(): lax.all_to_all(terms, 'seq', 0, 0, axis_index_groups=near, tiled=True)  15.2 us
    all_gather x1, blocking collectives, per_device(): frames = lax.all_gather(frames_in, 'head', axis=0, tiled=True)  15.1 us
    pallas_call x8, Pallas kernels, call(): pl.pallas_call(kernel, out_shape=outs, in_specs=specs, out_specs=[pl.Bloc...  10.6 us
    ppermute x6, waiting for transfers between devices, exchanged(): received[other] = lax.ppermute(sends[other - 1], 'head', pairs)  9.68 us
    ppermute x6, starting transfers between devices, passed_along(): lax.ppermute(value, 'seq', [(i, i + steps) for i in range(first, last)])  9.34 us
  transfers between devices with their start and end apart: 14, of which 7 were waited for; matrix products, arithmetic and copies ran while one was open for 0% of the time, Pallas kernels for 1%

profile of v2, /device:TPU:1, one launch (start us, length us, event | category | flops | bytes accessed | tf_op | source)
XLA Modules:
  0.0 135.0 jit_solution(17263738336493517586)
XLA Ops:
  0.7 15.1 %all_gather.6.frames_ref = bf16[256,1024]{1,0:T(8,128)(2,1)S(1)} all-gather(bf16[64,1024]{1,0:T(8,128)(2,1)} %param.7), channel_id=1, replica_groups=mesh['seq'=128,'head'=4] {'head'}, dimensions={0}, use_global_device_ids=true | all-gather | bytes 655360 | tf_op jit(solution)/shard_map/all_gather | solution.py:216
  15.7 1.0 copy-done.2
  17.2 1.4 %collective-permute-start.2 = (bf16[256,512]{1,0:T(8,128)(2,1)S(1)}, bf16[256,512]{1,0:T(8,128)(2,1)S(1)}, u32[]{:S(2)}, u32[]{:S(2)}) collective-permute-start(bf16[256,512]{1,0:T(8,128)(2,1)S(1)} %shard_map.103.kv0), channel_id=1, source_target_pairs={{0,12},{4,16},{8,20},{12,24},{16,28},{20,32},{24,36},{28,40},{32,4... | collective-permute-start | bytes 786440 | tf_op jit(solution)/shard_map/ppermute | solution.py:184
  18.7 1.4 %collective-permute-start.1 = (bf16[256,512]{1,0:T(8,128)(2,1)S(1)}, bf16[256,512]{1,0:T(8,128)(2,1)S(1)}, u32[]{:S(2)}, u32[]{:S(2)}) collective-permute-start(bf16[256,512]{1,0:T(8,128)(2,1)S(1)} %shard_map.103.kv0), channel_id=1, source_target_pairs={{0,8},{4,12},{8,16},{12,20},{16,24},{20,28},{24,32},{28,36},{32,40... | collective-permute-start | bytes 786440 | tf_op jit(solution)/shard_map/ppermute | solution.py:184
  20.1 2.6 %collective-permute-start = (bf16[256,512]{1,0:T(8,128)(2,1)S(1)}, bf16[256,512]{1,0:T(8,128)(2,1)S(1)}, u32[]{:S(2)}, u32[]{:S(2)}) collective-permute-start(bf16[256,512]{1,0:T(8,128)(2,1)S(1)} %shard_map.103.kv0), channel_id=1, source_target_pairs={{0,4},{4,8},{8,12},{12,16},{16,20},{20,24},{24,28},{28,32},{32,36}... | collective-permute-start | bytes 786440 | tf_op jit(solution)/shard_map/ppermute | solution.py:184
  22.9 9.2 %all_gather.7.grads_ref = bf16[256,1024]{1,0:T(8,128)(2,1)S(1)} all-gather(bf16[64,1024]{1,0:T(8,128)(2,1)S(1)} %copy-done.19), channel_id=1, replica_groups=mesh['seq'=128,'head'=4] {'head'}, dimensions={0}, use_global_device_ids=true | all-gather | bytes 655360 | tf_op jit(solution)/shard_map/all_gather | solution.py:219
  32.7 6.1 %shard_map.104 = (bf16[256,256]{1,0:T(8,128)(2,1)S(1)}, bf16[256,256]{1,0:T(8,128)(2,1)S(1)}, f32[256,512]{1,0:T(8,128)S(1)}, bf16[256,512]{1,0:T(8,128)(2,1)S(1...) custom-call(s32[1,3]{1,0:T(1,128)S(1)} %copy.12.mask_ref, bf16[256,256]{1,0:T(8,128)(2,1)S(1)} %get-tuple-element.26.qt_ref, ...), custom_call_target="tpu_custom_call" | custom-call | flops 3221225472 | bytes 2883596 | tf_op jit(solution)/shard_map/pallas_call | solution.py:39
  39.4 1.3 collective-permute-start.3
  40.7 1.3 collective-permute-start.4
  42.0 1.3 collective-permute-start.5
  43.3 6.0 %collective-permute-done.3.far1 = bf16[256,512]{1,0:T(8,128)(2,1)S(1)} collective-permute-done((bf16[256,512]{1,0:T(8,128)(2,1)S(1)}, bf16[256,512]{1,0:T(8,128)(2,1)S(1)}, u32[]{:S(2)}, u32[]{:S(2)}) %collective-permute-start.3) | collective-permute-done | bytes 262176 | tf_op jit(solution)/shard_map/ppermute | solution.py:184
  49.4 5.3 %collective-permute-done.4.far2 = bf16[256,512]{1,0:T(8,128)(2,1)S(1)} collective-permute-done((bf16[256,512]{1,0:T(8,128)(2,1)S(1)}, bf16[256,512]{1,0:T(8,128)(2,1)S(1)}, u32[]{:S(2)}, u32[]{:S(2)}) %collective-permute-start.4) | collective-permute-done | bytes 262176 | tf_op jit(solution)/shard_map/ppermute | solution.py:184
  54.7 7.6 %collective-permute-done.5.far3 = bf16[256,512]{1,0:T(8,128)(2,1)S(1)} collective-permute-done((bf16[256,512]{1,0:T(8,128)(2,1)S(1)}, bf16[256,512]{1,0:T(8,128)(2,1)S(1)}, u32[]{:S(2)}, u32[]{:S(2)}) %collective-permute-start.5) | collective-permute-done | bytes 262176 | tf_op jit(solution)/shard_map/ppermute | solution.py:184
  62.9 1.0 copy-done.6
  63.9 15.2 %all-to-all-start = ((bf16[8,256,256]{2,1,0:T(8,128)(2,1)}), bf16[8,256,256]{2,1,0:T(8,128)(2,1)S(1)}, u32[]{:S(2)}, u32[]{:S(2)}) async-start(bf16[8,256,256]{2,1,0:T(8,128)(2,1)} %copy-done.6), calls=%async_computation | async-start | bytes 2097152 | tf_op jit(solution)/shard_map/all_to_all | solution.py:246
  79.1 0.9 copy-done.10
  80.0 0.8 shard_map.106
  82.1 0.7 copy-done.13
  84.0 3.2 %collective-permute-start.9 = (bf16[64,1024]{1,0:T(8,128)(2,1)S(1)}, bf16[64,1024]{1,0:T(8,128)(2,1)S(1)}, u32[]{:S(2)}, u32[]{:S(2)}) collective-permute-start(bf16[64,1024]{1,0:T(8,128)(2,1)S(1)} %get-tuple-element.41), channel_id=1, source_target_pairs={{0,1},{1,0},{2,3},{3,2},{4,5},{5,4},{6,7},{7,6},{8,9},{9,8},{10,11... | collective-permute-start | bytes 393224 | tf_op jit(solution)/shard_map/ppermute | solution.py:192
  87.3 2.4 %collective-permute-start.10 = (bf16[64,1024]{1,0:T(8,128)(2,1)S(1)}, bf16[64,1024]{1,0:T(8,128)(2,1)S(1)}, u32[]{:S(2)}, u32[]{:S(2)}) collective-permute-start(bf16[64,1024]{1,0:T(8,128)(2,1)S(1)} %get-tuple-element.42), channel_id=1, source_target_pairs={{0,2},{1,3},{2,0},{3,1},{4,6},{5,7},{6,4},{7,5},{8,10},{9,11},{10,... | collective-permute-start | bytes 393224 | tf_op jit(solution)/shard_map/ppermute | solution.py:192
  89.7 4.5 %collective-permute-start.11 = (bf16[64,1024]{1,0:T(8,128)(2,1)S(1)}, bf16[64,1024]{1,0:T(8,128)(2,1)S(1)}, u32[]{:S(2)}, u32[]{:S(2)}) collective-permute-start(bf16[64,1024]{1,0:T(8,128)(2,1)S(1)} %get-tuple-element.43), channel_id=1, source_target_pairs={{0,3},{1,2},{2,1},{3,0},{4,7},{5,6},{6,5},{7,4},{8,11},{9,10},{10,... | collective-permute-start | bytes 393224 | tf_op jit(solution)/shard_map/ppermute | solution.py:192
  94.2 1.5 %collective-permute-done.10.part2 = bf16[64,1024]{1,0:T(8,128)(2,1)S(1)} collective-permute-done((bf16[64,1024]{1,0:T(8,128)(2,1)S(1)}, bf16[64,1024]{1,0:T(8,128)(2,1)S(1)}, u32[]{:S(2)}, u32[]{:S(2)}) %collective-permute-start.10) | collective-permute-done | bytes 131104 | tf_op jit(solution)/shard_map/ppermute | solution.py:192
  95.8 3.0 %collective-permute-done.11.part3 = bf16[64,1024]{1,0:T(8,128)(2,1)S(1)} collective-permute-done((bf16[64,1024]{1,0:T(8,128)(2,1)S(1)}, bf16[64,1024]{1,0:T(8,128)(2,1)S(1)}, u32[]{:S(2)}, u32[]{:S(2)}) %collective-permute-start.11) | collective-permute-done | bytes 131104 | tf_op jit(solution)/shard_map/ppermute | solution.py:192
  98.8 0.9 copy-done.12
  99.7 0.9 shard_map.108
  100.6 18.4 %all-to-all-start.1 = ((bf16[16,16,256]{2,1,0:T(8,128)(2,1)}), bf16[16,16,256]{2,1,0:T(8,128)(2,1)S(1)}, u32[]{:S(2)}, u32[]{:S(2)}) async-start(bf16[16,16,256]{2,1,0:T(8,128)(2,1)} %bitcast.1), calls=%async_computation.1 | async-start | bytes 262144 | tf_op jit(solution)/shard_map/all_to_all | solution.py:264
  118.9 2.6 %collective-permute-start.6 = (bf16[64,1024]{1,0:T(8,128)(2,1)S(1)}, bf16[64,1024]{1,0:T(8,128)(2,1)S(1)}, u32[]{:S(2)}, u32[]{:S(2)}) collective-permute-start(bf16[64,1024]{1,0:T(8,128)(2,1)S(1)} %copy-done.18), channel_id=1, source_target_pairs={{0,1},{1,0},{2,3},{3,2},{4,5},{5,4},{6,7},{7,6},{8,9},{9,8},{10,11... | collective-permute-start | bytes 393224 | tf_op jit(solution)/shard_map/ppermute | solution.py:192
  121.5 3.0 %collective-permute-start.7 = (bf16[64,1024]{1,0:T(8,128)(2,1)S(1)}, bf16[64,1024]{1,0:T(8,128)(2,1)S(1)}, u32[]{:S(2)}, u32[]{:S(2)}) collective-permute-start(bf16[64,1024]{1,0:T(8,128)(2,1)S(1)} %copy-done.16), channel_id=1, source_target_pairs={{0,2},{1,3},{2,0},{3,1},{4,6},{5,7},{6,4},{7,5},{8,10},{9,11},{10,... | collective-permute-start | bytes 393224 | tf_op jit(solution)/shard_map/ppermute | solution.py:192
  124.6 3.9 %collective-permute-start.8 = (bf16[64,1024]{1,0:T(8,128)(2,1)S(1)}, bf16[64,1024]{1,0:T(8,128)(2,1)S(1)}, u32[]{:S(2)}, u32[]{:S(2)}) collective-permute-start(bf16[64,1024]{1,0:T(8,128)(2,1)S(1)} %copy-done.14), channel_id=1, source_target_pairs={{0,3},{1,2},{2,1},{3,0},{4,7},{5,6},{6,5},{7,4},{8,11},{9,10},{10,... | collective-permute-start | bytes 393224 | tf_op jit(solution)/shard_map/ppermute | solution.py:192
  128.5 1.5 %collective-permute-done.7.part2 = bf16[64,1024]{1,0:T(8,128)(2,1)S(1)} collective-permute-done((bf16[64,1024]{1,0:T(8,128)(2,1)S(1)}, bf16[64,1024]{1,0:T(8,128)(2,1)S(1)}, u32[]{:S(2)}, u32[]{:S(2)}) %collective-permute-start.7) | collective-permute-done | bytes 131104 | tf_op jit(solution)/shard_map/ppermute | solution.py:192
  130.0 3.6 %collective-permute-done.8.part3 = bf16[64,1024]{1,0:T(8,128)(2,1)S(1)} collective-permute-done((bf16[64,1024]{1,0:T(8,128)(2,1)S(1)}, bf16[64,1024]{1,0:T(8,128)(2,1)S(1)}, u32[]{:S(2)}, u32[]{:S(2)}) %collective-permute-start.8) | collective-permute-done | bytes 131104 | tf_op jit(solution)/shard_map/ppermute | solution.py:192
  133.7 0.7 shard_map.107
  (48 shorter events, 5.7 us)
Async XLA Ops:
  0.6 22.1 %copy-start = (s32[128,3]{0,1:T(4,128)S(1)}, s32[128,3]{0,1:T(4,128)}, u32[]{:S(2)}) copy-start(s32[128,3]{0,1:T(4,128)} %param.12) | copy-start | bytes 4612
  0.6 15.1 %copy-start.1 = (bf16[1024,256]{1,0:T(8,128)(2,1)S(1)}, bf16[1024,256]{1,0:T(8,128)(2,1)}, u32[]{:S(2)}) copy-start(bf16[1024,256]{1,0:T(8,128)(2,1)} %key_weight_ref.3) | copy-start | bytes 1572868
  15.7 1.0 copy-start.2
  16.8 6.1 %copy-start.19 = (bf16[64,1024]{1,0:T(8,128)(2,1)S(1)}, bf16[64,1024]{1,0:T(8,128)(2,1)}, u32[]{:S(2)}) copy-start(bf16[64,1024]{1,0:T(8,128)(2,1)} %param.13) | copy-start | bytes 393220
  16.8 15.4 %copy-start.5 = (bf16[256,1024]{1,0:T(8,128)(2,1)S(1)}, bf16[256,1024]{1,0:T(8,128)(2,1)}, u32[]{:S(2)}) copy-start(bf16[256,1024]{1,0:T(8,128)(2,1)} %out_weight_ref.3) | copy-start | bytes 1572868
  17.2 14.9 %copy-start.4 = (bf16[1024,256]{1,0:T(8,128)(2,1)S(1)}, bf16[1024,256]{1,0:T(8,128)(2,1)}, u32[]{:S(2)}) copy-start(bf16[1024,256]{1,0:T(8,128)(2,1)} %query_weight_ref.3) | copy-start | bytes 1572868
  17.2 15.4 %collective-permute-start.2 = (bf16[256,512]{1,0:T(8,128)(2,1)S(1)}, bf16[256,512]{1,0:T(8,128)(2,1)S(1)}, u32[]{:S(2)}, u32[]{:S(2)}) collective-permute-start(bf16[256,512]{1,0:T(8,128)(2,1)S(1)} %shard_map.103.kv0), channel_id=1, source_target_pairs={{0,12},{4,16},{8,20},{12,24},{16,28},{20,32},{24,36},{28,40},{32,4... | collective-permute-start | bytes 786440 | tf_op jit(solution)/shard_map/ppermute | solution.py:184
  18.7 14.0 %collective-permute-start.1 = (bf16[256,512]{1,0:T(8,128)(2,1)S(1)}, bf16[256,512]{1,0:T(8,128)(2,1)S(1)}, u32[]{:S(2)}, u32[]{:S(2)}) collective-permute-start(bf16[256,512]{1,0:T(8,128)(2,1)S(1)} %shard_map.103.kv0), channel_id=1, source_target_pairs={{0,8},{4,12},{8,16},{12,20},{16,24},{20,28},{24,32},{28,36},{32,40... | collective-permute-start | bytes 786440 | tf_op jit(solution)/shard_map/ppermute | solution.py:184
  20.1 12.6 %collective-permute-start = (bf16[256,512]{1,0:T(8,128)(2,1)S(1)}, bf16[256,512]{1,0:T(8,128)(2,1)S(1)}, u32[]{:S(2)}, u32[]{:S(2)}) collective-permute-start(bf16[256,512]{1,0:T(8,128)(2,1)S(1)} %shard_map.103.kv0), channel_id=1, source_target_pairs={{0,4},{4,8},{8,12},{12,16},{16,20},{20,24},{24,28},{28,32},{32,36}... | collective-permute-start | bytes 786440 | tf_op jit(solution)/shard_map/ppermute | solution.py:184
  38.8 0.7 copy-start.9
  39.4 9.9 %collective-permute-start.3 = (bf16[256,512]{1,0:T(8,128)(2,1)S(1)}, bf16[256,512]{1,0:T(8,128)(2,1)S(1)}, u32[]{:S(2)}, u32[]{:S(2)}) collective-permute-start(bf16[256,512]{1,0:T(8,128)(2,1)S(1)} %get-tuple-element.31), channel_id=1, source_target_pairs={{4,0},{8,4},{12,8},{16,12},{20,16},{24,20},{28,24},{32,28},{36,32}... | collective-permute-start | bytes 786440 | tf_op jit(solution)/shard_map/ppermute | solution.py:184
  40.7 13.9 %collective-permute-start.4 = (bf16[256,512]{1,0:T(8,128)(2,1)S(1)}, bf16[256,512]{1,0:T(8,128)(2,1)S(1)}, u32[]{:S(2)}, u32[]{:S(2)}) collective-permute-start(bf16[256,512]{1,0:T(8,128)(2,1)S(1)} %get-tuple-element.32), channel_id=1, source_target_pairs={{8,0},{12,4},{16,8},{20,12},{24,16},{28,20},{32,24},{36,28},{40,32... | collective-permute-start | bytes 786440 | tf_op jit(solution)/shard_map/ppermute | solution.py:184
  42.0 20.3 %collective-permute-start.5 = (bf16[256,512]{1,0:T(8,128)(2,1)S(1)}, bf16[256,512]{1,0:T(8,128)(2,1)S(1)}, u32[]{:S(2)}, u32[]{:S(2)}) collective-permute-start(bf16[256,512]{1,0:T(8,128)(2,1)S(1)} %get-tuple-element.33), channel_id=1, source_target_pairs={{12,0},{16,4},{20,8},{24,12},{28,16},{32,20},{36,24},{40,28},{44,3... | collective-permute-start | bytes 786440 | tf_op jit(solution)/shard_map/ppermute | solution.py:184
  62.9 1.0 copy-start.6
  63.9 15.2 %copy-start.3 = (bf16[1024,256]{1,0:T(8,128)(2,1)S(1)}, bf16[1024,256]{1,0:T(8,128)(2,1)}, u32[]{:S(2)}) copy-start(bf16[1024,256]{1,0:T(8,128)(2,1)} %value_weight_ref.3) | copy-start | bytes 1572868
  63.9 34.9 %all-to-all-start = ((bf16[8,256,256]{2,1,0:T(8,128)(2,1)}), bf16[8,256,256]{2,1,0:T(8,128)(2,1)S(1)}, u32[]{:S(2)}, u32[]{:S(2)}) async-start(bf16[8,256,256]{2,1,0:T(8,128)(2,1)} %copy-done.6), calls=%async_computation | async-start | bytes 2097152 | tf_op jit(solution)/shard_map/all_to_all | solution.py:246
  79.1 0.9 copy-start.10
  80.8 0.7 copy-start.7
  81.4 0.7 copy-start.11
  82.1 0.7 copy-start.13
  84.0 10.2 %collective-permute-start.9 = (bf16[64,1024]{1,0:T(8,128)(2,1)S(1)}, bf16[64,1024]{1,0:T(8,128)(2,1)S(1)}, u32[]{:S(2)}, u32[]{:S(2)}) collective-permute-start(bf16[64,1024]{1,0:T(8,128)(2,1)S(1)} %get-tuple-element.41), channel_id=1, source_target_pairs={{0,1},{1,0},{2,3},{3,2},{4,5},{5,4},{6,7},{7,6},{8,9},{9,8},{10,11... | collective-permute-start | bytes 393224 | tf_op jit(solution)/shard_map/ppermute | solution.py:192
  87.3 8.5 %collective-permute-start.10 = (bf16[64,1024]{1,0:T(8,128)(2,1)S(1)}, bf16[64,1024]{1,0:T(8,128)(2,1)S(1)}, u32[]{:S(2)}, u32[]{:S(2)}) collective-permute-start(bf16[64,1024]{1,0:T(8,128)(2,1)S(1)} %get-tuple-element.42), channel_id=1, source_target_pairs={{0,2},{1,3},{2,0},{3,1},{4,6},{5,7},{6,4},{7,5},{8,10},{9,11},{10,... | collective-permute-start | bytes 393224 | tf_op jit(solution)/shard_map/ppermute | solution.py:192
  89.7 9.1 %collective-permute-start.11 = (bf16[64,1024]{1,0:T(8,128)(2,1)S(1)}, bf16[64,1024]{1,0:T(8,128)(2,1)S(1)}, u32[]{:S(2)}, u32[]{:S(2)}) collective-permute-start(bf16[64,1024]{1,0:T(8,128)(2,1)S(1)} %get-tuple-element.43), channel_id=1, source_target_pairs={{0,3},{1,2},{2,1},{3,0},{4,7},{5,6},{6,5},{7,4},{8,11},{9,10},{10,... | collective-permute-start | bytes 393224 | tf_op jit(solution)/shard_map/ppermute | solution.py:192
  98.8 0.9 copy-start.12
  99.7 19.2 %copy-start.18 = (bf16[64,1024]{1,0:T(8,128)(2,1)S(1)}, bf16[64,1024]{1,0:T(8,128)(2,1)}, u32[]{:S(2)}) copy-start(bf16[64,1024]{1,0:T(8,128)(2,1)} %copy-done.17) | copy-start | bytes 393220
  99.7 21.8 %copy-start.16 = (bf16[64,1024]{1,0:T(8,128)(2,1)S(1)}, bf16[64,1024]{1,0:T(8,128)(2,1)}, u32[]{:S(2)}) copy-start(bf16[64,1024]{1,0:T(8,128)(2,1)} %copy-done.15) | copy-start | bytes 393220
  100.5 24.0 %copy-start.14 = (bf16[64,1024]{1,0:T(8,128)(2,1)S(1)}, bf16[64,1024]{1,0:T(8,128)(2,1)}, u32[]{:S(2)}) copy-start(bf16[64,1024]{1,0:T(8,128)(2,1)} %copy-done.13) | copy-start | bytes 393220
  100.5 33.1 %copy-start.8 = (bf16[64,1024]{1,0:T(8,128)(2,1)S(1)}, bf16[64,1024]{1,0:T(8,128)(2,1)}, u32[]{:S(2)}) copy-start(bf16[64,1024]{1,0:T(8,128)(2,1)} %copy-done.7) | copy-start | bytes 393220
  100.6 33.8 %all-to-all-start.1 = ((bf16[16,16,256]{2,1,0:T(8,128)(2,1)}), bf16[16,16,256]{2,1,0:T(8,128)(2,1)S(1)}, u32[]{:S(2)}, u32[]{:S(2)}) async-start(bf16[16,16,256]{2,1,0:T(8,128)(2,1)} %bitcast.1), calls=%async_computation.1 | async-start | bytes 262144 | tf_op jit(solution)/shard_map/all_to_all | solution.py:264
  118.9 9.6 %collective-permute-start.6 = (bf16[64,1024]{1,0:T(8,128)(2,1)S(1)}, bf16[64,1024]{1,0:T(8,128)(2,1)S(1)}, u32[]{:S(2)}, u32[]{:S(2)}) collective-permute-start(bf16[64,1024]{1,0:T(8,128)(2,1)S(1)} %copy-done.18), channel_id=1, source_target_pairs={{0,1},{1,0},{2,3},{3,2},{4,5},{5,4},{6,7},{7,6},{8,9},{9,8},{10,11... | collective-permute-start | bytes 393224 | tf_op jit(solution)/shard_map/ppermute | solution.py:192
  121.5 8.5 %collective-permute-start.7 = (bf16[64,1024]{1,0:T(8,128)(2,1)S(1)}, bf16[64,1024]{1,0:T(8,128)(2,1)S(1)}, u32[]{:S(2)}, u32[]{:S(2)}) collective-permute-start(bf16[64,1024]{1,0:T(8,128)(2,1)S(1)} %copy-done.16), channel_id=1, source_target_pairs={{0,2},{1,3},{2,0},{3,1},{4,6},{5,7},{6,4},{7,5},{8,10},{9,11},{10,... | collective-permute-start | bytes 393224 | tf_op jit(solution)/shard_map/ppermute | solution.py:192
  124.6 9.1 %collective-permute-start.8 = (bf16[64,1024]{1,0:T(8,128)(2,1)S(1)}, bf16[64,1024]{1,0:T(8,128)(2,1)S(1)}, u32[]{:S(2)}, u32[]{:S(2)}) collective-permute-start(bf16[64,1024]{1,0:T(8,128)(2,1)S(1)} %copy-done.14), channel_id=1, source_target_pairs={{0,3},{1,2},{2,1},{3,0},{4,7},{5,6},{6,5},{7,4},{8,11},{9,10},{10,... | collective-permute-start | bytes 393224 | tf_op jit(solution)/shard_map/ppermute | solution.py:192
  (2 other events, 1.3 us)

commit v3 on v2

--- a/solution.py
+++ b/solution.py
@@ -65,7 +65,10 @@
     kv_ref[:, span:] = dot_nn(frames_ref[...], value_weight_ref[...]).astype(BF16)
 
 
-def query_kernel(frames_ref, grads_ref, query_weight_ref, out_weight_ref, qt_ref, back_ref):
+def query_kernel(
+    frames_ref, grads_ref, query_weight_ref, out_weight_ref, kv_ref, qt_ref, back_ref, again_ref
+):
+    again_ref[...] = kv_ref[...]
     queries = dot_nn(frames_ref[...], query_weight_ref[...]).astype(BF16).astype(F32)
     qt_ref[...] = (jnp.transpose(queries) * (HEAD_DIM**-0.5)).astype(BF16)
     back_ref[...] = dot_nt(out_weight_ref[...], grads_ref[...]).astype(BF16)
@@ -150,16 +153,19 @@
 
 
 def input_kernel(
-    head_ref, dq_ref, kv_grad_ref, query_weight_ref, key_weight_ref, value_weight_ref, att_ref, out_weight_ref,
-    own_ref, send1, send2, send3, mixed_own_ref, mixed_send1, mixed_send2, mixed_send3, held_mixed, held,
+    head_ref, dq_ref, kv_grad_ref, query_weight_ref, key_weight_ref, value_weight_ref,
+    own_ref, send1, send2, send3, held,
 ):
     span = dq_ref.shape[1]
-    held_mixed[...] = dot_nn(att_ref[...], out_weight_ref[...])
     term = dot_nt(dq_ref[...], query_weight_ref[...])
     term = term + dot_nt(kv_grad_ref[:, :span], key_weight_ref[...])
     held[...] = term + dot_nt(kv_grad_ref[:, span:], value_weight_ref[...])
     shares(head_ref, held, (own_ref, send1, send2, send3))
-    shares(head_ref, held_mixed, (mixed_own_ref, mixed_send1, mixed_send2, mixed_send3))
+
+
+def mix_kernel(head_ref, att_ref, out_weight_ref, after_ref, own_ref, send1, send2, send3, held):
+    held[...] = dot_nn(att_ref[...], out_weight_ref[...])
+    shares(head_ref, held, (own_ref, send1, send2, send3))
 
 
 def near_kernel(pieces_ref, part0, part1, part2, part3, terms_ref, frames_grad_ref):
@@ -215,14 +221,15 @@
 
     frames = lax.all_gather(frames_in, "head", axis=0, tiled=True)
     [kv] = call(kv_kernel, [kv_shape], [frames, key_weight, value_weight], flops=2 * square * width)
-    kvs = [kv] + [passed_along(kv, steps) for steps in range(1, WINDOW)]
+    kv2 = passed_along(kv, 2)
     grads = lax.all_gather(out_grad, "head", axis=0, tiled=True)
-    qt, bt = call(
+    qt, bt, again = call(
         query_kernel,
-        [side, side],
-        [frames, grads, query_weight, out_weight],
+        [side, side, kv_shape],
+        [frames, grads, query_weight, out_weight, kv],
         flops=2 * square * width,
     )
+    kvs = [again, passed_along(again, 1), kv2, passed_along(again, 3)]
     attended, dq, own, *fars = call(
         attention_kernel,
         [shape_of((count, span), BF16)] * 2
@@ -245,24 +252,30 @@
     )
     terms = lax.all_to_all(terms, "seq", 0, 0, axis_index_groups=near, tiled=True)
     shared = shape_of((share, width), BF16)
-    sends = call(
+    kept, *sends = call(
         input_kernel,
-        [shared] * (2 * groups),
-        [group, dq, kv_grad, query_weight, key_weight, value_weight, attended, out_weight],
-        [held, held],
+        [shared] * groups,
+        [group, dq, kv_grad, query_weight, key_weight, value_weight],
+        [held],
         smem=1,
-        flops=4 * square * width,
-    )
-    frames_parts = [sends[0], *exchanged(sends[1:groups])]
-    mixed_parts = [sends[groups], *exchanged(sends[groups + 1 :])]
+        flops=3 * square * width,
+    )
     terms, frames_grad = call(
         near_kernel,
         [shape_of((2 * outer * tail, span), BF16), shared],
-        [terms, *frames_parts],
+        [terms, kept, *exchanged(sends)],
+    )
+    mixed_kept, *mixed_sends = call(
+        mix_kernel,
+        [shared] * groups,
+        [group, attended, out_weight, terms],
+        [held],
+        smem=1,
+        flops=square * width,
     )
     terms = terms.reshape(outer, 2 * tail, span)
     terms = lax.all_to_all(terms, "seq", 0, 0, axis_index_groups=across, tiled=True)
-    [mixed] = call(mixed_kernel, [shared], mixed_parts)
+    [mixed] = call(mixed_kernel, [shared], [mixed_kept, *exchanged(mixed_sends)])
     value_sum, out_sum = call(far_kernel, [shape_of((tail, span), F32)] * 2, [terms])
     return mixed, frames_grad, value_sum, out_sum.T
 

time: 136 us -> 141 us (1.037)
  local copies, waits for them, and re-layouts: 7.94 us -> 10.1 us
  Pallas kernels: 10.6 us -> 12.3 us
    ppermute x6, starting transfers between devices: 9.34 us -> 14.4 us  [passed_along(): lax.ppermute(value, 'seq', [(i, i + steps) for i in range(first, last)])]
    all_to_all x1, starting transfers between devices: 15.2 us -> 10.8 us  [per_device(): lax.all_to_all(terms, 'seq', 0, 0, axis_index_groups=near, tiled=True)]
    unnamed x41 -> x37, local copies, waits for them, and re-layouts: 7.86 us -> 10 us
    pallas_call x8 -> x9, Pallas kernels: 10.6 us -> 12.3 us  [call(): pl.pallas_call(kernel, out_shape=outs, in_specs=specs, out_specs=[pl.Bloc...]
  transfers between devices with their start and end apart: 14 -> 14, of which waited for: 7 -> 9; matrix products, arithmetic and copies ran while one was open for 0% -> 0% of each run, Pallas kernels for 1% -> 2%
where the time goes in v3:
time: 141 us; the launch traced here: 140 us
  starting transfers between devices  63.1 us (45%)
  waiting for transfers between devices  29.9 us (21%)
  blocking collectives  23.9 us (17%)
  Pallas kernels  12.3 us (9%)
  local copies, waits for them, and re-layouts  10.1 us (7%)
    ppermute x6, starting transfers between devices, exchanged(): received[other] = lax.ppermute(sends[other - 1], 'head', pairs)  20.7 us
    ppermute x6, waiting for transfers between devices, passed_along(): lax.ppermute(value, 'seq', [(i, i + steps) for i in range(first, last)])  20.3 us
    all_to_all x1, starting transfers between devices, per_device(): lax.all_to_all(terms, 'seq', 0, 0, axis_index_groups=across, tiled=True)  17.3 us
    all_gather x1, blocking collectives, per_device(): frames = lax.all_gather(frames_in, 'head', axis=0, tiled=True)  15.1 us
    ppermute x6, starting transfers between devices, passed_along(): lax.ppermute(value, 'seq', [(i, i + steps) for i in range(first, last)])  14.4 us
    pallas_call x9, Pallas kernels, call(): pl.pallas_call(kernel, out_shape=outs, in_specs=specs, out_specs=[pl.Bloc...  12.3 us
    all_to_all x1, starting transfers between devices, per_device(): lax.all_to_all(terms, 'seq', 0, 0, axis_index_groups=near, tiled=True)  10.8 us
    unnamed x37, local copies, waits for them, and re-layouts  10 us
  transfers between devices with their start and end apart: 14, of which 9 were waited for; matrix products, arithmetic and copies ran while one was open for 0% of the time, Pallas kernels for 2%

profile of v3, /device:TPU:1, one launch (start us, length us, event | category | flops | bytes accessed | tf_op | source)
XLA Modules:
  0.0 140.1 jit_solution(14682537691979244909)
XLA Ops:
  0.7 15.1 %all_gather.6.frames_ref = bf16[256,1024]{1,0:T(8,128)(2,1)S(1)} all-gather(bf16[64,1024]{1,0:T(8,128)(2,1)} %param.7), channel_id=1, replica_groups=mesh['seq'=128,'head'=4] {'head'}, dimensions={0}, use_global_device_ids=true | all-gather | bytes 655360 | tf_op jit(solution)/shard_map/all_gather | solution.py:222
  15.7 1.0 copy-done.2
  17.2 1.4 %collective-permute-start.1 = (bf16[256,512]{1,0:T(8,128)(2,1)S(1)}, bf16[256,512]{1,0:T(8,128)(2,1)S(1)}, u32[]{:S(2)}, u32[]{:S(2)}) collective-permute-start(bf16[256,512]{1,0:T(8,128)(2,1)S(1)} %shard_map.102.kv_ref), channel_id=1, source_target_pairs={{0,8},{4,12},{8,16},{12,20},{16,24},{20,28},{24,32},{28,36},{32,40... | collective-permute-start | bytes 786440 | tf_op jit(solution)/shard_map/ppermute | solution.py:190
  18.7 8.8 %all_gather.7.grads_ref = bf16[256,1024]{1,0:T(8,128)(2,1)S(1)} all-gather(bf16[64,1024]{1,0:T(8,128)(2,1)S(1)} %copy-done.17), channel_id=1, replica_groups=mesh['seq'=128,'head'=4] {'head'}, dimensions={0}, use_global_device_ids=true | all-gather | bytes 655360 | tf_op jit(solution)/shard_map/all_gather | solution.py:225
  29.3 7.1 %collective-permute-start.2 = (bf16[256,512]{1,0:T(8,128)(2,1)S(1)}, bf16[256,512]{1,0:T(8,128)(2,1)}, u32[]{:S(2)}, u32[]{:S(2)}) collective-permute-start(bf16[256,512]{1,0:T(8,128)(2,1)S(1)} %get-tuple-element.29.kv0), channel_id=1, source_target_pairs={{0,12},{4,16},{8,20},{12,24},{16,28},{20,32},{24,36},{28,40},{32,4... | collective-permute-start | bytes 786440 | tf_op jit(solution)/shard_map/ppermute | solution.py:190
  36.4 2.0 %collective-permute-start = (bf16[256,512]{1,0:T(8,128)(2,1)S(1)}, bf16[256,512]{1,0:T(8,128)(2,1)}, u32[]{:S(2)}, u32[]{:S(2)}) collective-permute-start(bf16[256,512]{1,0:T(8,128)(2,1)S(1)} %get-tuple-element.29.kv0), channel_id=1, source_target_pairs={{0,4},{4,8},{8,12},{12,16},{16,20},{20,24},{24,28},{28,32},{32,36}... | collective-permute-start | bytes 786440 | tf_op jit(solution)/shard_map/ppermute | solution.py:190
  39.3 2.0 %collective-permute-done.2.kv3 = bf16[256,512]{1,0:T(8,128)(2,1)} collective-permute-done((bf16[256,512]{1,0:T(8,128)(2,1)S(1)}, bf16[256,512]{1,0:T(8,128)(2,1)}, u32[]{:S(2)}, u32[]{:S(2)}) %collective-permute-start.2) | collective-permute-done | bytes 262176 | tf_op jit(solution)/shard_map/ppermute | solution.py:190
  41.3 2.0 %collective-permute-done.kv1 = bf16[256,512]{1,0:T(8,128)(2,1)} collective-permute-done((bf16[256,512]{1,0:T(8,128)(2,1)S(1)}, bf16[256,512]{1,0:T(8,128)(2,1)}, u32[]{:S(2)}, u32[]{:S(2)}) %collective-permute-start) | collective-permute-done | bytes 262176 | tf_op jit(solution)/shard_map/ppermute | solution.py:190
  43.3 0.9 copy-done.12
  44.2 0.9 copy-done.14
  45.1 0.9 copy-done.16
  46.0 6.6 %shard_map.104 = (bf16[256,256]{1,0:T(8,128)(2,1)S(1)}, bf16[256,256]{1,0:T(8,128)(2,1)S(1)}, f32[256,512]{1,0:T(8,128)S(1)}, bf16[256,512]{1,0:T(8,128)(2,1)S(1...) custom-call(s32[1,3]{1,0:T(1,128)S(1)} %copy.12.mask_ref, bf16[256,256]{1,0:T(8,128)(2,1)S(1)} %copy-done.14, ...), custom_call_target="tpu_custom_call" | custom-call | flops 3221225472 | bytes 2883596 | tf_op jit(solution)/shard_map/pallas_call | solution.py:39
  53.2 1.3 collective-permute-start.3
  54.5 1.3 collective-permute-start.4
  55.8 1.3 collective-permute-start.5
  57.1 6.0 %collective-permute-done.3.far1 = bf16[256,512]{1,0:T(8,128)(2,1)S(1)} collective-permute-done((bf16[256,512]{1,0:T(8,128)(2,1)S(1)}, bf16[256,512]{1,0:T(8,128)(2,1)S(1)}, u32[]{:S(2)}, u32[]{:S(2)}) %collective-permute-start.3) | collective-permute-done | bytes 262176 | tf_op jit(solution)/shard_map/ppermute | solution.py:190
  63.1 3.4 %collective-permute-done.4.far2 = bf16[256,512]{1,0:T(8,128)(2,1)S(1)} collective-permute-done((bf16[256,512]{1,0:T(8,128)(2,1)S(1)}, bf16[256,512]{1,0:T(8,128)(2,1)S(1)}, u32[]{:S(2)}, u32[]{:S(2)}) %collective-permute-start.4) | collective-permute-done | bytes 262176 | tf_op jit(solution)/shard_map/ppermute | solution.py:190
  66.5 7.0 %collective-permute-done.5.far3 = bf16[256,512]{1,0:T(8,128)(2,1)S(1)} collective-permute-done((bf16[256,512]{1,0:T(8,128)(2,1)S(1)}, bf16[256,512]{1,0:T(8,128)(2,1)S(1)}, u32[]{:S(2)}, u32[]{:S(2)}) %collective-permute-start.5) | collective-permute-done | bytes 262176 | tf_op jit(solution)/shard_map/ppermute | solution.py:190
  74.1 1.0 copy-done.6
  75.1 10.8 %all-to-all-start = ((bf16[8,256,256]{2,1,0:T(8,128)(2,1)}), bf16[8,256,256]{2,1,0:T(8,128)(2,1)S(1)}, u32[]{:S(2)}, u32[]{:S(2)}) async-start(bf16[8,256,256]{2,1,0:T(8,128)(2,1)} %copy-done.6), calls=%async_computation | async-start | bytes 2097152 | tf_op jit(solution)/shard_map/all_to_all | solution.py:253
  88.1 4.3 %collective-permute-start.6 = (bf16[64,1024]{1,0:T(8,128)(2,1)S(1)}, bf16[64,1024]{1,0:T(8,128)(2,1)S(1)}, u32[]{:S(2)}, u32[]{:S(2)}) collective-permute-start(bf16[64,1024]{1,0:T(8,128)(2,1)S(1)} %get-tuple-element.39), channel_id=1, source_target_pairs={{0,1},{1,0},{2,3},{3,2},{4,5},{5,4},{6,7},{7,6},{8,9},{9,8},{10,11... | collective-permute-start | bytes 393224 | tf_op jit(solution)/shard_map/ppermute | solution.py:198
  92.5 2.4 %collective-permute-start.7 = (bf16[64,1024]{1,0:T(8,128)(2,1)S(1)}, bf16[64,1024]{1,0:T(8,128)(2,1)S(1)}, u32[]{:S(2)}, u32[]{:S(2)}) collective-permute-start(bf16[64,1024]{1,0:T(8,128)(2,1)S(1)} %get-tuple-element.40), channel_id=1, source_target_pairs={{0,2},{1,3},{2,0},{3,1},{4,6},{5,7},{6,4},{7,5},{8,10},{9,11},{10,... | collective-permute-start | bytes 393224 | tf_op jit(solution)/shard_map/ppermute | solution.py:198
  94.9 4.5 %collective-permute-start.8 = (bf16[64,1024]{1,0:T(8,128)(2,1)S(1)}, bf16[64,1024]{1,0:T(8,128)(2,1)S(1)}, u32[]{:S(2)}, u32[]{:S(2)}) collective-permute-start(bf16[64,1024]{1,0:T(8,128)(2,1)S(1)} %get-tuple-element.41), channel_id=1, source_target_pairs={{0,3},{1,2},{2,1},{3,0},{4,7},{5,6},{6,5},{7,4},{8,11},{9,10},{10,... | collective-permute-start | bytes 393224 | tf_op jit(solution)/shard_map/ppermute | solution.py:198
  99.5 2.0 %collective-permute-done.7.part2 = bf16[64,1024]{1,0:T(8,128)(2,1)S(1)} collective-permute-done((bf16[64,1024]{1,0:T(8,128)(2,1)S(1)}, bf16[64,1024]{1,0:T(8,128)(2,1)S(1)}, u32[]{:S(2)}, u32[]{:S(2)}) %collective-permute-start.7) | collective-permute-done | bytes 131104 | tf_op jit(solution)/shard_map/ppermute | solution.py:198
  101.5 3.0 %collective-permute-done.8.part3 = bf16[64,1024]{1,0:T(8,128)(2,1)S(1)} collective-permute-done((bf16[64,1024]{1,0:T(8,128)(2,1)S(1)}, bf16[64,1024]{1,0:T(8,128)(2,1)S(1)}, u32[]{:S(2)}, u32[]{:S(2)}) %collective-permute-start.8) | collective-permute-done | bytes 131104 | tf_op jit(solution)/shard_map/ppermute | solution.py:198
  104.5 0.9 copy-done.10
  106.2 17.3 %all-to-all-start.1 = ((bf16[16,16,256]{2,1,0:T(8,128)(2,1)}), bf16[16,16,256]{2,1,0:T(8,128)(2,1)S(1)}, u32[]{:S(2)}, u32[]{:S(2)}) async-start(bf16[16,16,256]{2,1,0:T(8,128)(2,1)} %bitcast.1), calls=%async_computation.1 | async-start | bytes 262144 | tf_op jit(solution)/shard_map/all_to_all | solution.py:277
  123.5 1.3 shard_map.108
  124.8 1.9 %collective-permute-start.9 = (bf16[64,1024]{1,0:T(8,128)(2,1)S(1)}, bf16[64,1024]{1,0:T(8,128)(2,1)S(1)}, u32[]{:S(2)}, u32[]{:S(2)}) collective-permute-start(bf16[64,1024]{1,0:T(8,128)(2,1)S(1)} %get-tuple-element.44), channel_id=1, source_target_pairs={{0,1},{1,0},{2,3},{3,2},{4,5},{5,4},{6,7},{7,6},{8,9},{9,8},{10,11... | collective-permute-start | bytes 393224 | tf_op jit(solution)/shard_map/ppermute | solution.py:198
  126.8 2.6 %collective-permute-start.10 = (bf16[64,1024]{1,0:T(8,128)(2,1)S(1)}, bf16[64,1024]{1,0:T(8,128)(2,1)S(1)}, u32[]{:S(2)}, u32[]{:S(2)}) collective-permute-start(bf16[64,1024]{1,0:T(8,128)(2,1)S(1)} %get-tuple-element.45), channel_id=1, source_target_pairs={{0,2},{1,3},{2,0},{3,1},{4,6},{5,7},{6,4},{7,5},{8,10},{9,11},{10,... | collective-permute-start | bytes 393224 | tf_op jit(solution)/shard_map/ppermute | solution.py:198
  129.4 4.8 %collective-permute-start.11 = (bf16[64,1024]{1,0:T(8,128)(2,1)S(1)}, bf16[64,1024]{1,0:T(8,128)(2,1)S(1)}, u32[]{:S(2)}, u32[]{:S(2)}) collective-permute-start(bf16[64,1024]{1,0:T(8,128)(2,1)S(1)} %get-tuple-element.46), channel_id=1, source_target_pairs={{0,3},{1,2},{2,1},{3,0},{4,7},{5,6},{6,5},{7,4},{8,11},{9,10},{10,... | collective-permute-start | bytes 393224 | tf_op jit(solution)/shard_map/ppermute | solution.py:198
  134.7 4.1 %collective-permute-done.11.part3 = bf16[64,1024]{1,0:T(8,128)(2,1)S(1)} collective-permute-done((bf16[64,1024]{1,0:T(8,128)(2,1)S(1)}, bf16[64,1024]{1,0:T(8,128)(2,1)S(1)}, u32[]{:S(2)}, u32[]{:S(2)}) %collective-permute-start.11) | collective-permute-done | bytes 131104 | tf_op jit(solution)/shard_map/ppermute | solution.py:198
  (45 shorter events, 9.3 us)
Async XLA Ops:
  0.6 38.5 %copy-start = (s32[128,3]{0,1:T(4,128)S(1)}, s32[128,3]{0,1:T(4,128)}, u32[]{:S(2)}) copy-start(s32[128,3]{0,1:T(4,128)} %param.12) | copy-start | bytes 4612
  0.6 15.1 %copy-start.1 = (bf16[1024,256]{1,0:T(8,128)(2,1)S(1)}, bf16[1024,256]{1,0:T(8,128)(2,1)}, u32[]{:S(2)}) copy-start(bf16[1024,256]{1,0:T(8,128)(2,1)} %key_weight_ref.3) | copy-start | bytes 1572868
  15.7 1.0 copy-start.2
  16.8 1.9 %copy-start.17 = (bf16[64,1024]{1,0:T(8,128)(2,1)S(1)}, bf16[64,1024]{1,0:T(8,128)(2,1)}, u32[]{:S(2)}) copy-start(bf16[64,1024]{1,0:T(8,128)(2,1)} %param.13) | copy-start | bytes 393220
  16.8 10.7 %copy-start.5 = (bf16[256,1024]{1,0:T(8,128)(2,1)S(1)}, bf16[256,1024]{1,0:T(8,128)(2,1)}, u32[]{:S(2)}) copy-start(bf16[256,1024]{1,0:T(8,128)(2,1)} %out_weight_ref.3) | copy-start | bytes 1572868
  17.2 10.3 %copy-start.4 = (bf16[1024,256]{1,0:T(8,128)(2,1)S(1)}, bf16[1024,256]{1,0:T(8,128)(2,1)}, u32[]{:S(2)}) copy-start(bf16[1024,256]{1,0:T(8,128)(2,1)} %query_weight_ref.3) | copy-start | bytes 1572868
  17.2 22.1 %collective-permute-start.1 = (bf16[256,512]{1,0:T(8,128)(2,1)S(1)}, bf16[256,512]{1,0:T(8,128)(2,1)S(1)}, u32[]{:S(2)}, u32[]{:S(2)}) collective-permute-start(bf16[256,512]{1,0:T(8,128)(2,1)S(1)} %shard_map.102.kv_ref), channel_id=1, source_target_pairs={{0,8},{4,12},{8,16},{12,20},{16,24},{20,28},{24,32},{28,36},{32,40... | collective-permute-start | bytes 786440 | tf_op jit(solution)/shard_map/ppermute | solution.py:190
  28.0 0.7 copy-start.13
  28.7 0.7 copy-start.15
  29.3 11.9 %collective-permute-start.2 = (bf16[256,512]{1,0:T(8,128)(2,1)S(1)}, bf16[256,512]{1,0:T(8,128)(2,1)}, u32[]{:S(2)}, u32[]{:S(2)}) collective-permute-start(bf16[256,512]{1,0:T(8,128)(2,1)S(1)} %get-tuple-element.29.kv0), channel_id=1, source_target_pairs={{0,12},{4,16},{8,20},{12,24},{16,28},{20,32},{24,36},{28,40},{32,4... | collective-permute-start | bytes 786440 | tf_op jit(solution)/shard_map/ppermute | solution.py:190
  36.4 6.8 %collective-permute-start = (bf16[256,512]{1,0:T(8,128)(2,1)S(1)}, bf16[256,512]{1,0:T(8,128)(2,1)}, u32[]{:S(2)}, u32[]{:S(2)}) collective-permute-start(bf16[256,512]{1,0:T(8,128)(2,1)S(1)} %get-tuple-element.29.kv0), channel_id=1, source_target_pairs={{0,4},{4,8},{8,12},{12,16},{16,20},{20,24},{24,28},{28,32},{32,36}... | collective-permute-start | bytes 786440 | tf_op jit(solution)/shard_map/ppermute | solution.py:190
  38.4 0.7 copy-start.11
  43.3 0.9 copy-start.12
  44.2 0.9 copy-start.14
  45.1 0.9 copy-start.16
  52.6 0.7 copy-start.7
  53.2 9.9 %collective-permute-start.3 = (bf16[256,512]{1,0:T(8,128)(2,1)S(1)}, bf16[256,512]{1,0:T(8,128)(2,1)S(1)}, u32[]{:S(2)}, u32[]{:S(2)}) collective-permute-start(bf16[256,512]{1,0:T(8,128)(2,1)S(1)} %get-tuple-element.32), channel_id=1, source_target_pairs={{4,0},{8,4},{12,8},{16,12},{20,16},{24,20},{28,24},{32,28},{36,32}... | collective-permute-start | bytes 786440 | tf_op jit(solution)/shard_map/ppermute | solution.py:190
  54.5 12.0 %collective-permute-start.4 = (bf16[256,512]{1,0:T(8,128)(2,1)S(1)}, bf16[256,512]{1,0:T(8,128)(2,1)S(1)}, u32[]{:S(2)}, u32[]{:S(2)}) collective-permute-start(bf16[256,512]{1,0:T(8,128)(2,1)S(1)} %get-tuple-element.33), channel_id=1, source_target_pairs={{8,0},{12,4},{16,8},{20,12},{24,16},{28,20},{32,24},{36,28},{40,32... | collective-permute-start | bytes 786440 | tf_op jit(solution)/shard_map/ppermute | solution.py:190
  55.8 17.7 %collective-permute-start.5 = (bf16[256,512]{1,0:T(8,128)(2,1)S(1)}, bf16[256,512]{1,0:T(8,128)(2,1)S(1)}, u32[]{:S(2)}, u32[]{:S(2)}) collective-permute-start(bf16[256,512]{1,0:T(8,128)(2,1)S(1)} %get-tuple-element.34), channel_id=1, source_target_pairs={{12,0},{16,4},{20,8},{24,12},{28,16},{32,20},{36,24},{40,28},{44,3... | collective-permute-start | bytes 786440 | tf_op jit(solution)/shard_map/ppermute | solution.py:190
  74.1 1.0 copy-start.6
  75.1 10.8 %copy-start.3 = (bf16[1024,256]{1,0:T(8,128)(2,1)S(1)}, bf16[1024,256]{1,0:T(8,128)(2,1)}, u32[]{:S(2)}) copy-start(bf16[1024,256]{1,0:T(8,128)(2,1)} %value_weight_ref.3) | copy-start | bytes 1572868
  75.1 29.4 %all-to-all-start = ((bf16[8,256,256]{2,1,0:T(8,128)(2,1)}), bf16[8,256,256]{2,1,0:T(8,128)(2,1)S(1)}, u32[]{:S(2)}, u32[]{:S(2)}) async-start(bf16[8,256,256]{2,1,0:T(8,128)(2,1)} %copy-done.6), calls=%async_computation | async-start | bytes 2097152 | tf_op jit(solution)/shard_map/all_to_all | solution.py:253
  85.9 0.9 copy-start.8
  87.5 0.7 copy-start.9
  88.1 11.3 %collective-permute-start.6 = (bf16[64,1024]{1,0:T(8,128)(2,1)S(1)}, bf16[64,1024]{1,0:T(8,128)(2,1)S(1)}, u32[]{:S(2)}, u32[]{:S(2)}) collective-permute-start(bf16[64,1024]{1,0:T(8,128)(2,1)S(1)} %get-tuple-element.39), channel_id=1, source_target_pairs={{0,1},{1,0},{2,3},{3,2},{4,5},{5,4},{6,7},{7,6},{8,9},{9,8},{10,11... | collective-permute-start | bytes 393224 | tf_op jit(solution)/shard_map/ppermute | solution.py:198
  92.5 9.0 %collective-permute-start.7 = (bf16[64,1024]{1,0:T(8,128)(2,1)S(1)}, bf16[64,1024]{1,0:T(8,128)(2,1)S(1)}, u32[]{:S(2)}, u32[]{:S(2)}) collective-permute-start(bf16[64,1024]{1,0:T(8,128)(2,1)S(1)} %get-tuple-element.40), channel_id=1, source_target_pairs={{0,2},{1,3},{2,0},{3,1},{4,6},{5,7},{6,4},{7,5},{8,10},{9,11},{10,... | collective-permute-start | bytes 393224 | tf_op jit(solution)/shard_map/ppermute | solution.py:198
  94.9 9.6 %collective-permute-start.8 = (bf16[64,1024]{1,0:T(8,128)(2,1)S(1)}, bf16[64,1024]{1,0:T(8,128)(2,1)S(1)}, u32[]{:S(2)}, u32[]{:S(2)}) collective-permute-start(bf16[64,1024]{1,0:T(8,128)(2,1)S(1)} %get-tuple-element.41), channel_id=1, source_target_pairs={{0,3},{1,2},{2,1},{3,0},{4,7},{5,6},{6,5},{7,4},{8,11},{9,10},{10,... | collective-permute-start | bytes 393224 | tf_op jit(solution)/shard_map/ppermute | solution.py:198
  104.5 0.9 copy-start.10
  106.2 33.3 %all-to-all-start.1 = ((bf16[16,16,256]{2,1,0:T(8,128)(2,1)}), bf16[16,16,256]{2,1,0:T(8,128)(2,1)S(1)}, u32[]{:S(2)}, u32[]{:S(2)}) async-start(bf16[16,16,256]{2,1,0:T(8,128)(2,1)} %bitcast.1), calls=%async_computation.1 | async-start | bytes 262144 | tf_op jit(solution)/shard_map/all_to_all | solution.py:277
  124.8 9.4 %collective-permute-start.9 = (bf16[64,1024]{1,0:T(8,128)(2,1)S(1)}, bf16[64,1024]{1,0:T(8,128)(2,1)S(1)}, u32[]{:S(2)}, u32[]{:S(2)}) collective-permute-start(bf16[64,1024]{1,0:T(8,128)(2,1)S(1)} %get-tuple-element.44), channel_id=1, source_target_pairs={{0,1},{1,0},{2,3},{3,2},{4,5},{5,4},{6,7},{7,6},{8,9},{9,8},{10,11... | collective-permute-start | bytes 393224 | tf_op jit(solution)/shard_map/ppermute | solution.py:198
  126.8 8.0 %collective-permute-start.10 = (bf16[64,1024]{1,0:T(8,128)(2,1)S(1)}, bf16[64,1024]{1,0:T(8,128)(2,1)S(1)}, u32[]{:S(2)}, u32[]{:S(2)}) collective-permute-start(bf16[64,1024]{1,0:T(8,128)(2,1)S(1)} %get-tuple-element.45), channel_id=1, source_target_pairs={{0,2},{1,3},{2,0},{3,1},{4,6},{5,7},{6,4},{7,5},{8,10},{9,11},{10,... | collective-permute-start | bytes 393224 | tf_op jit(solution)/shard_map/ppermute | solution.py:198
  129.4 9.4 %collective-permute-start.11 = (bf16[64,1024]{1,0:T(8,128)(2,1)S(1)}, bf16[64,1024]{1,0:T(8,128)(2,1)S(1)}, u32[]{:S(2)}, u32[]{:S(2)}) collective-permute-start(bf16[64,1024]{1,0:T(8,128)(2,1)S(1)} %get-tuple-element.46), channel_id=1, source_target_pairs={{0,3},{1,2},{2,1},{3,0},{4,7},{5,6},{6,5},{7,4},{8,11},{9,10},{10,... | collective-permute-start | bytes 393224 | tf_op jit(solution)/shard_map/ppermute | solution.py:198

commit v4 on v2

--- a/solution.py
+++ b/solution.py
@@ -130,7 +130,10 @@
     return total
 
 
-def weights_kernel(cuts, frames_ref, grads_ref, att_ref, own_ref, far1, far2, far3, kv_grad_ref, terms_ref):
+def weights_kernel(
+    cuts, head_ref, frames_ref, grads_ref, att_ref, own_ref, far1, far2, far3, pair_ref, other_pair_ref,
+    kv_grad_ref, terms_ref, keep_ref, send_ref, held,
+):
     outer, inner, tail = cuts
     rounded = added((own_ref, far1, far2, far3)).astype(BF16)
     kv_grad_ref[...] = rounded
@@ -140,6 +143,11 @@
     for i in range(inner):
         piece = jnp.stack([value_term[:, i], out_term[:, i]], axis=1)
         terms_ref[i] = piece.reshape(2 * outer * tail, span).astype(BF16)
+    held[...] = added((pair_ref, other_pair_ref))
+    chip = lax.shift_right_logical(head_ref[0], 1)
+    half = keep_ref.shape[0]
+    keep_ref[...] = held[pl.ds(pl.multiple_of(chip * half, half), half), :]
+    send_ref[...] = held[pl.ds(pl.multiple_of((1 - chip) * half, half), half), :].astype(BF16)
 
 
 def shares(head_ref, term, outs):
@@ -149,22 +157,32 @@
         out[...] = term[pl.ds(start, half), :].astype(BF16)
 
 
+def mix_kernel(head_ref, att_ref, out_weight_ref, after_ref, keep_ref, send_ref, held):
+    held[...] = dot_nn(att_ref[...], out_weight_ref[...])
+    half = keep_ref.shape[0] // 2
+    core = jnp.bitwise_and(head_ref[0], 1)
+    for chip in range(2):
+        rows = pl.ds(chip * half, half)
+        start = pl.multiple_of((2 * chip + core) * half, half)
+        keep_ref[rows, :] = held[pl.ds(start, half), :].astype(BF16)
+        start = pl.multiple_of((2 * chip + 1 - core) * half, half)
+        send_ref[rows, :] = held[pl.ds(start, half), :].astype(BF16)
+
+
 def input_kernel(
-    head_ref, dq_ref, kv_grad_ref, query_weight_ref, key_weight_ref, value_weight_ref, att_ref, out_weight_ref,
-    own_ref, send1, send2, send3, mixed_own_ref, mixed_send1, mixed_send2, mixed_send3, held_mixed, held,
+    head_ref, dq_ref, kv_grad_ref, query_weight_ref, key_weight_ref, value_weight_ref,
+    own_ref, send1, send2, send3, held,
 ):
     span = dq_ref.shape[1]
-    held_mixed[...] = dot_nn(att_ref[...], out_weight_ref[...])
     term = dot_nt(dq_ref[...], query_weight_ref[...])
     term = term + dot_nt(kv_grad_ref[:, :span], key_weight_ref[...])
     held[...] = term + dot_nt(kv_grad_ref[:, span:], value_weight_ref[...])
     shares(head_ref, held, (own_ref, send1, send2, send3))
-    shares(head_ref, held_mixed, (mixed_own_ref, mixed_send1, mixed_send2, mixed_send3))
-
-
-def near_kernel(pieces_ref, part0, part1, part2, part3, terms_ref, frames_grad_ref):
+
+
+def near_kernel(pieces_ref, part0, part1, after_ref, terms_ref, mixed_ref):
     terms_ref[...] = added([pieces_ref.at[i] for i in range(pieces_ref.shape[0])]).astype(BF16)
-    frames_grad_ref[...] = added((part0, part1, part2, part3)).astype(BF16)
+    mixed_ref[...] = added((part0, part1)).astype(BF16)
 
 
 def far_kernel(pieces_ref, value_ref, out_ref):
@@ -174,14 +192,18 @@
     out_ref[...] = total[rows:]
 
 
-def mixed_kernel(part0, part1, part2, part3, mixed_ref):
-    mixed_ref[...] = added((part0, part1, part2, part3)).astype(BF16)
+def head_sum_kernel(part0, part1, part2, part3, sum_ref):
+    sum_ref[...] = added((part0, part1, part2, part3)).astype(BF16)
 
 
 def passed_along(value, steps):
     count = lax.axis_size("seq")
     first, last = max(0, -steps), min(count, count - steps)
     return lax.ppermute(value, "seq", [(i, i + steps) for i in range(first, last)])
+
+
+def with_head(value, other):
+    return lax.ppermute(value, "head", [(i, i ^ other) for i in range(lax.axis_size("head"))])
 
 
 def exchanged(sends):
@@ -237,32 +259,47 @@
         transcendentals=pairs,
     )
     fars = [passed_along(fars[k - 1], -k) for k in range(1, WINDOW)]
-    kv_grad, terms = call(
+    shared = shape_of((share, width), BF16)
+    pair = shape_of((2 * share, width), BF16)
+    pair_kept, pair_sent = call(
+        mix_kernel,
+        [pair, pair],
+        [group, attended, out_weight, fars[0]],
+        [held],
+        smem=1,
+        flops=square * width,
+    )
+    kv_grad, terms, mixed_kept, mixed_sent = call(
         functools.partial(weights_kernel, (outer, inner, tail)),
-        [kv_shape, shape_of((inner, 2 * outer * tail, span), BF16)],
-        [frames, grads, attended, own, *fars],
+        [
+            kv_shape,
+            shape_of((inner, 2 * outer * tail, span), BF16),
+            shape_of((share, width), F32),
+            shared,
+        ],
+        [group, frames, grads, attended, own, *fars, pair_kept, with_head(pair_sent, 1)],
+        [pltpu.VMEM((2 * share, width), F32)],
+        smem=1,
         flops=2 * square * width,
     )
+    mixed_received = with_head(mixed_sent, 2)
     terms = lax.all_to_all(terms, "seq", 0, 0, axis_index_groups=near, tiled=True)
-    shared = shape_of((share, width), BF16)
-    sends = call(
+    kept, *sends = call(
         input_kernel,
-        [shared] * (2 * groups),
-        [group, dq, kv_grad, query_weight, key_weight, value_weight, attended, out_weight],
-        [held, held],
+        [shared] * groups,
+        [group, dq, kv_grad, query_weight, key_weight, value_weight],
+        [held],
         smem=1,
-        flops=4 * square * width,
-    )
-    frames_parts = [sends[0], *exchanged(sends[1:groups])]
-    mixed_parts = [sends[groups], *exchanged(sends[groups + 1 :])]
-    terms, frames_grad = call(
+        flops=3 * square * width,
+    )
+    terms, mixed = call(
         near_kernel,
         [shape_of((2 * outer * tail, span), BF16), shared],
-        [terms, *frames_parts],
+        [terms, mixed_kept, mixed_received, kept],
     )
     terms = terms.reshape(outer, 2 * tail, span)
     terms = lax.all_to_all(terms, "seq", 0, 0, axis_index_groups=across, tiled=True)
-    [mixed] = call(mixed_kernel, [shared], mixed_parts)
+    [frames_grad] = call(head_sum_kernel, [shared], [kept, *exchanged(sends)])
     value_sum, out_sum = call(far_kernel, [shape_of((tail, span), F32)] * 2, [terms])
     return mixed, frames_grad, value_sum, out_sum.T
 

time: 136 us -> 139 us (1.022)
  local copies, waits for them, and re-layouts: 7.94 us -> 11 us
  starting transfers between devices: 62.6 us -> 60.2 us
  Pallas kernels: 10.6 us -> 12 us
    ppermute x0 -> x2, waiting for transfers between devices: none -> 9.4 us  [with_head(): lax.ppermute(value, 'head', [(i, i ^ other) for i in range(lax.axis_size(...]
    ppermute x6 -> x3, starting transfers between devices: 19.7 us -> 11.5 us  [exchanged(): received[other] = lax.ppermute(sends[other - 1], 'head', pairs)]
    ppermute x0 -> x2, starting transfers between devices: none -> 5.3 us  [with_head(): lax.ppermute(value, 'head', [(i, i ^ other) for i in range(lax.axis_size(...]
    ppermute x6 -> x3, waiting for transfers between devices: 9.68 us -> 4.82 us  [exchanged(): received[other] = lax.ppermute(sends[other - 1], 'head', pairs)]
    ppermute x6, waiting for transfers between devices: 19 us -> 15.2 us  [passed_along(): lax.ppermute(value, 'seq', [(i, i + steps) for i in range(first, last)])]
    unnamed x41 -> x53, local copies, waits for them, and re-layouts: 7.86 us -> 11 us
    pallas_call x8 -> x9, Pallas kernels: 10.6 us -> 12 us  [call(): pl.pallas_call(kernel, out_shape=outs, in_specs=specs, out_specs=[pl.Bloc...]
  transfers between devices with their start and end apart: 14 -> 13, of which waited for: 7 -> 6; matrix products, arithmetic and copies ran while one was open for 0% -> 0% of each run, Pallas kernels for 1% -> 2%
where the time goes in v4:
time: 139 us; the launch traced here: 138 us
  starting transfers between devices  60.2 us (43%)
  waiting for transfers between devices  29.5 us (21%)
  blocking collectives  24.3 us (17%)
  Pallas kernels  12 us (9%)
  local copies, waits for them, and re-layouts  11 us (8%)
    all_to_all x1, starting transfers between devices, per_device(): lax.all_to_all(terms, 'seq', 0, 0, axis_index_groups=across, tiled=True)  18.2 us
    all_to_all x1, starting transfers between devices, per_device(): lax.all_to_all(terms, 'seq', 0, 0, axis_index_groups=near, tiled=True)  15.2 us
    ppermute x6, waiting for transfers between devices, passed_along(): lax.ppermute(value, 'seq', [(i, i + steps) for i in range(first, last)])  15.2 us
    all_gather x1, blocking collectives, per_device(): frames = lax.all_gather(frames_in, 'head', axis=0, tiled=True)  15.1 us
    pallas_call x9, Pallas kernels, call(): pl.pallas_call(kernel, out_shape=outs, in_specs=specs, out_specs=[pl.Bloc...  12 us
    ppermute x3, starting transfers between devices, exchanged(): received[other] = lax.ppermute(sends[other - 1], 'head', pairs)  11.5 us
    unnamed x53, local copies, waits for them, and re-layouts  11 us
    ppermute x6, starting transfers between devices, passed_along(): lax.ppermute(value, 'seq', [(i, i + steps) for i in range(first, last)])  10 us
  transfers between devices with their start and end apart: 13, of which 6 were waited for; matrix products, arithmetic and copies ran while one was open for 0% of the time, Pallas kernels for 2%

profile of v4, /device:TPU:1, one launch (start us, length us, event | category | flops | bytes accessed | tf_op | source)
XLA Modules:
  0.0 137.9 jit_solution(3569614658476774599)
XLA Ops:
  0.7 15.1 %all_gather.6.frames_ref = bf16[256,1024]{1,0:T(8,128)(2,1)S(1)} all-gather(bf16[64,1024]{1,0:T(8,128)(2,1)} %param.7), channel_id=1, replica_groups=mesh['seq'=128,'head'=4] {'head'}, dimensions={0}, use_global_device_ids=true | all-gather | bytes 655360 | tf_op jit(solution)/shard_map/all_gather | solution.py:238
  15.7 1.0 copy-done.2
  17.2 1.4 %collective-permute-start.2 = (bf16[256,512]{1,0:T(8,128)(2,1)S(1)}, bf16[256,512]{1,0:T(8,128)(2,1)S(1)}, u32[]{:S(2)}, u32[]{:S(2)}) collective-permute-start(bf16[256,512]{1,0:T(8,128)(2,1)S(1)} %shard_map.103.kv0), channel_id=1, source_target_pairs={{0,12},{4,16},{8,20},{12,24},{16,28},{20,32},{24,36},{28,40},{32,4... | collective-permute-start | bytes 786440 | tf_op jit(solution)/shard_map/ppermute | solution.py:202
  18.7 1.4 %collective-permute-start.1 = (bf16[256,512]{1,0:T(8,128)(2,1)S(1)}, bf16[256,512]{1,0:T(8,128)(2,1)S(1)}, u32[]{:S(2)}, u32[]{:S(2)}) collective-permute-start(bf16[256,512]{1,0:T(8,128)(2,1)S(1)} %shard_map.103.kv0), channel_id=1, source_target_pairs={{0,8},{4,12},{8,16},{12,20},{16,24},{20,28},{24,32},{28,36},{32,40... | collective-permute-start | bytes 786440 | tf_op jit(solution)/shard_map/ppermute | solution.py:202
  20.1 3.3 %collective-permute-start = (bf16[256,512]{1,0:T(8,128)(2,1)S(1)}, bf16[256,512]{1,0:T(8,128)(2,1)}, u32[]{:S(2)}, u32[]{:S(2)}) collective-permute-start(bf16[256,512]{1,0:T(8,128)(2,1)S(1)} %shard_map.103.kv0), channel_id=1, source_target_pairs={{0,4},{4,8},{8,12},{12,16},{16,20},{20,24},{24,28},{28,32},{32,36}... | collective-permute-start | bytes 786440 | tf_op jit(solution)/shard_map/ppermute | solution.py:202
  23.6 9.2 %all_gather.7.grads_ref = bf16[256,1024]{1,0:T(8,128)(2,1)S(1)} all-gather(bf16[64,1024]{1,0:T(8,128)(2,1)S(1)} %copy-done.25), channel_id=1, replica_groups=mesh['seq'=128,'head'=4] {'head'}, dimensions={0}, use_global_device_ids=true | all-gather | bytes 655360 | tf_op jit(solution)/shard_map/all_gather | solution.py:241
  34.1 0.7 copy-done.15
  34.8 0.9 copy-done.14
  35.8 0.9 copy-done.16
  36.7 6.5 %shard_map.104 = (bf16[256,256]{1,0:T(8,128)(2,1)S(1)}, bf16[256,256]{1,0:T(8,128)(2,1)S(1)}, f32[256,512]{1,0:T(8,128)S(1)}, bf16[256,512]{1,0:T(8,128)(2,1)}, ...) custom-call(s32[1,3]{1,0:T(1,128)S(1)} %copy.12.mask_ref, bf16[256,256]{1,0:T(8,128)(2,1)S(1)} %get-tuple-element.26.qt_ref, ...), custom_call_target="tpu_custom_call" | custom-call | flops 3221225472 | bytes 2883596 | tf_op jit(solution)/shard_map/pallas_call | solution.py:39
  44.6 0.7 copy-done.18
  45.3 1.3 collective-permute-start.3
  46.6 1.3 collective-permute-start.4
  47.9 1.3 collective-permute-start.5
  49.2 6.0 %collective-permute-done.3.after_ref.far1 = bf16[256,512]{1,0:T(8,128)(2,1)S(1)} collective-permute-done((bf16[256,512]{1,0:T(8,128)(2,1)}, bf16[256,512]{1,0:T(8,128)(2,1)S(1)}, u32[]{:S(2)}, u32[]{:S(2)}) %collective-permute-start.3) | collective-permute-done | bytes 262176 | tf_op jit(solution)/shard_map/ppermute | solution.py:202
  55.6 2.9 %collective-permute-start.6 = (bf16[128,1024]{1,0:T(8,128)(2,1)S(1)}, bf16[128,1024]{1,0:T(8,128)(2,1)S(1)}, u32[]{:S(2)}, u32[]{:S(2)}) collective-permute-start(bf16[128,1024]{1,0:T(8,128)(2,1)S(1)} %get-tuple-element.34), channel_id=1, source_target_pairs={{0,1},{1,0},{2,3},{3,2},{4,5},{5,4},{6,7},{7,6},{8,9},{9,8},{10,11... | collective-permute-start | bytes 786440 | tf_op jit(solution)/shard_map/ppermute | solution.py:206
  58.4 1.7 %collective-permute-done.4.far2 = bf16[256,512]{1,0:T(8,128)(2,1)S(1)} collective-permute-done((bf16[256,512]{1,0:T(8,128)(2,1)}, bf16[256,512]{1,0:T(8,128)(2,1)S(1)}, u32[]{:S(2)}, u32[]{:S(2)}) %collective-permute-start.4) | collective-permute-done | bytes 262176 | tf_op jit(solution)/shard_map/ppermute | solution.py:202
  60.1 7.5 %collective-permute-done.5.far3 = bf16[256,512]{1,0:T(8,128)(2,1)S(1)} collective-permute-done((bf16[256,512]{1,0:T(8,128)(2,1)}, bf16[256,512]{1,0:T(8,128)(2,1)S(1)}, u32[]{:S(2)}, u32[]{:S(2)}) %collective-permute-start.5) | collective-permute-done | bytes 262176 | tf_op jit(solution)/shard_map/ppermute | solution.py:202
  67.7 1.3 shard_map.106
  69.0 1.0 copy-done.6
  70.0 0.7 copy-done.7
  71.4 15.2 %all-to-all-start = ((bf16[8,256,256]{2,1,0:T(8,128)(2,1)}), bf16[8,256,256]{2,1,0:T(8,128)(2,1)S(1)}, u32[]{:S(2)}, u32[]{:S(2)}) async-start(bf16[8,256,256]{2,1,0:T(8,128)(2,1)} %copy-done.6), calls=%async_computation | async-start | bytes 2097152 | tf_op jit(solution)/shard_map/all_to_all | solution.py:286
  86.6 2.4 %collective-permute-start.7 = (bf16[64,1024]{1,0:T(8,128)(2,1)}, bf16[64,1024]{1,0:T(8,128)(2,1)S(1)}, u32[]{:S(2)}, u32[]{:S(2)}) collective-permute-start(bf16[64,1024]{1,0:T(8,128)(2,1)} %get-tuple-element.37), channel_id=1, source_target_pairs={{0,2},{1,3},{2,0},{3,1},{4,6},{5,7},{6,4},{7,5},{8,10},{9,11},{10,... | collective-permute-start | bytes 393224 | tf_op jit(solution)/shard_map/ppermute | solution.py:206
  91.7 9.4 %collective-permute-done.7.part1 = bf16[64,1024]{1,0:T(8,128)(2,1)S(1)} collective-permute-done((bf16[64,1024]{1,0:T(8,128)(2,1)}, bf16[64,1024]{1,0:T(8,128)(2,1)S(1)}, u32[]{:S(2)}, u32[]{:S(2)}) %collective-permute-start.7) | collective-permute-done | bytes 131104 | tf_op jit(solution)/shard_map/ppermute | solution.py:206
  101.1 0.8 shard_map.108
  102.0 18.2 %all-to-all-start.1 = ((bf16[16,16,256]{2,1,0:T(8,128)(2,1)}), bf16[16,16,256]{2,1,0:T(8,128)(2,1)S(1)}, u32[]{:S(2)}, u32[]{:S(2)}) async-start(bf16[16,16,256]{2,1,0:T(8,128)(2,1)} %bitcast.1), calls=%async_computation.1 | async-start | bytes 262144 | tf_op jit(solution)/shard_map/all_to_all | solution.py:301
  120.2 4.5 %collective-permute-start.8 = (bf16[64,1024]{1,0:T(8,128)(2,1)S(1)}, bf16[64,1024]{1,0:T(8,128)(2,1)S(1)}, u32[]{:S(2)}, u32[]{:S(2)}) collective-permute-start(bf16[64,1024]{1,0:T(8,128)(2,1)S(1)} %copy-done.24), channel_id=1, source_target_pairs={{0,1},{1,0},{2,3},{3,2},{4,5},{5,4},{6,7},{7,6},{8,9},{9,8},{10,11... | collective-permute-start | bytes 393224 | tf_op jit(solution)/shard_map/ppermute | solution.py:214
  124.7 3.0 %collective-permute-start.9 = (bf16[64,1024]{1,0:T(8,128)(2,1)S(1)}, bf16[64,1024]{1,0:T(8,128)(2,1)S(1)}, u32[]{:S(2)}, u32[]{:S(2)}) collective-permute-start(bf16[64,1024]{1,0:T(8,128)(2,1)S(1)} %copy-done.22), channel_id=1, source_target_pairs={{0,2},{1,3},{2,0},{3,1},{4,6},{5,7},{6,4},{7,5},{8,10},{9,11},{10,... | collective-permute-start | bytes 393224 | tf_op jit(solution)/shard_map/ppermute | solution.py:214
  127.8 4.0 %collective-permute-start.10 = (bf16[64,1024]{1,0:T(8,128)(2,1)S(1)}, bf16[64,1024]{1,0:T(8,128)(2,1)S(1)}, u32[]{:S(2)}, u32[]{:S(2)}) collective-permute-start(bf16[64,1024]{1,0:T(8,128)(2,1)S(1)} %copy-done.20), channel_id=1, source_target_pairs={{0,3},{1,2},{2,1},{3,0},{4,7},{5,6},{6,5},{7,4},{8,11},{9,10},{10,... | collective-permute-start | bytes 393224 | tf_op jit(solution)/shard_map/ppermute | solution.py:214
  131.7 1.5 %collective-permute-done.9.part2 = bf16[64,1024]{1,0:T(8,128)(2,1)S(1)} collective-permute-done((bf16[64,1024]{1,0:T(8,128)(2,1)S(1)}, bf16[64,1024]{1,0:T(8,128)(2,1)S(1)}, u32[]{:S(2)}, u32[]{:S(2)}) %collective-permute-start.9) | collective-permute-done | bytes 131104 | tf_op jit(solution)/shard_map/ppermute | solution.py:214
  133.3 3.3 %collective-permute-done.10.part3 = bf16[64,1024]{1,0:T(8,128)(2,1)S(1)} collective-permute-done((bf16[64,1024]{1,0:T(8,128)(2,1)S(1)}, bf16[64,1024]{1,0:T(8,128)(2,1)S(1)}, u32[]{:S(2)}, u32[]{:S(2)}) %collective-permute-start.10) | collective-permute-done | bytes 131104 | tf_op jit(solution)/shard_map/ppermute | solution.py:214
  136.6 0.7 shard_map.109
  (59 shorter events, 7.6 us)
Async XLA Ops:
  0.6 22.8 %copy-start = (s32[128,3]{0,1:T(4,128)S(1)}, s32[128,3]{0,1:T(4,128)}, u32[]{:S(2)}) copy-start(s32[128,3]{0,1:T(4,128)} %param.12) | copy-start | bytes 4612
  0.6 15.1 %copy-start.1 = (bf16[1024,256]{1,0:T(8,128)(2,1)S(1)}, bf16[1024,256]{1,0:T(8,128)(2,1)}, u32[]{:S(2)}) copy-start(bf16[1024,256]{1,0:T(8,128)(2,1)} %key_weight_ref.3) | copy-start | bytes 1572868
  15.7 1.0 copy-start.2
  16.8 6.8 %copy-start.25 = (bf16[64,1024]{1,0:T(8,128)(2,1)S(1)}, bf16[64,1024]{1,0:T(8,128)(2,1)}, u32[]{:S(2)}) copy-start(bf16[64,1024]{1,0:T(8,128)(2,1)} %param.13) | copy-start | bytes 393220
  16.8 16.1 %copy-start.5 = (bf16[256,1024]{1,0:T(8,128)(2,1)S(1)}, bf16[256,1024]{1,0:T(8,128)(2,1)}, u32[]{:S(2)}) copy-start(bf16[256,1024]{1,0:T(8,128)(2,1)} %out_weight_ref.3) | copy-start | bytes 1572868
  17.2 15.6 %copy-start.4 = (bf16[1024,256]{1,0:T(8,128)(2,1)S(1)}, bf16[1024,256]{1,0:T(8,128)(2,1)}, u32[]{:S(2)}) copy-start(bf16[1024,256]{1,0:T(8,128)(2,1)} %query_weight_ref.3) | copy-start | bytes 1572868
  17.2 16.1 %collective-permute-start.2 = (bf16[256,512]{1,0:T(8,128)(2,1)S(1)}, bf16[256,512]{1,0:T(8,128)(2,1)S(1)}, u32[]{:S(2)}, u32[]{:S(2)}) collective-permute-start(bf16[256,512]{1,0:T(8,128)(2,1)S(1)} %shard_map.103.kv0), channel_id=1, source_target_pairs={{0,12},{4,16},{8,20},{12,24},{16,28},{20,32},{24,36},{28,40},{32,4... | collective-permute-start | bytes 786440 | tf_op jit(solution)/shard_map/ppermute | solution.py:202
  18.7 15.4 %collective-permute-start.1 = (bf16[256,512]{1,0:T(8,128)(2,1)S(1)}, bf16[256,512]{1,0:T(8,128)(2,1)S(1)}, u32[]{:S(2)}, u32[]{:S(2)}) collective-permute-start(bf16[256,512]{1,0:T(8,128)(2,1)S(1)} %shard_map.103.kv0), channel_id=1, source_target_pairs={{0,8},{4,12},{8,16},{12,20},{16,24},{20,28},{24,32},{28,36},{32,40... | collective-permute-start | bytes 786440 | tf_op jit(solution)/shard_map/ppermute | solution.py:202
  20.1 14.7 %collective-permute-start = (bf16[256,512]{1,0:T(8,128)(2,1)S(1)}, bf16[256,512]{1,0:T(8,128)(2,1)}, u32[]{:S(2)}, u32[]{:S(2)}) collective-permute-start(bf16[256,512]{1,0:T(8,128)(2,1)S(1)} %shard_map.103.kv0), channel_id=1, source_target_pairs={{0,4},{4,8},{8,12},{12,16},{16,20},{20,24},{24,28},{28,32},{32,36}... | collective-permute-start | bytes 786440 | tf_op jit(solution)/shard_map/ppermute | solution.py:202
  33.4 0.7 copy-start.13
  34.1 0.7 copy-start.15
  34.8 1.0 copy-start.14
  35.8 0.9 copy-start.16
  45.3 9.8 %collective-permute-start.3 = (bf16[256,512]{1,0:T(8,128)(2,1)}, bf16[256,512]{1,0:T(8,128)(2,1)S(1)}, u32[]{:S(2)}, u32[]{:S(2)}) collective-permute-start(bf16[256,512]{1,0:T(8,128)(2,1)} %get-tuple-element.30), channel_id=1, source_target_pairs={{4,0},{8,4},{12,8},{16,12},{20,16},{24,20},{28,24},{32,28},{36,32}... | collective-permute-start | bytes 786440 | tf_op jit(solution)/shard_map/ppermute | solution.py:202
  46.6 13.5 %collective-permute-start.4 = (bf16[256,512]{1,0:T(8,128)(2,1)}, bf16[256,512]{1,0:T(8,128)(2,1)S(1)}, u32[]{:S(2)}, u32[]{:S(2)}) collective-permute-start(bf16[256,512]{1,0:T(8,128)(2,1)} %copy-done.18), channel_id=1, source_target_pairs={{8,0},{12,4},{16,8},{20,12},{24,16},{28,20},{32,24},{36,28},{40,32... | collective-permute-start | bytes 786440 | tf_op jit(solution)/shard_map/ppermute | solution.py:202
  47.9 19.8 %collective-permute-start.5 = (bf16[256,512]{1,0:T(8,128)(2,1)}, bf16[256,512]{1,0:T(8,128)(2,1)S(1)}, u32[]{:S(2)}, u32[]{:S(2)}) collective-permute-start(bf16[256,512]{1,0:T(8,128)(2,1)} %copy-done.17), channel_id=1, source_target_pairs={{12,0},{16,4},{20,8},{24,12},{28,16},{32,20},{36,24},{40,28},{44,3... | collective-permute-start | bytes 786440 | tf_op jit(solution)/shard_map/ppermute | solution.py:202
  55.6 12.1 %collective-permute-start.6 = (bf16[128,1024]{1,0:T(8,128)(2,1)S(1)}, bf16[128,1024]{1,0:T(8,128)(2,1)S(1)}, u32[]{:S(2)}, u32[]{:S(2)}) collective-permute-start(bf16[128,1024]{1,0:T(8,128)(2,1)S(1)} %get-tuple-element.34), channel_id=1, source_target_pairs={{0,1},{1,0},{2,3},{3,2},{4,5},{5,4},{6,7},{7,6},{8,9},{9,8},{10,11... | collective-permute-start | bytes 786440 | tf_op jit(solution)/shard_map/ppermute | solution.py:206
  69.0 1.0 copy-start.6
  70.0 0.7 copy-start.7
  71.4 17.6 %copy-start.3 = (bf16[1024,256]{1,0:T(8,128)(2,1)S(1)}, bf16[1024,256]{1,0:T(8,128)(2,1)}, u32[]{:S(2)}) copy-start(bf16[1024,256]{1,0:T(8,128)(2,1)} %value_weight_ref.3) | copy-start | bytes 1572868
  71.4 17.6 %copy-start.8 = (bf16[256,512]{1,0:T(8,128)(2,1)S(1)}, bf16[256,512]{1,0:T(8,128)(2,1)}, u32[]{:S(2)}) copy-start(bf16[256,512]{1,0:T(8,128)(2,1)} %copy-done.7) | copy-start | bytes 786436
  71.4 17.7 %copy-start.12 = (bf16[256,256]{1,0:T(8,128)(2,1)S(1)}, bf16[256,256]{1,0:T(8,128)(2,1)}, u32[]{:S(2)}) copy-start(bf16[256,256]{1,0:T(8,128)(2,1)} %copy-done.11) | copy-start | bytes 393220
  71.4 29.7 %all-to-all-start = ((bf16[8,256,256]{2,1,0:T(8,128)(2,1)}), bf16[8,256,256]{2,1,0:T(8,128)(2,1)S(1)}, u32[]{:S(2)}, u32[]{:S(2)}) async-start(bf16[8,256,256]{2,1,0:T(8,128)(2,1)} %copy-done.6), calls=%async_computation | async-start | bytes 2097152 | tf_op jit(solution)/shard_map/all_to_all | solution.py:286
  86.6 14.5 %collective-permute-start.7 = (bf16[64,1024]{1,0:T(8,128)(2,1)}, bf16[64,1024]{1,0:T(8,128)(2,1)S(1)}, u32[]{:S(2)}, u32[]{:S(2)}) collective-permute-start(bf16[64,1024]{1,0:T(8,128)(2,1)} %get-tuple-element.37), channel_id=1, source_target_pairs={{0,2},{1,3},{2,0},{3,1},{4,6},{5,7},{6,4},{7,5},{8,10},{9,11},{10,... | collective-permute-start | bytes 393224 | tf_op jit(solution)/shard_map/ppermute | solution.py:206
  89.1 12.1 %copy-start.10 = (f32[64,1024]{1,0:T(8,128)S(1)}, f32[64,1024]{1,0:T(8,128)}, u32[]{:S(2)}) copy-start(f32[64,1024]{1,0:T(8,128)} %copy-done.9) | copy-start | bytes 786436
  101.1 19.1 %copy-start.24 = (bf16[64,1024]{1,0:T(8,128)(2,1)S(1)}, bf16[64,1024]{1,0:T(8,128)(2,1)}, u32[]{:S(2)}) copy-start(bf16[64,1024]{1,0:T(8,128)(2,1)} %copy-done.23) | copy-start | bytes 393220
  102.0 22.8 %copy-start.22 = (bf16[64,1024]{1,0:T(8,128)(2,1)S(1)}, bf16[64,1024]{1,0:T(8,128)(2,1)}, u32[]{:S(2)}) copy-start(bf16[64,1024]{1,0:T(8,128)(2,1)} %copy-done.21) | copy-start | bytes 393220
  102.0 25.8 %copy-start.20 = (bf16[64,1024]{1,0:T(8,128)(2,1)S(1)}, bf16[64,1024]{1,0:T(8,128)(2,1)}, u32[]{:S(2)}) copy-start(bf16[64,1024]{1,0:T(8,128)(2,1)} %copy-done.19) | copy-start | bytes 393220
  102.0 35.3 %all-to-all-start.1 = ((bf16[16,16,256]{2,1,0:T(8,128)(2,1)}), bf16[16,16,256]{2,1,0:T(8,128)(2,1)S(1)}, u32[]{:S(2)}, u32[]{:S(2)}) async-start(bf16[16,16,256]{2,1,0:T(8,128)(2,1)} %bitcast.1), calls=%async_computation.1 | async-start | bytes 262144 | tf_op jit(solution)/shard_map/all_to_all | solution.py:301
  120.2 11.5 %collective-permute-start.8 = (bf16[64,1024]{1,0:T(8,128)(2,1)S(1)}, bf16[64,1024]{1,0:T(8,128)(2,1)S(1)}, u32[]{:S(2)}, u32[]{:S(2)}) collective-permute-start(bf16[64,1024]{1,0:T(8,128)(2,1)S(1)} %copy-done.24), channel_id=1, source_target_pairs={{0,1},{1,0},{2,3},{3,2},{4,5},{5,4},{6,7},{7,6},{8,9},{9,8},{10,11... | collective-permute-start | bytes 393224 | tf_op jit(solution)/shard_map/ppermute | solution.py:214
  124.7 8.5 %collective-permute-start.9 = (bf16[64,1024]{1,0:T(8,128)(2,1)S(1)}, bf16[64,1024]{1,0:T(8,128)(2,1)S(1)}, u32[]{:S(2)}, u32[]{:S(2)}) collective-permute-start(bf16[64,1024]{1,0:T(8,128)(2,1)S(1)} %copy-done.22), channel_id=1, source_target_pairs={{0,2},{1,3},{2,0},{3,1},{4,6},{5,7},{6,4},{7,5},{8,10},{9,11},{10,... | collective-permute-start | bytes 393224 | tf_op jit(solution)/shard_map/ppermute | solution.py:214
  127.8 8.8 %collective-permute-start.10 = (bf16[64,1024]{1,0:T(8,128)(2,1)S(1)}, bf16[64,1024]{1,0:T(8,128)(2,1)S(1)}, u32[]{:S(2)}, u32[]{:S(2)}) collective-permute-start(bf16[64,1024]{1,0:T(8,128)(2,1)S(1)} %copy-done.20), channel_id=1, source_target_pairs={{0,3},{1,2},{2,1},{3,0},{4,7},{5,6},{6,5},{7,4},{8,11},{9,10},{10,... | collective-permute-start | bytes 393224 | tf_op jit(solution)/shard_map/ppermute | solution.py:214
  (7 other events, 4.7 us)

commit v5 on v4

--- a/solution.py
+++ b/solution.py
@@ -10,7 +10,7 @@
 HEAD_DIM = 64
 WINDOW = 4
 FAR = 1e30
-VMEM_LIMIT = 24 * 1024 * 1024
+VMEM_LIMIT = 12 * 1024 * 1024
 
 F32 = jnp.float32
 BF16 = jnp.bfloat16
@@ -206,15 +206,6 @@
     return lax.ppermute(value, "head", [(i, i ^ other) for i in range(lax.axis_size("head"))])
 
 
-def exchanged(sends):
-    count = lax.axis_size("head")
-    received = {}
-    for other in range(count - 1, 0, -1):
-        pairs = [(i, i ^ other) for i in range(count)]
-        received[other] = lax.ppermute(sends[other - 1], "head", pairs)
-    return [received[other] for other in range(1, count)]
-
-
 def per_device(inner, frames_in, query_weight, key_weight, value_weight, out_weight, read_mask, out_grad):
     seq = lax.axis_size("seq")
     groups = lax.axis_size("head")
@@ -292,14 +283,16 @@
         smem=1,
         flops=3 * square * width,
     )
+    received = [with_head(sends[0], 1)]
     terms, mixed = call(
         near_kernel,
         [shape_of((2 * outer * tail, span), BF16), shared],
-        [terms, mixed_kept, mixed_received, kept],
+        [terms, mixed_kept, mixed_received, received[0]],
     )
     terms = terms.reshape(outer, 2 * tail, span)
     terms = lax.all_to_all(terms, "seq", 0, 0, axis_index_groups=across, tiled=True)
-    [frames_grad] = call(head_sum_kernel, [shared], [kept, *exchanged(sends)])
+    received += [with_head(sends[other - 1], other) for other in range(2, groups)]
+    [frames_grad] = call(head_sum_kernel, [shared], [kept, *received])
     value_sum, out_sum = call(far_kernel, [shape_of((tail, span), F32)] * 2, [terms])
     return mixed, frames_grad, value_sum, out_sum.T
 

time: 139 us -> 136 us (0.978)
  waiting for transfers between devices: 29.5 us -> 25.3 us
  starting transfers between devices: 60.2 us -> 61.8 us
    ppermute x2 -> x5, starting transfers between devices: 5.3 us -> 18.3 us  [with_head(): lax.ppermute(value, 'head', [(i, i ^ other) for i in range(lax.axis_size(...]
    ppermute x3 -> x0, starting transfers between devices: 11.5 us -> none  [exchanged(): received[other] = lax.ppermute(sends[other - 1], 'head', pairs)]
    ppermute x3 -> x0, waiting for transfers between devices: 4.82 us -> none  [exchanged(): received[other] = lax.ppermute(sends[other - 1], 'head', pairs)]
    ppermute x2 -> x5, waiting for transfers between devices: 9.4 us -> 10.1 us  [with_head(): lax.ppermute(value, 'head', [(i, i ^ other) for i in range(lax.axis_size(...]
    unnamed x53 -> x49, local copies, waits for them, and re-layouts: 11 us -> 10.3 us
where the time goes in v5:
time: 136 us; the launch traced here: 135 us
  starting transfers between devices  61.8 us (45%)
  waiting for transfers between devices  25.3 us (19%)
  blocking collectives  24.3 us (18%)
  Pallas kernels  12 us (9%)
  local copies, waits for them, and re-layouts  10.4 us (8%)
    ppermute x5, starting transfers between devices, with_head(): lax.ppermute(value, 'head', [(i, i ^ other) for i in range(lax.axis_size(...  18.3 us
    all_to_all x1, starting transfers between devices, per_device(): lax.all_to_all(terms, 'seq', 0, 0, axis_index_groups=across, tiled=True)  18.2 us
    all_to_all x1, starting transfers between devices, per_device(): lax.all_to_all(terms, 'seq', 0, 0, axis_index_groups=near, tiled=True)  15.2 us
    ppermute x6, waiting for transfers between devices, passed_along(): lax.ppermute(value, 'seq', [(i, i + steps) for i in range(first, last)])  15.2 us
    all_gather x1, blocking collectives, per_device(): frames = lax.all_gather(frames_in, 'head', axis=0, tiled=True)  15.1 us
    pallas_call x9, Pallas kernels, call(): pl.pallas_call(kernel, out_shape=outs, in_specs=specs, out_specs=[pl.Bloc...  12 us
    unnamed x49, local copies, waits for them, and re-layouts  10.3 us
    ppermute x5, waiting for transfers between devices, with_head(): lax.ppermute(value, 'head', [(i, i ^ other) for i in range(lax.axis_size(...  10.1 us
  transfers between devices with their start and end apart: 13, of which 6 were waited for; matrix products, arithmetic and copies ran while one was open for 0% of the time, Pallas kernels for 2%

profile of v5, /device:TPU:1, one launch (start us, length us, event | category | flops | bytes accessed | tf_op | source)
XLA Modules:
  0.0 134.7 jit_solution(9960742899577429637)
XLA Ops:
  0.7 15.1 %all_gather.6.frames_ref = bf16[256,1024]{1,0:T(8,128)(2,1)S(1)} all-gather(bf16[64,1024]{1,0:T(8,128)(2,1)} %param.7), channel_id=1, replica_groups=mesh['seq'=128,'head'=4] {'head'}, dimensions={0}, use_global_device_ids=true | all-gather | bytes 655360 | tf_op jit(solution)/shard_map/all_gather | solution.py:229
  15.7 1.0 copy-done.2
  17.2 1.4 %collective-permute-start.2 = (bf16[256,512]{1,0:T(8,128)(2,1)S(1)}, bf16[256,512]{1,0:T(8,128)(2,1)S(1)}, u32[]{:S(2)}, u32[]{:S(2)}) collective-permute-start(bf16[256,512]{1,0:T(8,128)(2,1)S(1)} %shard_map.103.kv0), channel_id=1, source_target_pairs={{0,12},{4,16},{8,20},{12,24},{16,28},{20,32},{24,36},{28,40},{32,4... | collective-permute-start | bytes 786440 | tf_op jit(solution)/shard_map/ppermute | solution.py:202
  18.7 1.4 %collective-permute-start.1 = (bf16[256,512]{1,0:T(8,128)(2,1)S(1)}, bf16[256,512]{1,0:T(8,128)(2,1)S(1)}, u32[]{:S(2)}, u32[]{:S(2)}) collective-permute-start(bf16[256,512]{1,0:T(8,128)(2,1)S(1)} %shard_map.103.kv0), channel_id=1, source_target_pairs={{0,8},{4,12},{8,16},{12,20},{16,24},{20,28},{24,32},{28,36},{32,40... | collective-permute-start | bytes 786440 | tf_op jit(solution)/shard_map/ppermute | solution.py:202
  20.1 3.3 %collective-permute-start = (bf16[256,512]{1,0:T(8,128)(2,1)S(1)}, bf16[256,512]{1,0:T(8,128)(2,1)}, u32[]{:S(2)}, u32[]{:S(2)}) collective-permute-start(bf16[256,512]{1,0:T(8,128)(2,1)S(1)} %shard_map.103.kv0), channel_id=1, source_target_pairs={{0,4},{4,8},{8,12},{12,16},{16,20},{20,24},{24,28},{28,32},{32,36}... | collective-permute-start | bytes 786440 | tf_op jit(solution)/shard_map/ppermute | solution.py:202
  23.6 9.2 %all_gather.7.grads_ref = bf16[256,1024]{1,0:T(8,128)(2,1)S(1)} all-gather(bf16[64,1024]{1,0:T(8,128)(2,1)S(1)} %copy-done.23), channel_id=1, replica_groups=mesh['seq'=128,'head'=4] {'head'}, dimensions={0}, use_global_device_ids=true | all-gather | bytes 655360 | tf_op jit(solution)/shard_map/all_gather | solution.py:232
  33.4 0.7 copy-done.13
  34.1 0.7 copy-done.15
  34.8 0.9 copy-done.14
  35.7 0.9 copy-done.16
  36.7 6.5 %shard_map.104 = (bf16[256,256]{1,0:T(8,128)(2,1)S(1)}, bf16[256,256]{1,0:T(8,128)(2,1)S(1)}, f32[256,512]{1,0:T(8,128)S(1)}, bf16[256,512]{1,0:T(8,128)(2,1)}, ...) custom-call(s32[1,3]{1,0:T(1,128)S(1)} %copy.12.mask_ref, bf16[256,256]{1,0:T(8,128)(2,1)S(1)} %get-tuple-element.26.qt_ref, ...), custom_call_target="tpu_custom_call" | custom-call | flops 3221225472 | bytes 2883596 | tf_op jit(solution)/shard_map/pallas_call | solution.py:39
  44.6 0.7 copy-done.18
  45.3 1.3 collective-permute-start.3
  46.6 1.3 collective-permute-start.4
  47.9 1.3 collective-permute-start.5
  49.2 6.0 %collective-permute-done.3.after_ref.far1 = bf16[256,512]{1,0:T(8,128)(2,1)S(1)} collective-permute-done((bf16[256,512]{1,0:T(8,128)(2,1)}, bf16[256,512]{1,0:T(8,128)(2,1)S(1)}, u32[]{:S(2)}, u32[]{:S(2)}) %collective-permute-start.3) | collective-permute-done | bytes 262176 | tf_op jit(solution)/shard_map/ppermute | solution.py:202
  55.5 2.9 %collective-permute-start.6 = (bf16[128,1024]{1,0:T(8,128)(2,1)S(1)}, bf16[128,1024]{1,0:T(8,128)(2,1)S(1)}, u32[]{:S(2)}, u32[]{:S(2)}) collective-permute-start(bf16[128,1024]{1,0:T(8,128)(2,1)S(1)} %get-tuple-element.34), channel_id=1, source_target_pairs={{0,1},{1,0},{2,3},{3,2},{4,5},{5,4},{6,7},{7,6},{8,9},{9,8},{10,11... | collective-permute-start | bytes 786440 | tf_op jit(solution)/shard_map/ppermute | solution.py:206
  58.4 1.6 %collective-permute-done.4.far2 = bf16[256,512]{1,0:T(8,128)(2,1)S(1)} collective-permute-done((bf16[256,512]{1,0:T(8,128)(2,1)}, bf16[256,512]{1,0:T(8,128)(2,1)S(1)}, u32[]{:S(2)}, u32[]{:S(2)}) %collective-permute-start.4) | collective-permute-done | bytes 262176 | tf_op jit(solution)/shard_map/ppermute | solution.py:202
  60.0 7.6 %collective-permute-done.5.far3 = bf16[256,512]{1,0:T(8,128)(2,1)S(1)} collective-permute-done((bf16[256,512]{1,0:T(8,128)(2,1)}, bf16[256,512]{1,0:T(8,128)(2,1)S(1)}, u32[]{:S(2)}, u32[]{:S(2)}) %collective-permute-start.5) | collective-permute-done | bytes 262176 | tf_op jit(solution)/shard_map/ppermute | solution.py:202
  67.7 1.3 shard_map.106
  69.0 1.0 copy-done.6
  70.0 0.7 copy-done.7
  71.4 15.2 %all-to-all-start = ((bf16[8,256,256]{2,1,0:T(8,128)(2,1)}), bf16[8,256,256]{2,1,0:T(8,128)(2,1)S(1)}, u32[]{:S(2)}, u32[]{:S(2)}) async-start(bf16[8,256,256]{2,1,0:T(8,128)(2,1)} %copy-done.6), calls=%async_computation | async-start | bytes 2097152 | tf_op jit(solution)/shard_map/all_to_all | solution.py:277
  86.6 2.4 %collective-permute-start.7 = (bf16[64,1024]{1,0:T(8,128)(2,1)}, bf16[64,1024]{1,0:T(8,128)(2,1)S(1)}, u32[]{:S(2)}, u32[]{:S(2)}) collective-permute-start(bf16[64,1024]{1,0:T(8,128)(2,1)} %get-tuple-element.37), channel_id=1, source_target_pairs={{0,2},{1,3},{2,0},{3,1},{4,6},{5,7},{6,4},{7,5},{8,10},{9,11},{10,... | collective-permute-start | bytes 393224 | tf_op jit(solution)/shard_map/ppermute | solution.py:206
  91.0 3.5 %collective-permute-start.8 = (bf16[64,1024]{1,0:T(8,128)(2,1)S(1)}, bf16[64,1024]{1,0:T(8,128)(2,1)S(1)}, u32[]{:S(2)}, u32[]{:S(2)}) collective-permute-start(bf16[64,1024]{1,0:T(8,128)(2,1)S(1)} %get-tuple-element.40), channel_id=1, source_target_pairs={{0,1},{1,0},{2,3},{3,2},{4,5},{5,4},{6,7},{7,6},{8,9},{9,8},{10,11... | collective-permute-start | bytes 393224 | tf_op jit(solution)/shard_map/ppermute | solution.py:206
  94.5 6.5 %collective-permute-done.7.part1 = bf16[64,1024]{1,0:T(8,128)(2,1)S(1)} collective-permute-done((bf16[64,1024]{1,0:T(8,128)(2,1)}, bf16[64,1024]{1,0:T(8,128)(2,1)S(1)}, u32[]{:S(2)}, u32[]{:S(2)}) %collective-permute-start.7) | collective-permute-done | bytes 131104 | tf_op jit(solution)/shard_map/ppermute | solution.py:206
  101.1 0.8 shard_map.108
  102.0 18.2 %all-to-all-start.1 = ((bf16[16,16,256]{2,1,0:T(8,128)(2,1)}), bf16[16,16,256]{2,1,0:T(8,128)(2,1)S(1)}, u32[]{:S(2)}, u32[]{:S(2)}) async-start(bf16[16,16,256]{2,1,0:T(8,128)(2,1)} %bitcast.1), calls=%async_computation.1 | async-start | bytes 262144 | tf_op jit(solution)/shard_map/all_to_all | solution.py:293
  120.2 3.3 %collective-permute-start.9 = (bf16[64,1024]{1,0:T(8,128)(2,1)S(1)}, bf16[64,1024]{1,0:T(8,128)(2,1)S(1)}, u32[]{:S(2)}, u32[]{:S(2)}) collective-permute-start(bf16[64,1024]{1,0:T(8,128)(2,1)S(1)} %copy-done.22), channel_id=1, source_target_pairs={{0,2},{1,3},{2,0},{3,1},{4,6},{5,7},{6,4},{7,5},{8,10},{9,11},{10,... | collective-permute-start | bytes 393224 | tf_op jit(solution)/shard_map/ppermute | solution.py:206
  123.5 6.2 %collective-permute-start.10 = (bf16[64,1024]{1,0:T(8,128)(2,1)S(1)}, bf16[64,1024]{1,0:T(8,128)(2,1)S(1)}, u32[]{:S(2)}, u32[]{:S(2)}) collective-permute-start(bf16[64,1024]{1,0:T(8,128)(2,1)S(1)} %copy-done.20), channel_id=1, source_target_pairs={{0,3},{1,2},{2,1},{3,0},{4,7},{5,6},{6,5},{7,4},{8,11},{9,10},{10,... | collective-permute-start | bytes 393224 | tf_op jit(solution)/shard_map/ppermute | solution.py:206
  129.8 3.5 %collective-permute-done.10.part3 = bf16[64,1024]{1,0:T(8,128)(2,1)S(1)} collective-permute-done((bf16[64,1024]{1,0:T(8,128)(2,1)S(1)}, bf16[64,1024]{1,0:T(8,128)(2,1)S(1)}, u32[]{:S(2)}, u32[]{:S(2)}) %collective-permute-start.10) | collective-permute-done | bytes 131104 | tf_op jit(solution)/shard_map/ppermute | solution.py:206
  133.3 0.7 shard_map.109
  (55 shorter events, 6.3 us)
Async XLA Ops:
  0.6 22.8 %copy-start = (s32[128,3]{0,1:T(4,128)S(1)}, s32[128,3]{0,1:T(4,128)}, u32[]{:S(2)}) copy-start(s32[128,3]{0,1:T(4,128)} %param.12) | copy-start | bytes 4612
  0.6 15.1 %copy-start.1 = (bf16[1024,256]{1,0:T(8,128)(2,1)S(1)}, bf16[1024,256]{1,0:T(8,128)(2,1)}, u32[]{:S(2)}) copy-start(bf16[1024,256]{1,0:T(8,128)(2,1)} %key_weight_ref.3) | copy-start | bytes 1572868
  15.7 1.0 copy-start.2
  16.8 6.8 %copy-start.23 = (bf16[64,1024]{1,0:T(8,128)(2,1)S(1)}, bf16[64,1024]{1,0:T(8,128)(2,1)}, u32[]{:S(2)}) copy-start(bf16[64,1024]{1,0:T(8,128)(2,1)} %param.13) | copy-start | bytes 393220
  16.8 16.1 %copy-start.5 = (bf16[256,1024]{1,0:T(8,128)(2,1)S(1)}, bf16[256,1024]{1,0:T(8,128)(2,1)}, u32[]{:S(2)}) copy-start(bf16[256,1024]{1,0:T(8,128)(2,1)} %out_weight_ref.3) | copy-start | bytes 1572868
  17.2 15.6 %copy-start.4 = (bf16[1024,256]{1,0:T(8,128)(2,1)S(1)}, bf16[1024,256]{1,0:T(8,128)(2,1)}, u32[]{:S(2)}) copy-start(bf16[1024,256]{1,0:T(8,128)(2,1)} %query_weight_ref.3) | copy-start | bytes 1572868
  17.2 16.1 %collective-permute-start.2 = (bf16[256,512]{1,0:T(8,128)(2,1)S(1)}, bf16[256,512]{1,0:T(8,128)(2,1)S(1)}, u32[]{:S(2)}, u32[]{:S(2)}) collective-permute-start(bf16[256,512]{1,0:T(8,128)(2,1)S(1)} %shard_map.103.kv0), channel_id=1, source_target_pairs={{0,12},{4,16},{8,20},{12,24},{16,28},{20,32},{24,36},{28,40},{32,4... | collective-permute-start | bytes 786440 | tf_op jit(solution)/shard_map/ppermute | solution.py:202
  18.7 15.4 %collective-permute-start.1 = (bf16[256,512]{1,0:T(8,128)(2,1)S(1)}, bf16[256,512]{1,0:T(8,128)(2,1)S(1)}, u32[]{:S(2)}, u32[]{:S(2)}) collective-permute-start(bf16[256,512]{1,0:T(8,128)(2,1)S(1)} %shard_map.103.kv0), channel_id=1, source_target_pairs={{0,8},{4,12},{8,16},{12,20},{16,24},{20,28},{24,32},{28,36},{32,40... | collective-permute-start | bytes 786440 | tf_op jit(solution)/shard_map/ppermute | solution.py:202
  20.1 14.7 %collective-permute-start = (bf16[256,512]{1,0:T(8,128)(2,1)S(1)}, bf16[256,512]{1,0:T(8,128)(2,1)}, u32[]{:S(2)}, u32[]{:S(2)}) collective-permute-start(bf16[256,512]{1,0:T(8,128)(2,1)S(1)} %shard_map.103.kv0), channel_id=1, source_target_pairs={{0,4},{4,8},{8,12},{12,16},{16,20},{20,24},{24,28},{28,32},{32,36}... | collective-permute-start | bytes 786440 | tf_op jit(solution)/shard_map/ppermute | solution.py:202
  33.4 0.7 copy-start.13
  34.1 0.7 copy-start.15
  34.8 1.0 copy-start.14
  35.7 0.9 copy-start.16
  44.6 0.7 copy-start.18
  45.3 9.8 %collective-permute-start.3 = (bf16[256,512]{1,0:T(8,128)(2,1)}, bf16[256,512]{1,0:T(8,128)(2,1)S(1)}, u32[]{:S(2)}, u32[]{:S(2)}) collective-permute-start(bf16[256,512]{1,0:T(8,128)(2,1)} %get-tuple-element.30), channel_id=1, source_target_pairs={{4,0},{8,4},{12,8},{16,12},{20,16},{24,20},{28,24},{32,28},{36,32}... | collective-permute-start | bytes 786440 | tf_op jit(solution)/shard_map/ppermute | solution.py:202
  46.6 13.5 %collective-permute-start.4 = (bf16[256,512]{1,0:T(8,128)(2,1)}, bf16[256,512]{1,0:T(8,128)(2,1)S(1)}, u32[]{:S(2)}, u32[]{:S(2)}) collective-permute-start(bf16[256,512]{1,0:T(8,128)(2,1)} %copy-done.18), channel_id=1, source_target_pairs={{8,0},{12,4},{16,8},{20,12},{24,16},{28,20},{32,24},{36,28},{40,32... | collective-permute-start | bytes 786440 | tf_op jit(solution)/shard_map/ppermute | solution.py:202
  47.9 19.8 %collective-permute-start.5 = (bf16[256,512]{1,0:T(8,128)(2,1)}, bf16[256,512]{1,0:T(8,128)(2,1)S(1)}, u32[]{:S(2)}, u32[]{:S(2)}) collective-permute-start(bf16[256,512]{1,0:T(8,128)(2,1)} %copy-done.17), channel_id=1, source_target_pairs={{12,0},{16,4},{20,8},{24,12},{28,16},{32,20},{36,24},{40,28},{44,3... | collective-permute-start | bytes 786440 | tf_op jit(solution)/shard_map/ppermute | solution.py:202
  55.5 12.1 %collective-permute-start.6 = (bf16[128,1024]{1,0:T(8,128)(2,1)S(1)}, bf16[128,1024]{1,0:T(8,128)(2,1)S(1)}, u32[]{:S(2)}, u32[]{:S(2)}) collective-permute-start(bf16[128,1024]{1,0:T(8,128)(2,1)S(1)} %get-tuple-element.34), channel_id=1, source_target_pairs={{0,1},{1,0},{2,3},{3,2},{4,5},{5,4},{6,7},{7,6},{8,9},{9,8},{10,11... | collective-permute-start | bytes 786440 | tf_op jit(solution)/shard_map/ppermute | solution.py:206
  69.0 1.0 copy-start.6
  70.0 0.7 copy-start.7
  71.4 17.6 %copy-start.3 = (bf16[1024,256]{1,0:T(8,128)(2,1)S(1)}, bf16[1024,256]{1,0:T(8,128)(2,1)}, u32[]{:S(2)}) copy-start(bf16[1024,256]{1,0:T(8,128)(2,1)} %value_weight_ref.3) | copy-start | bytes 1572868
  71.4 17.6 %copy-start.8 = (bf16[256,512]{1,0:T(8,128)(2,1)S(1)}, bf16[256,512]{1,0:T(8,128)(2,1)}, u32[]{:S(2)}) copy-start(bf16[256,512]{1,0:T(8,128)(2,1)} %copy-done.7) | copy-start | bytes 786436
  71.4 17.6 %copy-start.12 = (bf16[256,256]{1,0:T(8,128)(2,1)S(1)}, bf16[256,256]{1,0:T(8,128)(2,1)}, u32[]{:S(2)}) copy-start(bf16[256,256]{1,0:T(8,128)(2,1)} %copy-done.11) | copy-start | bytes 393220
  71.4 29.7 %all-to-all-start = ((bf16[8,256,256]{2,1,0:T(8,128)(2,1)}), bf16[8,256,256]{2,1,0:T(8,128)(2,1)S(1)}, u32[]{:S(2)}, u32[]{:S(2)}) async-start(bf16[8,256,256]{2,1,0:T(8,128)(2,1)} %copy-done.6), calls=%async_computation | async-start | bytes 2097152 | tf_op jit(solution)/shard_map/all_to_all | solution.py:277
  86.6 14.4 %collective-permute-start.7 = (bf16[64,1024]{1,0:T(8,128)(2,1)}, bf16[64,1024]{1,0:T(8,128)(2,1)S(1)}, u32[]{:S(2)}, u32[]{:S(2)}) collective-permute-start(bf16[64,1024]{1,0:T(8,128)(2,1)} %get-tuple-element.37), channel_id=1, source_target_pairs={{0,2},{1,3},{2,0},{3,1},{4,6},{5,7},{6,4},{7,5},{8,10},{9,11},{10,... | collective-permute-start | bytes 393224 | tf_op jit(solution)/shard_map/ppermute | solution.py:206
  89.0 12.1 %copy-start.10 = (f32[64,1024]{1,0:T(8,128)S(1)}, f32[64,1024]{1,0:T(8,128)}, u32[]{:S(2)}) copy-start(f32[64,1024]{1,0:T(8,128)} %copy-done.9) | copy-start | bytes 786436
  91.0 10.0 %collective-permute-start.8 = (bf16[64,1024]{1,0:T(8,128)(2,1)S(1)}, bf16[64,1024]{1,0:T(8,128)(2,1)S(1)}, u32[]{:S(2)}, u32[]{:S(2)}) collective-permute-start(bf16[64,1024]{1,0:T(8,128)(2,1)S(1)} %get-tuple-element.40), channel_id=1, source_target_pairs={{0,1},{1,0},{2,3},{3,2},{4,5},{5,4},{6,7},{7,6},{8,9},{9,8},{10,11... | collective-permute-start | bytes 393224 | tf_op jit(solution)/shard_map/ppermute | solution.py:206
  102.0 18.2 %copy-start.22 = (bf16[64,1024]{1,0:T(8,128)(2,1)S(1)}, bf16[64,1024]{1,0:T(8,128)(2,1)}, u32[]{:S(2)}) copy-start(bf16[64,1024]{1,0:T(8,128)(2,1)} %copy-done.21) | copy-start | bytes 393220
  102.0 21.6 %copy-start.20 = (bf16[64,1024]{1,0:T(8,128)(2,1)S(1)}, bf16[64,1024]{1,0:T(8,128)(2,1)}, u32[]{:S(2)}) copy-start(bf16[64,1024]{1,0:T(8,128)(2,1)} %copy-done.19) | copy-start | bytes 393220
  102.0 32.1 %all-to-all-start.1 = ((bf16[16,16,256]{2,1,0:T(8,128)(2,1)}), bf16[16,16,256]{2,1,0:T(8,128)(2,1)S(1)}, u32[]{:S(2)}, u32[]{:S(2)}) async-start(bf16[16,16,256]{2,1,0:T(8,128)(2,1)} %bitcast.1), calls=%async_computation.1 | async-start | bytes 262144 | tf_op jit(solution)/shard_map/all_to_all | solution.py:293
  120.2 9.6 %collective-permute-start.9 = (bf16[64,1024]{1,0:T(8,128)(2,1)S(1)}, bf16[64,1024]{1,0:T(8,128)(2,1)S(1)}, u32[]{:S(2)}, u32[]{:S(2)}) collective-permute-start(bf16[64,1024]{1,0:T(8,128)(2,1)S(1)} %copy-done.22), channel_id=1, source_target_pairs={{0,2},{1,3},{2,0},{3,1},{4,6},{5,7},{6,4},{7,5},{8,10},{9,11},{10,... | collective-permute-start | bytes 393224 | tf_op jit(solution)/shard_map/ppermute | solution.py:206
  123.5 9.8 %collective-permute-start.10 = (bf16[64,1024]{1,0:T(8,128)(2,1)S(1)}, bf16[64,1024]{1,0:T(8,128)(2,1)S(1)}, u32[]{:S(2)}, u32[]{:S(2)}) collective-permute-start(bf16[64,1024]{1,0:T(8,128)(2,1)S(1)} %copy-done.20), channel_id=1, source_target_pairs={{0,3},{1,2},{2,1},{3,0},{4,7},{5,6},{6,5},{7,4},{8,11},{9,10},{10,... | collective-permute-start | bytes 393224 | tf_op jit(solution)/shard_map/ppermute | solution.py:206
  (5 other events, 3.4 us)

commit v6 on v2

--- a/solution.py
+++ b/solution.py
@@ -10,7 +10,7 @@
 HEAD_DIM = 64
 WINDOW = 4
 FAR = 1e30
-VMEM_LIMIT = 24 * 1024 * 1024
+VMEM_LIMIT = 12 * 1024 * 1024
 
 F32 = jnp.float32
 BF16 = jnp.bfloat16
@@ -151,20 +151,35 @@
 
 def input_kernel(
     head_ref, dq_ref, kv_grad_ref, query_weight_ref, key_weight_ref, value_weight_ref, att_ref, out_weight_ref,
-    own_ref, send1, send2, send3, mixed_own_ref, mixed_send1, mixed_send2, mixed_send3, held_mixed, held,
+    own_ref, send1, send2, send3, pair_ref, held_mixed, held,
 ):
     span = dq_ref.shape[1]
     held_mixed[...] = dot_nn(att_ref[...], out_weight_ref[...])
     term = dot_nt(dq_ref[...], query_weight_ref[...])
     term = term + dot_nt(kv_grad_ref[:, :span], key_weight_ref[...])
     held[...] = term + dot_nt(kv_grad_ref[:, span:], value_weight_ref[...])
-    shares(head_ref, held, (own_ref, send1, send2, send3))
-    shares(head_ref, held_mixed, (mixed_own_ref, mixed_send1, mixed_send2, mixed_send3))
-
-
-def near_kernel(pieces_ref, part0, part1, part2, part3, terms_ref, frames_grad_ref):
+    half = own_ref.shape[0]
+    shares(head_ref, held, (own_ref, send1.at[pl.ds(0, half), :], send2, send3))
+    core = jnp.bitwise_and(head_ref[0], 1)
+    for chip in range(2):
+        start = pl.multiple_of((2 * chip + core) * half, half)
+        pair_ref[pl.ds(chip * half, half), :] = held_mixed[pl.ds(start, half), :].astype(BF16)
+        start = pl.multiple_of((2 * chip + 1 - core) * half, half)
+        send1[pl.ds((1 + chip) * half, half), :] = held_mixed[pl.ds(start, half), :].astype(BF16)
+
+
+def near_kernel(
+    head_ref, pieces_ref, own_ref, pair_ref, from1, from3, frames_send_ref, terms_ref, part_ref, send2, held
+):
     terms_ref[...] = added([pieces_ref.at[i] for i in range(pieces_ref.shape[0])]).astype(BF16)
-    frames_grad_ref[...] = added((part0, part1, part2, part3)).astype(BF16)
+    half = own_ref.shape[0]
+    held[...] = added((pair_ref, from1.at[pl.ds(half, 2 * half), :]))
+    chip = lax.shift_right_logical(head_ref[0], 1)
+    part_ref[pl.ds(0, half), :] = added((own_ref, from1.at[pl.ds(0, half), :], from3))
+    part_ref[pl.ds(half, half), :] = held[pl.ds(pl.multiple_of(chip * half, half), half), :]
+    send2[pl.ds(0, half), :] = frames_send_ref[...]
+    mixed_send = held[pl.ds(pl.multiple_of((1 - chip) * half, half), half), :]
+    send2[pl.ds(half, half), :] = mixed_send.astype(BF16)
 
 
 def far_kernel(pieces_ref, value_ref, out_ref):
@@ -174,8 +189,11 @@
     out_ref[...] = total[rows:]
 
 
-def mixed_kernel(part0, part1, part2, part3, mixed_ref):
-    mixed_ref[...] = added((part0, part1, part2, part3)).astype(BF16)
+def head_sum_kernel(part_ref, from2, frames_grad_ref, mixed_ref):
+    total = added((part_ref, from2))
+    half = mixed_ref.shape[0]
+    frames_grad_ref[...] = total[:half].astype(BF16)
+    mixed_ref[...] = total[half:].astype(BF16)
 
 
 def passed_along(value, steps):
@@ -184,13 +202,8 @@
     return lax.ppermute(value, "seq", [(i, i + steps) for i in range(first, last)])
 
 
-def exchanged(sends):
-    count = lax.axis_size("head")
-    received = {}
-    for other in range(count - 1, 0, -1):
-        pairs = [(i, i ^ other) for i in range(count)]
-        received[other] = lax.ppermute(sends[other - 1], "head", pairs)
-    return [received[other] for other in range(1, count)]
+def with_head(value, other):
+    return lax.ppermute(value, "head", [(i, i ^ other) for i in range(lax.axis_size("head"))])
 
 
 def per_device(inner, frames_in, query_weight, key_weight, value_weight, out_weight, read_mask, out_grad):
@@ -245,24 +258,34 @@
     )
     terms = lax.all_to_all(terms, "seq", 0, 0, axis_index_groups=near, tiled=True)
     shared = shape_of((share, width), BF16)
-    sends = call(
+    own, send1, send2, send3, pair = call(
         input_kernel,
-        [shared] * (2 * groups),
+        [
+            shared,
+            shape_of((3 * share, width), BF16),
+            shared,
+            shared,
+            shape_of((2 * share, width), BF16),
+        ],
         [group, dq, kv_grad, query_weight, key_weight, value_weight, attended, out_weight],
         [held, held],
         smem=1,
         flops=4 * square * width,
     )
-    frames_parts = [sends[0], *exchanged(sends[1:groups])]
-    mixed_parts = [sends[groups], *exchanged(sends[groups + 1 :])]
-    terms, frames_grad = call(
+    terms, part, send2 = call(
         near_kernel,
-        [shape_of((2 * outer * tail, span), BF16), shared],
-        [terms, *frames_parts],
+        [
+            shape_of((2 * outer * tail, span), BF16),
+            shape_of((2 * share, width), F32),
+            shape_of((2 * share, width), BF16),
+        ],
+        [group, terms, own, pair, with_head(send1, 1), with_head(send3, 3), send2],
+        [pltpu.VMEM((2 * share, width), F32)],
+        smem=1,
     )
     terms = terms.reshape(outer, 2 * tail, span)
     terms = lax.all_to_all(terms, "seq", 0, 0, axis_index_groups=across, tiled=True)
-    [mixed] = call(mixed_kernel, [shared], mixed_parts)
+    frames_grad, mixed = call(head_sum_kernel, [shared, shared], [part, with_head(send2, 2)])
     value_sum, out_sum = call(far_kernel, [shape_of((tail, span), F32)] * 2, [terms])
     return mixed, frames_grad, value_sum, out_sum.T
 

time: 136 us -> 131 us (0.963)
  starting transfers between devices: 62.6 us -> 51.5 us
  waiting for transfers between devices: 28.6 us -> 34 us
    ppermute x6 -> x3, starting transfers between devices: 19.7 us -> 8.55 us  [with_head(): lax.ppermute(value, 'head', [(i, i ^ other) for i in range(lax.axis_size(...]
    ppermute x6 -> x3, waiting for transfers between devices: 9.68 us -> 14.6 us  [with_head(): lax.ppermute(value, 'head', [(i, i ^ other) for i in range(lax.axis_size(...]
    unnamed x41 -> x33, local copies, waits for them, and re-layouts: 7.86 us -> 8.46 us
  transfers between devices with their start and end apart: 14 -> 11, of which waited for: 7 -> 6; matrix products, arithmetic and copies ran while one was open for 0% -> 0% of each run, Pallas kernels for 1% -> 2%
where the time goes in v6:
time: 131 us; the launch traced here: 130 us
  starting transfers between devices  51.5 us (39%)
  waiting for transfers between devices  34 us (26%)
  blocking collectives  24.3 us (19%)
  Pallas kernels  10.7 us (8%)
  local copies, waits for them, and re-layouts  8.53 us (7%)
    ppermute x6, waiting for transfers between devices, passed_along(): lax.ppermute(value, 'seq', [(i, i + steps) for i in range(first, last)])  19 us
    all_to_all x1, starting transfers between devices, per_device(): lax.all_to_all(terms, 'seq', 0, 0, axis_index_groups=across, tiled=True)  18.4 us
    all_to_all x1, starting transfers between devices, per_device(): lax.all_to_all(terms, 'seq', 0, 0, axis_index_groups=near, tiled=True)  15.2 us
    all_gather x1, blocking collectives, per_device(): frames = lax.all_gather(frames_in, 'head', axis=0, tiled=True)  15.1 us
    ppermute x3, waiting for transfers between devices, with_head(): lax.ppermute(value, 'head', [(i, i ^ other) for i in range(lax.axis_size(...  14.6 us
    pallas_call x8, Pallas kernels, call(): pl.pallas_call(kernel, out_shape=outs, in_specs=specs, out_specs=[pl.Bloc...  10.7 us
    ppermute x6, starting transfers between devices, passed_along(): lax.ppermute(value, 'seq', [(i, i + steps) for i in range(first, last)])  9.34 us
    all_gather x1, blocking collectives, per_device(): grads = lax.all_gather(out_grad, 'head', axis=0, tiled=True)  9.24 us
  transfers between devices with their start and end apart: 11, of which 6 were waited for; matrix products, arithmetic and copies ran while one was open for 0% of the time, Pallas kernels for 2%

profile of v6, /device:TPU:1, one launch (start us, length us, event | category | flops | bytes accessed | tf_op | source)
XLA Modules:
  0.0 129.9 jit_solution(5238614382871593263)
XLA Ops:
  0.7 15.1 %all_gather.6.frames_ref = bf16[256,1024]{1,0:T(8,128)(2,1)S(1)} all-gather(bf16[64,1024]{1,0:T(8,128)(2,1)} %param.7), channel_id=1, replica_groups=mesh['seq'=128,'head'=4] {'head'}, dimensions={0}, use_global_device_ids=true | all-gather | bytes 655360 | tf_op jit(solution)/shard_map/all_gather | solution.py:229
  15.7 1.0 copy-done.2
  17.2 1.4 %collective-permute-start.2 = (bf16[256,512]{1,0:T(8,128)(2,1)S(1)}, bf16[256,512]{1,0:T(8,128)(2,1)S(1)}, u32[]{:S(2)}, u32[]{:S(2)}) collective-permute-start(bf16[256,512]{1,0:T(8,128)(2,1)S(1)} %shard_map.103.kv0), channel_id=1, source_target_pairs={{0,12},{4,16},{8,20},{12,24},{16,28},{20,32},{24,36},{28,40},{32,4... | collective-permute-start | bytes 786440 | tf_op jit(solution)/shard_map/ppermute | solution.py:202
  18.7 1.4 %collective-permute-start.1 = (bf16[256,512]{1,0:T(8,128)(2,1)S(1)}, bf16[256,512]{1,0:T(8,128)(2,1)S(1)}, u32[]{:S(2)}, u32[]{:S(2)}) collective-permute-start(bf16[256,512]{1,0:T(8,128)(2,1)S(1)} %shard_map.103.kv0), channel_id=1, source_target_pairs={{0,8},{4,12},{8,16},{12,20},{16,24},{20,28},{24,32},{28,36},{32,40... | collective-permute-start | bytes 786440 | tf_op jit(solution)/shard_map/ppermute | solution.py:202
  20.1 2.6 %collective-permute-start = (bf16[256,512]{1,0:T(8,128)(2,1)S(1)}, bf16[256,512]{1,0:T(8,128)(2,1)S(1)}, u32[]{:S(2)}, u32[]{:S(2)}) collective-permute-start(bf16[256,512]{1,0:T(8,128)(2,1)S(1)} %shard_map.103.kv0), channel_id=1, source_target_pairs={{0,4},{4,8},{8,12},{12,16},{16,20},{20,24},{24,28},{28,32},{32,36}... | collective-permute-start | bytes 786440 | tf_op jit(solution)/shard_map/ppermute | solution.py:202
  22.9 9.2 %all_gather.7.grads_ref = bf16[256,1024]{1,0:T(8,128)(2,1)S(1)} all-gather(bf16[64,1024]{1,0:T(8,128)(2,1)S(1)} %copy-done.15), channel_id=1, replica_groups=mesh['seq'=128,'head'=4] {'head'}, dimensions={0}, use_global_device_ids=true | all-gather | bytes 655360 | tf_op jit(solution)/shard_map/all_gather | solution.py:232
  32.7 6.1 %shard_map.104 = (bf16[256,256]{1,0:T(8,128)(2,1)S(1)}, bf16[256,256]{1,0:T(8,128)(2,1)S(1)}, f32[256,512]{1,0:T(8,128)S(1)}, bf16[256,512]{1,0:T(8,128)(2,1)S(1...) custom-call(s32[1,3]{1,0:T(1,128)S(1)} %copy.12.mask_ref, bf16[256,256]{1,0:T(8,128)(2,1)S(1)} %get-tuple-element.26.qt_ref, ...), custom_call_target="tpu_custom_call" | custom-call | flops 3221225472 | bytes 2883596 | tf_op jit(solution)/shard_map/pallas_call | solution.py:39
  38.8 0.6 copy-done.9
  39.4 1.3 collective-permute-start.3
  40.7 1.3 collective-permute-start.4
  42.0 1.3 collective-permute-start.5
  43.3 6.0 %collective-permute-done.3.far1 = bf16[256,512]{1,0:T(8,128)(2,1)S(1)} collective-permute-done((bf16[256,512]{1,0:T(8,128)(2,1)S(1)}, bf16[256,512]{1,0:T(8,128)(2,1)S(1)}, u32[]{:S(2)}, u32[]{:S(2)}) %collective-permute-start.3) | collective-permute-done | bytes 262176 | tf_op jit(solution)/shard_map/ppermute | solution.py:202
  49.4 5.3 %collective-permute-done.4.far2 = bf16[256,512]{1,0:T(8,128)(2,1)S(1)} collective-permute-done((bf16[256,512]{1,0:T(8,128)(2,1)S(1)}, bf16[256,512]{1,0:T(8,128)(2,1)S(1)}, u32[]{:S(2)}, u32[]{:S(2)}) %collective-permute-start.4) | collective-permute-done | bytes 262176 | tf_op jit(solution)/shard_map/ppermute | solution.py:202
  54.7 7.6 %collective-permute-done.5.far3 = bf16[256,512]{1,0:T(8,128)(2,1)S(1)} collective-permute-done((bf16[256,512]{1,0:T(8,128)(2,1)S(1)}, bf16[256,512]{1,0:T(8,128)(2,1)S(1)}, u32[]{:S(2)}, u32[]{:S(2)}) %collective-permute-start.5) | collective-permute-done | bytes 262176 | tf_op jit(solution)/shard_map/ppermute | solution.py:202
  62.9 1.0 copy-done.6
  63.9 0.7 copy-done.7
  64.6 15.2 %all-to-all-start = ((bf16[8,256,256]{2,1,0:T(8,128)(2,1)}), bf16[8,256,256]{2,1,0:T(8,128)(2,1)S(1)}, u32[]{:S(2)}, u32[]{:S(2)}) async-start(bf16[8,256,256]{2,1,0:T(8,128)(2,1)} %copy-done.6), calls=%async_computation | async-start | bytes 2097152 | tf_op jit(solution)/shard_map/all_to_all | solution.py:259
  79.8 0.9 copy-done.8
  80.8 0.9 copy-done.10
  81.7 0.9 shard_map.106
  82.6 0.6 copy-done.11
  83.2 0.7 copy-done.13
  83.9 3.2 %collective-permute-start.6 = (bf16[192,1024]{1,0:T(8,128)(2,1)S(1)}, bf16[192,1024]{1,0:T(8,128)(2,1)S(1)}, u32[]{:S(2)}, u32[]{:S(2)}) collective-permute-start(bf16[192,1024]{1,0:T(8,128)(2,1)S(1)} %get-tuple-element.38), channel_id=1, source_target_pairs={{0,1},{1,0},{2,3},{3,2},{4,5},{5,4},{6,7},{7,6},{8,9},{9,8},{10,11... | collective-permute-start | bytes 1179656 | tf_op jit(solution)/shard_map/ppermute | solution.py:206
  87.1 2.3 %collective-permute-start.7 = (bf16[64,1024]{1,0:T(8,128)(2,1)S(1)}, bf16[64,1024]{1,0:T(8,128)(2,1)S(1)}, u32[]{:S(2)}, u32[]{:S(2)}) collective-permute-start(bf16[64,1024]{1,0:T(8,128)(2,1)S(1)} %get-tuple-element.39), channel_id=1, source_target_pairs={{0,3},{1,2},{2,1},{3,0},{4,7},{5,6},{6,5},{7,4},{8,11},{9,10},{10,... | collective-permute-start | bytes 393224 | tf_op jit(solution)/shard_map/ppermute | solution.py:206
  89.4 6.2 %collective-permute-done.7.from3 = bf16[64,1024]{1,0:T(8,128)(2,1)S(1)} collective-permute-done((bf16[64,1024]{1,0:T(8,128)(2,1)S(1)}, bf16[64,1024]{1,0:T(8,128)(2,1)S(1)}, u32[]{:S(2)}, u32[]{:S(2)}) %collective-permute-start.7) | collective-permute-done | bytes 131104 | tf_op jit(solution)/shard_map/ppermute | solution.py:206
  95.6 0.9 copy-done.12
  96.5 0.9 copy-done.14
  97.4 0.9 shard_map.107
  98.3 18.4 %all-to-all-start.1 = ((bf16[16,16,256]{2,1,0:T(8,128)(2,1)}), bf16[16,16,256]{2,1,0:T(8,128)(2,1)S(1)}, u32[]{:S(2)}, u32[]{:S(2)}) async-start(bf16[16,16,256]{2,1,0:T(8,128)(2,1)} %bitcast.1), calls=%async_computation.1 | async-start | bytes 262144 | tf_op jit(solution)/shard_map/all_to_all | solution.py:287
  116.7 3.0 %collective-permute-start.8 = (bf16[128,1024]{1,0:T(8,128)(2,1)S(1)}, bf16[128,1024]{1,0:T(8,128)(2,1)S(1)}, u32[]{:S(2)}, u32[]{:S(2)}) collective-permute-start(bf16[128,1024]{1,0:T(8,128)(2,1)S(1)} %get-tuple-element.42), channel_id=1, source_target_pairs={{0,2},{1,3},{2,0},{3,1},{4,6},{5,7},{6,4},{7,5},{8,10},{9,11},{10,... | collective-permute-start | bytes 786440 | tf_op jit(solution)/shard_map/ppermute | solution.py:206
  119.7 8.4 %collective-permute-done.8.from2 = bf16[128,1024]{1,0:T(8,128)(2,1)S(1)} collective-permute-done((bf16[128,1024]{1,0:T(8,128)(2,1)S(1)}, bf16[128,1024]{1,0:T(8,128)(2,1)S(1)}, u32[]{:S(2)}, u32[]{:S(2)}) %collective-permute-start.8) | collective-permute-done | bytes 262176 | tf_op jit(solution)/shard_map/ppermute | solution.py:206
  128.1 0.7 shard_map.108
  (34 shorter events, 2.9 us)
Async XLA Ops:
  0.6 22.1 %copy-start = (s32[128,3]{0,1:T(4,128)S(1)}, s32[128,3]{0,1:T(4,128)}, u32[]{:S(2)}) copy-start(s32[128,3]{0,1:T(4,128)} %param.12) | copy-start | bytes 4612
  0.6 15.1 %copy-start.1 = (bf16[1024,256]{1,0:T(8,128)(2,1)S(1)}, bf16[1024,256]{1,0:T(8,128)(2,1)}, u32[]{:S(2)}) copy-start(bf16[1024,256]{1,0:T(8,128)(2,1)} %key_weight_ref.3) | copy-start | bytes 1572868
  15.7 1.0 copy-start.2
  16.8 6.1 %copy-start.15 = (bf16[64,1024]{1,0:T(8,128)(2,1)S(1)}, bf16[64,1024]{1,0:T(8,128)(2,1)}, u32[]{:S(2)}) copy-start(bf16[64,1024]{1,0:T(8,128)(2,1)} %param.13) | copy-start | bytes 393220
  16.8 15.4 %copy-start.5 = (bf16[256,1024]{1,0:T(8,128)(2,1)S(1)}, bf16[256,1024]{1,0:T(8,128)(2,1)}, u32[]{:S(2)}) copy-start(bf16[256,1024]{1,0:T(8,128)(2,1)} %out_weight_ref.3) | copy-start | bytes 1572868
  17.2 14.9 %copy-start.4 = (bf16[1024,256]{1,0:T(8,128)(2,1)S(1)}, bf16[1024,256]{1,0:T(8,128)(2,1)}, u32[]{:S(2)}) copy-start(bf16[1024,256]{1,0:T(8,128)(2,1)} %query_weight_ref.3) | copy-start | bytes 1572868
  17.2 15.4 %collective-permute-start.2 = (bf16[256,512]{1,0:T(8,128)(2,1)S(1)}, bf16[256,512]{1,0:T(8,128)(2,1)S(1)}, u32[]{:S(2)}, u32[]{:S(2)}) collective-permute-start(bf16[256,512]{1,0:T(8,128)(2,1)S(1)} %shard_map.103.kv0), channel_id=1, source_target_pairs={{0,12},{4,16},{8,20},{12,24},{16,28},{20,32},{24,36},{28,40},{32,4... | collective-permute-start | bytes 786440 | tf_op jit(solution)/shard_map/ppermute | solution.py:202
  18.7 14.0 %collective-permute-start.1 = (bf16[256,512]{1,0:T(8,128)(2,1)S(1)}, bf16[256,512]{1,0:T(8,128)(2,1)S(1)}, u32[]{:S(2)}, u32[]{:S(2)}) collective-permute-start(bf16[256,512]{1,0:T(8,128)(2,1)S(1)} %shard_map.103.kv0), channel_id=1, source_target_pairs={{0,8},{4,12},{8,16},{12,20},{16,24},{20,28},{24,32},{28,36},{32,40... | collective-permute-start | bytes 786440 | tf_op jit(solution)/shard_map/ppermute | solution.py:202
  20.1 12.6 %collective-permute-start = (bf16[256,512]{1,0:T(8,128)(2,1)S(1)}, bf16[256,512]{1,0:T(8,128)(2,1)S(1)}, u32[]{:S(2)}, u32[]{:S(2)}) collective-permute-start(bf16[256,512]{1,0:T(8,128)(2,1)S(1)} %shard_map.103.kv0), channel_id=1, source_target_pairs={{0,4},{4,8},{8,12},{12,16},{16,20},{20,24},{24,28},{28,32},{32,36}... | collective-permute-start | bytes 786440 | tf_op jit(solution)/shard_map/ppermute | solution.py:202
  38.8 0.7 copy-start.9
  39.4 9.9 %collective-permute-start.3 = (bf16[256,512]{1,0:T(8,128)(2,1)S(1)}, bf16[256,512]{1,0:T(8,128)(2,1)S(1)}, u32[]{:S(2)}, u32[]{:S(2)}) collective-permute-start(bf16[256,512]{1,0:T(8,128)(2,1)S(1)} %get-tuple-element.30), channel_id=1, source_target_pairs={{4,0},{8,4},{12,8},{16,12},{20,16},{24,20},{28,24},{32,28},{36,32}... | collective-permute-start | bytes 786440 | tf_op jit(solution)/shard_map/ppermute | solution.py:202
  40.7 13.9 %collective-permute-start.4 = (bf16[256,512]{1,0:T(8,128)(2,1)S(1)}, bf16[256,512]{1,0:T(8,128)(2,1)S(1)}, u32[]{:S(2)}, u32[]{:S(2)}) collective-permute-start(bf16[256,512]{1,0:T(8,128)(2,1)S(1)} %get-tuple-element.31), channel_id=1, source_target_pairs={{8,0},{12,4},{16,8},{20,12},{24,16},{28,20},{32,24},{36,28},{40,32... | collective-permute-start | bytes 786440 | tf_op jit(solution)/shard_map/ppermute | solution.py:202
  42.0 20.3 %collective-permute-start.5 = (bf16[256,512]{1,0:T(8,128)(2,1)S(1)}, bf16[256,512]{1,0:T(8,128)(2,1)S(1)}, u32[]{:S(2)}, u32[]{:S(2)}) collective-permute-start(bf16[256,512]{1,0:T(8,128)(2,1)S(1)} %get-tuple-element.32), channel_id=1, source_target_pairs={{12,0},{16,4},{20,8},{24,12},{28,16},{32,20},{36,24},{40,28},{44,3... | collective-permute-start | bytes 786440 | tf_op jit(solution)/shard_map/ppermute | solution.py:202
  62.9 1.0 copy-start.6
  63.9 0.7 copy-start.7
  64.6 15.2 %copy-start.3 = (bf16[1024,256]{1,0:T(8,128)(2,1)S(1)}, bf16[1024,256]{1,0:T(8,128)(2,1)}, u32[]{:S(2)}) copy-start(bf16[1024,256]{1,0:T(8,128)(2,1)} %value_weight_ref.3) | copy-start | bytes 1572868
  64.6 31.0 %all-to-all-start = ((bf16[8,256,256]{2,1,0:T(8,128)(2,1)}), bf16[8,256,256]{2,1,0:T(8,128)(2,1)S(1)}, u32[]{:S(2)}, u32[]{:S(2)}) async-start(bf16[8,256,256]{2,1,0:T(8,128)(2,1)} %copy-done.6), calls=%async_computation | async-start | bytes 2097152 | tf_op jit(solution)/shard_map/all_to_all | solution.py:259
  79.8 1.0 copy-start.8
  80.8 0.9 copy-start.10
  82.6 0.7 copy-start.11
  83.2 0.7 copy-start.13
  83.9 11.7 %collective-permute-start.6 = (bf16[192,1024]{1,0:T(8,128)(2,1)S(1)}, bf16[192,1024]{1,0:T(8,128)(2,1)S(1)}, u32[]{:S(2)}, u32[]{:S(2)}) collective-permute-start(bf16[192,1024]{1,0:T(8,128)(2,1)S(1)} %get-tuple-element.38), channel_id=1, source_target_pairs={{0,1},{1,0},{2,3},{3,2},{4,5},{5,4},{6,7},{7,6},{8,9},{9,8},{10,11... | collective-permute-start | bytes 1179656 | tf_op jit(solution)/shard_map/ppermute | solution.py:206
  87.1 8.5 %collective-permute-start.7 = (bf16[64,1024]{1,0:T(8,128)(2,1)S(1)}, bf16[64,1024]{1,0:T(8,128)(2,1)S(1)}, u32[]{:S(2)}, u32[]{:S(2)}) collective-permute-start(bf16[64,1024]{1,0:T(8,128)(2,1)S(1)} %get-tuple-element.39), channel_id=1, source_target_pairs={{0,3},{1,2},{2,1},{3,0},{4,7},{5,6},{6,5},{7,4},{8,11},{9,10},{10,... | collective-permute-start | bytes 393224 | tf_op jit(solution)/shard_map/ppermute | solution.py:206
  95.6 0.9 copy-start.12
  96.5 0.9 copy-start.14
  98.3 31.0 %all-to-all-start.1 = ((bf16[16,16,256]{2,1,0:T(8,128)(2,1)}), bf16[16,16,256]{2,1,0:T(8,128)(2,1)S(1)}, u32[]{:S(2)}, u32[]{:S(2)}) async-start(bf16[16,16,256]{2,1,0:T(8,128)(2,1)} %bitcast.1), calls=%async_computation.1 | async-start | bytes 262144 | tf_op jit(solution)/shard_map/all_to_all | solution.py:287
  116.7 11.4 %collective-permute-start.8 = (bf16[128,1024]{1,0:T(8,128)(2,1)S(1)}, bf16[128,1024]{1,0:T(8,128)(2,1)S(1)}, u32[]{:S(2)}, u32[]{:S(2)}) collective-permute-start(bf16[128,1024]{1,0:T(8,128)(2,1)S(1)} %get-tuple-element.42), channel_id=1, source_target_pairs={{0,2},{1,3},{2,0},{3,1},{4,6},{5,7},{6,4},{7,5},{8,10},{9,11},{10,... | collective-permute-start | bytes 786440 | tf_op jit(solution)/shard_map/ppermute | solution.py:206

commit v7 on v6

--- a/solution.py
+++ b/solution.py
@@ -130,11 +130,14 @@
     return total
 
 
-def weights_kernel(cuts, frames_ref, grads_ref, att_ref, own_ref, far1, far2, far3, kv_grad_ref, terms_ref):
+def weights_kernel(
+    cuts, frames_ref, grads_ref, att_ref, dq_ref, own_ref, far1, far2, far3, kv_grad_ref, terms_ref
+):
     outer, inner, tail = cuts
     rounded = added((own_ref, far1, far2, far3)).astype(BF16)
-    kv_grad_ref[...] = rounded
     span = rounded.shape[1] // 2
+    kv_grad_ref[:, : 2 * span] = rounded
+    kv_grad_ref[:, 2 * span :] = dq_ref[...]
     value_term = dot_tn(frames_ref[...], rounded[:, span:]).reshape(outer, inner, tail, span)
     out_term = dot_tn(grads_ref[...], att_ref[...]).reshape(outer, inner, tail, span)
     for i in range(inner):
@@ -150,14 +153,14 @@
 
 
 def input_kernel(
-    head_ref, dq_ref, kv_grad_ref, query_weight_ref, key_weight_ref, value_weight_ref, att_ref, out_weight_ref,
+    head_ref, kv_grad_ref, query_weight_ref, key_weight_ref, value_weight_ref, att_ref, out_weight_ref,
     own_ref, send1, send2, send3, pair_ref, held_mixed, held,
 ):
-    span = dq_ref.shape[1]
+    span = query_weight_ref.shape[1]
     held_mixed[...] = dot_nn(att_ref[...], out_weight_ref[...])
-    term = dot_nt(dq_ref[...], query_weight_ref[...])
+    term = dot_nt(kv_grad_ref[:, 2 * span :], query_weight_ref[...])
     term = term + dot_nt(kv_grad_ref[:, :span], key_weight_ref[...])
-    held[...] = term + dot_nt(kv_grad_ref[:, span:], value_weight_ref[...])
+    held[...] = term + dot_nt(kv_grad_ref[:, span : 2 * span], value_weight_ref[...])
     half = own_ref.shape[0]
     shares(head_ref, held, (own_ref, send1.at[pl.ds(0, half), :], send2, send3))
     core = jnp.bitwise_and(head_ref[0], 1)
@@ -252,8 +255,8 @@
     fars = [passed_along(fars[k - 1], -k) for k in range(1, WINDOW)]
     kv_grad, terms = call(
         functools.partial(weights_kernel, (outer, inner, tail)),
-        [kv_shape, shape_of((inner, 2 * outer * tail, span), BF16)],
-        [frames, grads, attended, own, *fars],
+        [shape_of((count, 3 * span), BF16), shape_of((inner, 2 * outer * tail, span), BF16)],
+        [frames, grads, attended, dq, own, *fars],
         flops=2 * square * width,
     )
     terms = lax.all_to_all(terms, "seq", 0, 0, axis_index_groups=near, tiled=True)
@@ -267,7 +270,7 @@
             shared,
             shape_of((2 * share, width), BF16),
         ],
-        [group, dq, kv_grad, query_weight, key_weight, value_weight, attended, out_weight],
+        [group, kv_grad, query_weight, key_weight, value_weight, attended, out_weight],
         [held, held],
         smem=1,
         flops=4 * square * width,

time: 131 us -> 131 us (level)
  local copies, waits for them, and re-layouts: 8.53 us -> 7.06 us
    unnamed x33 -> x29, local copies, waits for them, and re-layouts: 8.46 us -> 6.98 us
where the time goes in v7:
time: 131 us; the launch traced here: 130 us
  starting transfers between devices  51.6 us (39%)
  waiting for transfers between devices  35 us (27%)
  blocking collectives  24.3 us (19%)
  Pallas kernels  10.8 us (8%)
  local copies, waits for them, and re-layouts  7.06 us (5%)
    ppermute x6, waiting for transfers between devices, passed_along(): lax.ppermute(value, 'seq', [(i, i + steps) for i in range(first, last)])  19 us
    all_to_all x1, starting transfers between devices, per_device(): lax.all_to_all(terms, 'seq', 0, 0, axis_index_groups=across, tiled=True)  18.5 us
    ppermute x3, waiting for transfers between devices, with_head(): lax.ppermute(value, 'head', [(i, i ^ other) for i in range(lax.axis_size(...  15.5 us
    all_to_all x1, starting transfers between devices, per_device(): lax.all_to_all(terms, 'seq', 0, 0, axis_index_groups=near, tiled=True)  15.2 us
    all_gather x1, blocking collectives, per_device(): frames = lax.all_gather(frames_in, 'head', axis=0, tiled=True)  15.1 us
    pallas_call x8, Pallas kernels, call(): pl.pallas_call(kernel, out_shape=outs, in_specs=specs, out_specs=[pl.Bloc...  10.8 us
    ppermute x6, starting transfers between devices, passed_along(): lax.ppermute(value, 'seq', [(i, i + steps) for i in range(first, last)])  9.35 us
    all_gather x1, blocking collectives, per_device(): grads = lax.all_gather(out_grad, 'head', axis=0, tiled=True)  9.24 us
  transfers between devices with their start and end apart: 11, of which 6 were waited for; matrix products, arithmetic and copies ran while one was open for 0% of the time, Pallas kernels for 2%

profile of v7, /device:TPU:1, one launch (start us, length us, event | category | flops | bytes accessed | tf_op | source)
XLA Modules:
  0.0 129.5 jit_solution(1995184665469459102)
XLA Ops:
  0.7 15.1 %all_gather.6.frames_ref = bf16[256,1024]{1,0:T(8,128)(2,1)S(1)} all-gather(bf16[64,1024]{1,0:T(8,128)(2,1)} %param.7), channel_id=1, replica_groups=mesh['seq'=128,'head'=4] {'head'}, dimensions={0}, use_global_device_ids=true | all-gather | bytes 655360 | tf_op jit(solution)/shard_map/all_gather | solution.py:232
  15.7 1.0 copy-done.2
  17.2 1.4 %collective-permute-start.2 = (bf16[256,512]{1,0:T(8,128)(2,1)S(1)}, bf16[256,512]{1,0:T(8,128)(2,1)S(1)}, u32[]{:S(2)}, u32[]{:S(2)}) collective-permute-start(bf16[256,512]{1,0:T(8,128)(2,1)S(1)} %shard_map.103.kv0), channel_id=1, source_target_pairs={{0,12},{4,16},{8,20},{12,24},{16,28},{20,32},{24,36},{28,40},{32,4... | collective-permute-start | bytes 786440 | tf_op jit(solution)/shard_map/ppermute | solution.py:205
  18.7 1.4 %collective-permute-start.1 = (bf16[256,512]{1,0:T(8,128)(2,1)S(1)}, bf16[256,512]{1,0:T(8,128)(2,1)S(1)}, u32[]{:S(2)}, u32[]{:S(2)}) collective-permute-start(bf16[256,512]{1,0:T(8,128)(2,1)S(1)} %shard_map.103.kv0), channel_id=1, source_target_pairs={{0,8},{4,12},{8,16},{12,20},{16,24},{20,28},{24,32},{28,36},{32,40... | collective-permute-start | bytes 786440 | tf_op jit(solution)/shard_map/ppermute | solution.py:205
  20.1 2.6 %collective-permute-start = (bf16[256,512]{1,0:T(8,128)(2,1)S(1)}, bf16[256,512]{1,0:T(8,128)(2,1)S(1)}, u32[]{:S(2)}, u32[]{:S(2)}) collective-permute-start(bf16[256,512]{1,0:T(8,128)(2,1)S(1)} %shard_map.103.kv0), channel_id=1, source_target_pairs={{0,4},{4,8},{8,12},{12,16},{16,20},{20,24},{24,28},{28,32},{32,36}... | collective-permute-start | bytes 786440 | tf_op jit(solution)/shard_map/ppermute | solution.py:205
  22.9 9.2 %all_gather.7.grads_ref = bf16[256,1024]{1,0:T(8,128)(2,1)S(1)} all-gather(bf16[64,1024]{1,0:T(8,128)(2,1)S(1)} %copy-done.13), channel_id=1, replica_groups=mesh['seq'=128,'head'=4] {'head'}, dimensions={0}, use_global_device_ids=true | all-gather | bytes 655360 | tf_op jit(solution)/shard_map/all_gather | solution.py:235
  32.7 6.1 %shard_map.104 = (bf16[256,256]{1,0:T(8,128)(2,1)S(1)}, bf16[256,256]{1,0:T(8,128)(2,1)S(1)}, f32[256,512]{1,0:T(8,128)S(1)}, bf16[256,512]{1,0:T(8,128)(2,1)S(1...) custom-call(s32[1,3]{1,0:T(1,128)S(1)} %copy.12.mask_ref, bf16[256,256]{1,0:T(8,128)(2,1)S(1)} %get-tuple-element.26.qt_ref, ...), custom_call_target="tpu_custom_call" | custom-call | flops 3221225472 | bytes 2883596 | tf_op jit(solution)/shard_map/pallas_call | solution.py:39
  38.8 1.3 collective-permute-start.3
  40.1 1.3 collective-permute-start.4
  41.4 1.3 collective-permute-start.5
  42.7 6.0 %collective-permute-done.3.far1 = bf16[256,512]{1,0:T(8,128)(2,1)S(1)} collective-permute-done((bf16[256,512]{1,0:T(8,128)(2,1)S(1)}, bf16[256,512]{1,0:T(8,128)(2,1)S(1)}, u32[]{:S(2)}, u32[]{:S(2)}) %collective-permute-start.3) | collective-permute-done | bytes 262176 | tf_op jit(solution)/shard_map/ppermute | solution.py:205
  48.7 5.4 %collective-permute-done.4.far2 = bf16[256,512]{1,0:T(8,128)(2,1)S(1)} collective-permute-done((bf16[256,512]{1,0:T(8,128)(2,1)S(1)}, bf16[256,512]{1,0:T(8,128)(2,1)S(1)}, u32[]{:S(2)}, u32[]{:S(2)}) %collective-permute-start.4) | collective-permute-done | bytes 262176 | tf_op jit(solution)/shard_map/ppermute | solution.py:205
  54.1 7.5 %collective-permute-done.5.far3 = bf16[256,512]{1,0:T(8,128)(2,1)S(1)} collective-permute-done((bf16[256,512]{1,0:T(8,128)(2,1)S(1)}, bf16[256,512]{1,0:T(8,128)(2,1)S(1)}, u32[]{:S(2)}, u32[]{:S(2)}) %collective-permute-start.5) | collective-permute-done | bytes 262176 | tf_op jit(solution)/shard_map/ppermute | solution.py:205
  61.6 0.6 shard_map.105
  62.3 1.0 copy-done.6
  63.2 0.7 copy-done.7
  64.0 15.2 %all-to-all-start = ((bf16[8,256,256]{2,1,0:T(8,128)(2,1)}), bf16[8,256,256]{2,1,0:T(8,128)(2,1)S(1)}, u32[]{:S(2)}, u32[]{:S(2)}) async-start(bf16[8,256,256]{2,1,0:T(8,128)(2,1)} %copy-done.6), calls=%async_computation | async-start | bytes 2097152 | tf_op jit(solution)/shard_map/all_to_all | solution.py:262
  79.2 1.0 copy-done.8
  80.2 0.9 shard_map.106
  81.1 0.6 copy-done.9
  81.8 0.7 copy-done.11
  82.4 3.2 %collective-permute-start.6 = (bf16[192,1024]{1,0:T(8,128)(2,1)S(1)}, bf16[192,1024]{1,0:T(8,128)(2,1)S(1)}, u32[]{:S(2)}, u32[]{:S(2)}) collective-permute-start(bf16[192,1024]{1,0:T(8,128)(2,1)S(1)} %get-tuple-element.38), channel_id=1, source_target_pairs={{0,1},{1,0},{2,3},{3,2},{4,5},{5,4},{6,7},{7,6},{8,9},{9,8},{10,11... | collective-permute-start | bytes 1179656 | tf_op jit(solution)/shard_map/ppermute | solution.py:209
  85.6 2.3 %collective-permute-start.7 = (bf16[64,1024]{1,0:T(8,128)(2,1)S(1)}, bf16[64,1024]{1,0:T(8,128)(2,1)S(1)}, u32[]{:S(2)}, u32[]{:S(2)}) collective-permute-start(bf16[64,1024]{1,0:T(8,128)(2,1)S(1)} %get-tuple-element.39), channel_id=1, source_target_pairs={{0,3},{1,2},{2,1},{3,0},{4,7},{5,6},{6,5},{7,4},{8,11},{9,10},{10,... | collective-permute-start | bytes 393224 | tf_op jit(solution)/shard_map/ppermute | solution.py:209
  88.0 7.0 %collective-permute-done.7.from3 = bf16[64,1024]{1,0:T(8,128)(2,1)S(1)} collective-permute-done((bf16[64,1024]{1,0:T(8,128)(2,1)S(1)}, bf16[64,1024]{1,0:T(8,128)(2,1)S(1)}, u32[]{:S(2)}, u32[]{:S(2)}) %collective-permute-start.7) | collective-permute-done | bytes 131104 | tf_op jit(solution)/shard_map/ppermute | solution.py:209
  94.9 0.9 copy-done.10
  95.8 0.9 copy-done.12
  96.7 0.9 shard_map.107
  97.6 18.5 %all-to-all-start.1 = ((bf16[16,16,256]{2,1,0:T(8,128)(2,1)}), bf16[16,16,256]{2,1,0:T(8,128)(2,1)S(1)}, u32[]{:S(2)}, u32[]{:S(2)}) async-start(bf16[16,16,256]{2,1,0:T(8,128)(2,1)} %bitcast.1), calls=%async_computation.1 | async-start | bytes 262144 | tf_op jit(solution)/shard_map/all_to_all | solution.py:290
  116.1 3.0 %collective-permute-start.8 = (bf16[128,1024]{1,0:T(8,128)(2,1)S(1)}, bf16[128,1024]{1,0:T(8,128)(2,1)S(1)}, u32[]{:S(2)}, u32[]{:S(2)}) collective-permute-start(bf16[128,1024]{1,0:T(8,128)(2,1)S(1)} %get-tuple-element.42), channel_id=1, source_target_pairs={{0,2},{1,3},{2,0},{3,1},{4,6},{5,7},{6,4},{7,5},{8,10},{9,11},{10,... | collective-permute-start | bytes 786440 | tf_op jit(solution)/shard_map/ppermute | solution.py:209
  119.1 8.5 %collective-permute-done.8.from2 = bf16[128,1024]{1,0:T(8,128)(2,1)S(1)} collective-permute-done((bf16[128,1024]{1,0:T(8,128)(2,1)S(1)}, bf16[128,1024]{1,0:T(8,128)(2,1)S(1)}, u32[]{:S(2)}, u32[]{:S(2)}) %collective-permute-start.8) | collective-permute-done | bytes 262176 | tf_op jit(solution)/shard_map/ppermute | solution.py:209
  127.6 0.7 shard_map.108
  128.9 0.6 shard_map.109
  (30 shorter events, 1.7 us)
Async XLA Ops:
  0.6 22.1 %copy-start = (s32[128,3]{0,1:T(4,128)S(1)}, s32[128,3]{0,1:T(4,128)}, u32[]{:S(2)}) copy-start(s32[128,3]{0,1:T(4,128)} %param.12) | copy-start | bytes 4612
  0.6 15.1 %copy-start.1 = (bf16[1024,256]{1,0:T(8,128)(2,1)S(1)}, bf16[1024,256]{1,0:T(8,128)(2,1)}, u32[]{:S(2)}) copy-start(bf16[1024,256]{1,0:T(8,128)(2,1)} %key_weight_ref.3) | copy-start | bytes 1572868
  15.7 1.0 copy-start.2
  16.8 6.1 %copy-start.13 = (bf16[64,1024]{1,0:T(8,128)(2,1)S(1)}, bf16[64,1024]{1,0:T(8,128)(2,1)}, u32[]{:S(2)}) copy-start(bf16[64,1024]{1,0:T(8,128)(2,1)} %param.13) | copy-start | bytes 393220
  16.8 15.4 %copy-start.5 = (bf16[256,1024]{1,0:T(8,128)(2,1)S(1)}, bf16[256,1024]{1,0:T(8,128)(2,1)}, u32[]{:S(2)}) copy-start(bf16[256,1024]{1,0:T(8,128)(2,1)} %out_weight_ref.3) | copy-start | bytes 1572868
  17.2 14.9 %copy-start.4 = (bf16[1024,256]{1,0:T(8,128)(2,1)S(1)}, bf16[1024,256]{1,0:T(8,128)(2,1)}, u32[]{:S(2)}) copy-start(bf16[1024,256]{1,0:T(8,128)(2,1)} %query_weight_ref.3) | copy-start | bytes 1572868
  17.2 15.4 %collective-permute-start.2 = (bf16[256,512]{1,0:T(8,128)(2,1)S(1)}, bf16[256,512]{1,0:T(8,128)(2,1)S(1)}, u32[]{:S(2)}, u32[]{:S(2)}) collective-permute-start(bf16[256,512]{1,0:T(8,128)(2,1)S(1)} %shard_map.103.kv0), channel_id=1, source_target_pairs={{0,12},{4,16},{8,20},{12,24},{16,28},{20,32},{24,36},{28,40},{32,4... | collective-permute-start | bytes 786440 | tf_op jit(solution)/shard_map/ppermute | solution.py:205
  18.7 14.0 %collective-permute-start.1 = (bf16[256,512]{1,0:T(8,128)(2,1)S(1)}, bf16[256,512]{1,0:T(8,128)(2,1)S(1)}, u32[]{:S(2)}, u32[]{:S(2)}) collective-permute-start(bf16[256,512]{1,0:T(8,128)(2,1)S(1)} %shard_map.103.kv0), channel_id=1, source_target_pairs={{0,8},{4,12},{8,16},{12,20},{16,24},{20,28},{24,32},{28,36},{32,40... | collective-permute-start | bytes 786440 | tf_op jit(solution)/shard_map/ppermute | solution.py:205
  20.1 12.6 %collective-permute-start = (bf16[256,512]{1,0:T(8,128)(2,1)S(1)}, bf16[256,512]{1,0:T(8,128)(2,1)S(1)}, u32[]{:S(2)}, u32[]{:S(2)}) collective-permute-start(bf16[256,512]{1,0:T(8,128)(2,1)S(1)} %shard_map.103.kv0), channel_id=1, source_target_pairs={{0,4},{4,8},{8,12},{12,16},{16,20},{20,24},{24,28},{28,32},{32,36}... | collective-permute-start | bytes 786440 | tf_op jit(solution)/shard_map/ppermute | solution.py:205
  38.8 9.9 %collective-permute-start.3 = (bf16[256,512]{1,0:T(8,128)(2,1)S(1)}, bf16[256,512]{1,0:T(8,128)(2,1)S(1)}, u32[]{:S(2)}, u32[]{:S(2)}) collective-permute-start(bf16[256,512]{1,0:T(8,128)(2,1)S(1)} %get-tuple-element.31), channel_id=1, source_target_pairs={{4,0},{8,4},{12,8},{16,12},{20,16},{24,20},{28,24},{32,28},{36,32}... | collective-permute-start | bytes 786440 | tf_op jit(solution)/shard_map/ppermute | solution.py:205
  40.1 14.0 %collective-permute-start.4 = (bf16[256,512]{1,0:T(8,128)(2,1)S(1)}, bf16[256,512]{1,0:T(8,128)(2,1)S(1)}, u32[]{:S(2)}, u32[]{:S(2)}) collective-permute-start(bf16[256,512]{1,0:T(8,128)(2,1)S(1)} %get-tuple-element.32), channel_id=1, source_target_pairs={{8,0},{12,4},{16,8},{20,12},{24,16},{28,20},{32,24},{36,28},{40,32... | collective-permute-start | bytes 786440 | tf_op jit(solution)/shard_map/ppermute | solution.py:205
  41.4 20.3 %collective-permute-start.5 = (bf16[256,512]{1,0:T(8,128)(2,1)S(1)}, bf16[256,512]{1,0:T(8,128)(2,1)S(1)}, u32[]{:S(2)}, u32[]{:S(2)}) collective-permute-start(bf16[256,512]{1,0:T(8,128)(2,1)S(1)} %get-tuple-element.33), channel_id=1, source_target_pairs={{12,0},{16,4},{20,8},{24,12},{28,16},{32,20},{36,24},{40,28},{44,3... | collective-permute-start | bytes 786440 | tf_op jit(solution)/shard_map/ppermute | solution.py:205
  62.3 1.0 copy-start.6
  63.2 0.7 copy-start.7
  64.0 15.2 %copy-start.3 = (bf16[1024,256]{1,0:T(8,128)(2,1)S(1)}, bf16[1024,256]{1,0:T(8,128)(2,1)}, u32[]{:S(2)}) copy-start(bf16[1024,256]{1,0:T(8,128)(2,1)} %value_weight_ref.3) | copy-start | bytes 1572868
  64.0 30.9 %all-to-all-start = ((bf16[8,256,256]{2,1,0:T(8,128)(2,1)}), bf16[8,256,256]{2,1,0:T(8,128)(2,1)S(1)}, u32[]{:S(2)}, u32[]{:S(2)}) async-start(bf16[8,256,256]{2,1,0:T(8,128)(2,1)} %copy-done.6), calls=%async_computation | async-start | bytes 2097152 | tf_op jit(solution)/shard_map/all_to_all | solution.py:262
  79.2 1.0 copy-start.8
  81.1 0.7 copy-start.9
  81.8 0.7 copy-start.11
  82.4 12.5 %collective-permute-start.6 = (bf16[192,1024]{1,0:T(8,128)(2,1)S(1)}, bf16[192,1024]{1,0:T(8,128)(2,1)S(1)}, u32[]{:S(2)}, u32[]{:S(2)}) collective-permute-start(bf16[192,1024]{1,0:T(8,128)(2,1)S(1)} %get-tuple-element.38), channel_id=1, source_target_pairs={{0,1},{1,0},{2,3},{3,2},{4,5},{5,4},{6,7},{7,6},{8,9},{9,8},{10,11... | collective-permute-start | bytes 1179656 | tf_op jit(solution)/shard_map/ppermute | solution.py:209
  85.6 9.3 %collective-permute-start.7 = (bf16[64,1024]{1,0:T(8,128)(2,1)S(1)}, bf16[64,1024]{1,0:T(8,128)(2,1)S(1)}, u32[]{:S(2)}, u32[]{:S(2)}) collective-permute-start(bf16[64,1024]{1,0:T(8,128)(2,1)S(1)} %get-tuple-element.39), channel_id=1, source_target_pairs={{0,3},{1,2},{2,1},{3,0},{4,7},{5,6},{6,5},{7,4},{8,11},{9,10},{10,... | collective-permute-start | bytes 393224 | tf_op jit(solution)/shard_map/ppermute | solution.py:209
  94.9 0.9 copy-start.10
  95.8 0.9 copy-start.12
  97.6 31.3 %all-to-all-start.1 = ((bf16[16,16,256]{2,1,0:T(8,128)(2,1)}), bf16[16,16,256]{2,1,0:T(8,128)(2,1)S(1)}, u32[]{:S(2)}, u32[]{:S(2)}) async-start(bf16[16,16,256]{2,1,0:T(8,128)(2,1)} %bitcast.1), calls=%async_computation.1 | async-start | bytes 262144 | tf_op jit(solution)/shard_map/all_to_all | solution.py:290
  116.1 11.5 %collective-permute-start.8 = (bf16[128,1024]{1,0:T(8,128)(2,1)S(1)}, bf16[128,1024]{1,0:T(8,128)(2,1)S(1)}, u32[]{:S(2)}, u32[]{:S(2)}) collective-permute-start(bf16[128,1024]{1,0:T(8,128)(2,1)S(1)} %get-tuple-element.42), channel_id=1, source_target_pairs={{0,2},{1,3},{2,0},{3,1},{4,6},{5,7},{6,4},{7,5},{8,10},{9,11},{10,... | collective-permute-start | bytes 786440 | tf_op jit(solution)/shard_map/ppermute | solution.py:209
